TPU v7x, 32 devices: a whole 2x2x4 slice. The times are simulated.
32 devices in a mesh: batch: 16 (over z, y, core), seq: 2 (over x).
Axes of the slice: x: 2, y: 2, z: 4, core: 2. Of those that a mesh axis runs over, the one named last changes fastest.
Arguments:
- tokens: bfloat16 [16, 1024, 1024], P('batch', 'seq'), may hold values from -6 to 6
- segments: int32 [16, 1024], P('batch', 'seq'), may hold values from 0 to 2, as said below
- cotangent: bfloat16 [16, 1024, 1024], P('batch', 'seq'), may hold values from -6 to 6
- mixer_gain: bfloat16 [1024], P(('batch', 'seq')), may hold values from 0.5 to 1.5
- mixer_shift: bfloat16 [1024], P(('batch', 'seq')), may hold values from -1.5 to 1.5
- mixer_weight: bfloat16 [1024, 3072], P(('batch', 'seq')), may hold values from -0.1875 to 0.1875
- mixer_bias: bfloat16 [3072], P(('batch', 'seq')), may hold values from -1.5 to 1.5
- merger_weight: bfloat16 [1024, 1024], P(('batch', 'seq')), may hold values from -0.75 to 0.75
- merger_bias: bfloat16 [1024], P(('batch', 'seq')), may hold values from -1.5 to 1.5
- feeder_gain: bfloat16 [1024], P(('batch', 'seq')), may hold values from 0.5 to 1.5
- feeder_shift: bfloat16 [1024], P(('batch', 'seq')), may hold values from -1.5 to 1.5
- widen_weight: bfloat16 [1024, 4096], P(('batch', 'seq')), may hold values from -0.1875 to 0.1875
- widen_bias: bfloat16 [4096], P(('batch', 'seq')), may hold values from -1.5 to 1.5
- narrow_weight: bfloat16 [4096, 1024], P(('batch', 'seq')), may hold values from -0.09375 to 0.09375
- narrow_bias: bfloat16 [1024], P(('batch', 'seq')), may hold values from -1.5 to 1.5
Outputs:
- layer_output: bfloat16 [16, 1024, 1024], P('batch', 'seq')
- tokens_grad: bfloat16 [16, 1024, 1024], P('batch', 'seq')
- mixer_gain_grad: float32 [1024], P(('batch', 'seq'))
- mixer_shift_grad: float32 [1024], P(('batch', 'seq'))
- mixer_weight_grad: float32 [1024, 3072], P(('batch', 'seq'))
- mixer_bias_grad: float32 [3072], P(('batch', 'seq'))
- merger_weight_grad: float32 [1024, 1024], P(('batch', 'seq'))
- merger_bias_grad: float32 [1024], P(('batch', 'seq'))
- feeder_gain_grad: float32 [1024], P(('batch', 'seq'))
- feeder_shift_grad: float32 [1024], P(('batch', 'seq'))
- widen_weight_grad: float32 [1024, 4096], P(('batch', 'seq'))
- widen_bias_grad: float32 [4096], P(('batch', 'seq'))
- narrow_weight_grad: float32 [4096, 1024], P(('batch', 'seq'))
- narrow_bias_grad: float32 [1024], P(('batch', 'seq'))
Inputs may be any that keep to these rules, and one draw needn't show every extreme that they name: `segments`: along each sequence the numbers start at 0 and never fall, at most three documents a sequence; the tokens that share a number form one document.
All inputs are finite; a program needn't handle non-finite values.
Results may differ from a plain program's by a relative error of at most 0.009.
Values may be sent and summed in bfloat16 or wider, within the bound.
No kernel may reach another device: no remote copies, remote signals or barrier semaphores. Data moves between devices by JAX's collectives and lax.ppermute only.
A program may use at most 320 MiB of HBM per device.

v0:
```python
import jax
import jax.numpy as jnp
from jax import lax
from jax.sharding import PartitionSpec as P

HD = 64
ROT = 16


EPS = 1e-05
SCALE = 0.125


def normalize(rows, gain, shift):
    mean = jnp.mean(rows, -1, keepdims=True)
    centered = rows - mean
    spread = jnp.mean(centered * centered, -1, keepdims=True)
    return centered * lax.rsqrt(spread + EPS) * gain + shift


def exact_gelu(value):
    return jax.nn.gelu(value, approximate=False)


def angles(position, half):
    freq = 10000.0 ** (-(jnp.arange(half).astype(jnp.float32) * 2.0) / float(2 * half))
    phase = position.astype(jnp.float32)[..., None] * freq
    return (jnp.cos(phase), jnp.sin(phase))


def turn(value, cosine, sine):
    half = cosine.shape[-1]
    front = value[..., :half]
    behind = value[..., half : 2 * half]
    remain = value[..., 2 * half :]
    cos_b = cosine[..., None, :]
    sin_b = sine[..., None, :]
    return jnp.concatenate(
        [front * cos_b - behind * sin_b, behind * cos_b + front * sin_b, remain], -1
    )


def contract_rows(left, right):
    return lax.dot_general(
        left, right, (((0,), (0,)), ((), ())), preferred_element_type=jnp.float32
    )


def contract_cols(left, right):
    return lax.dot_general(
        left, right, (((1,), (1,)), ((), ())), preferred_element_type=jnp.float32
    )


def local(
    tokens,
    segments,
    cotangent,
    mixer_gain,
    mixer_shift,
    mixer_weight,
    mixer_bias,
    merger_weight,
    merger_bias,
    feeder_gain,
    feeder_shift,
    widen_weight,
    widen_bias,
    narrow_weight,
    narrow_bias,
):
    shards = (
        mixer_gain,
        mixer_shift,
        mixer_weight,
        mixer_bias,
        merger_weight,
        merger_bias,
        feeder_gain,
        feeder_shift,
        widen_weight,
        widen_bias,
        narrow_weight,
        narrow_bias,
    )
    gathered = (
        lax.all_gather(shards[0], ("batch", "seq"), axis=0, tiled=True),
        lax.all_gather(shards[1], ("batch", "seq"), axis=0, tiled=True),
        lax.all_gather(shards[2], ("batch", "seq"), axis=0, tiled=True),
        lax.all_gather(shards[3], ("batch", "seq"), axis=0, tiled=True),
        lax.all_gather(shards[4], ("batch", "seq"), axis=0, tiled=True),
        lax.all_gather(shards[5], ("batch", "seq"), axis=0, tiled=True),
        lax.all_gather(shards[6], ("batch", "seq"), axis=0, tiled=True),
        lax.all_gather(shards[7], ("batch", "seq"), axis=0, tiled=True),
        lax.all_gather(shards[8], ("batch", "seq"), axis=0, tiled=True),
        lax.all_gather(shards[9], ("batch", "seq"), axis=0, tiled=True),
        lax.all_gather(shards[10], ("batch", "seq"), axis=0, tiled=True),
        lax.all_gather(shards[11], ("batch", "seq"), axis=0, tiled=True),
    )
    seqs, stretch, width = tokens.shape
    heads = width // HD
    rows = seqs * stretch
    whole_segs = lax.all_gather(segments, "seq", axis=1, tiled=True)
    length = whole_segs.shape[1]
    query_place = lax.axis_index("seq") * stretch + jnp.arange(stretch, dtype=jnp.int32)
    key_place = jnp.arange(length, dtype=jnp.int32)
    earlier = jnp.sum((whole_segs[:, None, :] < segments[:, :, None]).astype(jnp.int32), -1)
    cosine, sine = angles(query_place[None, :] - earlier, ROT // 2)
    flat = tokens.astype(jnp.float32).reshape(rows, width)
    first_f, pull_first = jax.vjp(
        normalize, flat, gathered[0].astype(jnp.float32), gathered[1].astype(jnp.float32)
    )
    second_f, pull_second = jax.vjp(
        normalize, flat, gathered[6].astype(jnp.float32), gathered[7].astype(jnp.float32)
    )
    first = first_f.astype(jnp.bfloat16)
    second = second_f.astype(jnp.bfloat16)
    project = jnp.dot(first, gathered[2], preferred_element_type=jnp.float32) + gathered[3].astype(
        jnp.float32
    )
    project = project.reshape(seqs, stretch, 3, heads, HD)
    query_f, pull_turn = jax.vjp(lambda value: turn(value, cosine, sine), project[:, :, 0])
    keys_f = turn(project[:, :, 1], cosine, sine)
    query = query_f.astype(jnp.bfloat16)
    keys = keys_f.astype(jnp.bfloat16).reshape(seqs, stretch, width)
    values = project[:, :, 2].astype(jnp.bfloat16).reshape(seqs, stretch, width)
    keys_all, values_all = (
        lax.all_gather(keys, "seq", axis=1, tiled=True),
        lax.all_gather(values, "seq", axis=1, tiled=True),
    )
    block = max(1, min(seqs, 512 // stretch))
    while seqs % block:
        block = block - 1
    count = seqs // block
    query_blocks = query.reshape(count, block, stretch, heads, HD)
    key_blocks = keys_all.reshape(count, block, length, heads, HD)
    value_blocks = values_all.reshape(count, block, length, heads, HD)
    query_segs = segments.reshape(count, block, stretch)
    key_segs = whole_segs.reshape(count, block, length)

    def masked_scores(query_part, key_part, query_seg, key_seg):
        scores = (
            jnp.einsum("bqhd,bkhd->bhqk", query_part, key_part, preferred_element_type=jnp.float32)
            * SCALE
        )
        allowed = (query_seg[:, :, None] == key_seg[:, None, :]) & (
            query_place[None, :, None] >= key_place[None, None, :]
        )
        allowed = allowed[:, None]
        return (jnp.where(allowed, scores, -1e30), allowed)

    def forward_block(item):
        query_part, key_part, value_part, query_seg, key_seg = item
        scores, allowed = masked_scores(query_part, key_part, query_seg, key_seg)
        top = jnp.max(scores, -1, keepdims=True)
        expo = jnp.where(allowed, jnp.exp(scores - top), 0.0)
        total = jnp.sum(expo, -1, keepdims=True)
        prob = (expo / total).astype(jnp.bfloat16)
        result = jnp.einsum("bhqk,bkhd->bqhd", prob, value_part, preferred_element_type=jnp.float32)
        return (result, (top + jnp.log(total))[..., 0])

    def score_side(item):
        query_part, key_part, value_part, query_seg, key_seg, result_grad, level = item
        scores, allowed = masked_scores(query_part, key_part, query_seg, key_seg)
        prob = jnp.where(allowed, jnp.exp(scores - level[..., None]), 0.0)
        prob_grad = jnp.einsum(
            "bqhd,bkhd->bhqk", result_grad, value_part, preferred_element_type=jnp.float32
        )
        center = jnp.sum(prob * prob_grad, -1, keepdims=True)
        score_grad = (prob * (prob_grad - center)).astype(jnp.bfloat16)
        query_grad = (
            jnp.einsum("bhqk,bkhd->bqhd", score_grad, key_part, preferred_element_type=jnp.float32)
            * SCALE
        )
        return (prob, score_grad, query_grad, center[..., 0])

    def backward_block(item):
        prob, score_grad, query_grad, center = score_side(item)
        query_part = item[0]
        result_grad = item[5]
        key_grad = (
            jnp.einsum(
                "bhqk,bqhd->bkhd", score_grad, query_part, preferred_element_type=jnp.float32
            )
            * SCALE
        )
        value_grad = jnp.einsum(
            "bhqk,bqhd->bkhd",
            prob.astype(jnp.bfloat16),
            result_grad,
            preferred_element_type=jnp.float32,
        )
        return (query_grad, key_grad, value_grad)

    mixed, level = lax.map(
        forward_block, (query_blocks, key_blocks, value_blocks, query_segs, key_segs)
    )
    mixed = mixed.astype(jnp.bfloat16).reshape(rows, width)
    branch_one = jnp.dot(mixed, gathered[4], preferred_element_type=jnp.float32) + gathered[
        5
    ].astype(jnp.float32)
    widened = jnp.dot(second, gathered[8], preferred_element_type=jnp.float32) + gathered[9].astype(
        jnp.float32
    )
    active_f, pull_gelu = jax.vjp(exact_gelu, widened)
    active = active_f.astype(jnp.bfloat16)
    branch_two = jnp.dot(active, gathered[10], preferred_element_type=jnp.float32) + gathered[
        11
    ].astype(jnp.float32)
    layer_output = (
        (flat + branch_one + branch_two).astype(jnp.bfloat16).reshape(seqs, stretch, width)
    )
    again = (
        lax.all_gather(shards[0], ("batch", "seq"), axis=0, tiled=True),
        lax.all_gather(shards[1], ("batch", "seq"), axis=0, tiled=True),
        lax.all_gather(shards[2], ("batch", "seq"), axis=0, tiled=True),
        lax.all_gather(shards[3], ("batch", "seq"), axis=0, tiled=True),
        lax.all_gather(shards[4], ("batch", "seq"), axis=0, tiled=True),
        lax.all_gather(shards[5], ("batch", "seq"), axis=0, tiled=True),
        lax.all_gather(shards[6], ("batch", "seq"), axis=0, tiled=True),
        lax.all_gather(shards[7], ("batch", "seq"), axis=0, tiled=True),
        lax.all_gather(shards[8], ("batch", "seq"), axis=0, tiled=True),
        lax.all_gather(shards[9], ("batch", "seq"), axis=0, tiled=True),
        lax.all_gather(shards[10], ("batch", "seq"), axis=0, tiled=True),
        lax.all_gather(shards[11], ("batch", "seq"), axis=0, tiled=True),
    )
    upstream = cotangent.reshape(rows, width)
    bias_grad = jnp.sum(upstream, 0, dtype=jnp.float32)
    merger_grad = contract_rows(mixed, upstream)
    narrow_grad = contract_rows(active, upstream)
    mixed_grad = contract_cols(upstream, again[4]).astype(jnp.bfloat16)
    active_grad = contract_cols(upstream, again[10])
    widened_grad = pull_gelu(active_grad)[0].astype(jnp.bfloat16)
    widen_bias_grad = jnp.sum(widened_grad, 0, dtype=jnp.float32)
    widen_grad = contract_rows(second, widened_grad)
    second_grad = contract_cols(widened_grad, again[8])
    result_grads = mixed_grad.reshape(count, block, stretch, heads, HD)
    attend_items = (
        query_blocks,
        key_blocks,
        value_blocks,
        query_segs,
        key_segs,
        result_grads,
        level,
    )
    query_grad, key_grad, value_grad = lax.map(backward_block, attend_items)
    key_back, value_back = (
        lax.psum_scatter(
            key_grad.reshape(seqs, length, width), "seq", scatter_dimension=1, tiled=True
        ),
        lax.psum_scatter(
            value_grad.reshape(seqs, length, width), "seq", scatter_dimension=1, tiled=True
        ),
    )
    query_pre = pull_turn(query_grad.reshape(seqs, stretch, heads, HD))[0]
    key_pre = pull_turn(key_back.reshape(seqs, stretch, heads, HD))[0]
    project_grad = jnp.stack([query_pre, key_pre, value_back.reshape(seqs, stretch, heads, HD)], 2)
    project_grad = project_grad.reshape(rows, 3 * width).astype(jnp.bfloat16)
    mixer_bias_grad = jnp.sum(project_grad, 0, dtype=jnp.float32)
    mixer_grad = contract_rows(first, project_grad)
    first_grad = contract_cols(project_grad, again[2])
    token_one, gain_one, shift_one = pull_first(first_grad)
    token_two, gain_two, shift_two = pull_second(second_grad)
    tokens_grad = (
        (cotangent.astype(jnp.float32).reshape(rows, width) + token_one + token_two)
        .astype(jnp.bfloat16)
        .reshape(seqs, stretch, width)
    )
    owned = (
        lax.psum_scatter(gain_one, ("batch", "seq"), scatter_dimension=0, tiled=True),
        lax.psum_scatter(shift_one, ("batch", "seq"), scatter_dimension=0, tiled=True),
        lax.psum_scatter(mixer_grad, ("batch", "seq"), scatter_dimension=0, tiled=True),
        lax.psum_scatter(mixer_bias_grad, ("batch", "seq"), scatter_dimension=0, tiled=True),
        lax.psum_scatter(merger_grad, ("batch", "seq"), scatter_dimension=0, tiled=True),
        lax.psum_scatter(bias_grad, ("batch", "seq"), scatter_dimension=0, tiled=True),
        lax.psum_scatter(gain_two, ("batch", "seq"), scatter_dimension=0, tiled=True),
        lax.psum_scatter(shift_two, ("batch", "seq"), scatter_dimension=0, tiled=True),
        lax.psum_scatter(widen_grad, ("batch", "seq"), scatter_dimension=0, tiled=True),
        lax.psum_scatter(widen_bias_grad, ("batch", "seq"), scatter_dimension=0, tiled=True),
        lax.psum_scatter(narrow_grad, ("batch", "seq"), scatter_dimension=0, tiled=True),
        lax.psum_scatter(bias_grad, ("batch", "seq"), scatter_dimension=0, tiled=True),
    )
    return (
        layer_output,
        tokens_grad,
        owned[0],
        owned[1],
        owned[2],
        owned[3],
        owned[4],
        owned[5],
        owned[6],
        owned[7],
        owned[8],
        owned[9],
        owned[10],
        owned[11],
    )


def solution(mesh):
    placed = (
        P("batch", "seq", None),
        P("batch", "seq"),
        P("batch", "seq", None),
        P(("batch", "seq")),
        P(("batch", "seq")),
        P(("batch", "seq"), None),
        P(("batch", "seq")),
        P(("batch", "seq"), None),
        P(("batch", "seq")),
        P(("batch", "seq")),
        P(("batch", "seq")),
        P(("batch", "seq"), None),
        P(("batch", "seq")),
        P(("batch", "seq"), None),
        P(("batch", "seq")),
    )
    return jax.shard_map(
        local,
        mesh=mesh,
        in_specs=placed,
        out_specs=(
            P("batch", "seq", None),
            P("batch", "seq", None),
            P(("batch", "seq")),
            P(("batch", "seq")),
            P(("batch", "seq"), None),
            P(("batch", "seq")),
            P(("batch", "seq"), None),
            P(("batch", "seq")),
            P(("batch", "seq")),
            P(("batch", "seq")),
            P(("batch", "seq"), None),
            P(("batch", "seq")),
            P(("batch", "seq"), None),
            P(("batch", "seq")),
        ),
        check_vma=False,
    )
```

profile of v0, /device:TPU:0, one launch (start us, length us, event | category | flops | bytes accessed | tf_op | source)
XLA Modules:
  0.0 1576.9 jit_solution(17047893243283323173)
XLA Ops:
  14.6 42.9 %all-reduce.21 = (bf16[1024]{0:T(1024)(128)(2,1)}, bf16[1024]{0:T(1024)(128)(2,1)}, bf16[3072]{0:T(1024)(128)(2,1)S(1)}, bf16[1024]{0:T(1024)(128)(2,1)S(1)}, bf...) all-reduce(bf16[1024]{0:T(1024)(128)(2,1)S(1)} %dynamic-update-slic, ...), channel_id=1, replica_groups=mesh['batch'=16,'seq'=2] {'batch','seq'}, use_global_device_ids=true, to_apply=%add.11 | all-reduce | flops 9216 | bytes 36864
  57.6 4.8 all_gather.56
  66.7 16.6 %all-gather.8.cloned.1.call-done = bf16[1024,3072]{1,0:T(8,128)(2,1)} async-done(((bf16[32,3072]{1,0:T(8,128)(2,1)}), bf16[1024,3072]{1,0:T(8,128)(2,1)}) %all-gather.8.cloned.1.call-update) | async-done | bytes 6291472 | tf_op jit(solution)/shard_map/all_gather | solution.py:89
  83.3 9.3 convolution_add_fusion
  92.7 6.6 copy.38
  104.7 36.6 %all-gather.14.cloned.1.call-done = bf16[1024,1024]{1,0:T(8,128)(2,1)} async-done(((bf16[32,1024]{1,0:T(8,128)(2,1)}), bf16[1024,1024]{1,0:T(8,128)(2,1)}) %all-gather.14.cloned.1.call-update) | async-done | bytes 2097168 | tf_op jit(solution)/shard_map/all_gather | solution.py:91
  141.3 4.2 convolution_convert_fusion
  151.4 24.1 %all-gather.12.cloned.1.call-done = bf16[1,1024,1024]{1,2,0:T(8,128)(2,1)} async-done(((bf16[1,512,1024]{1,2,0:T(8,128)(2,1)}), bf16[1,1024,1024]{1,2,0:T(8,128)(2,1)}) %all-gather.12.cloned.1.call-update) | async-done | bytes 2097168 | tf_op jit(solution)/shard_map/all_gather | solution.py:128
  175.4 16.2 %fusion.1 = (f32[16,512]{1,0:T(8,128)S(1)}, f32[16,512,1024]{2,1,0:T(8,128)}) fusion(pred[512,1024]{1,0:T(8,128)(4,1)S(1)} %fusion.40, bf16[1024,16,64]{0,2,1:T(8,128)(2,1)} %bitcast.162, bf16[512,16,48]{0,2,1:T(8,128)(2,1)S(1)} %fusion.65, bf16[512,16,8]{0,2,1:T(8,128)(2,1)} %get-tuple-element.118, bf16[512,16,8]{0,2,1:T(8,128)(2,1)S(1)} %get-tuple-element.117), kind=kOutput, calls=%fused_computation.7 | convolution fusion | flops 1102045184 | bytes 37257216 | tf_op jit(solution)/shard_map/while/body/eval_jaxpr/bqhd,bkhd->bhqk/dot_general | solution.py:143
  191.7 15.7 fusion
  210.6 26.8 %multiply_reduce_fusion = (f32[16,512]{1,0:T(8,128)S(1)}, f32[16,512,1024]{2,1,0:T(8,128)}) fusion(f32[16,512]{1,0:T(8,128)S(1)} %log_add_fusion, f32[16,512,1024]{2,1,0:T(8,128)} %get-tuple-element.135, pred[512,1024]{1,0:T(8,128)(4,1)S(1)} %fusion.40, bf16[512,16,64]{0,2,1:T(8,128)(2,1)S(1)} %bitcast.172, bf16[1024,16,64]{0,2,1:T(8,128)(2,1)} %bitcast.181), kind=kOutput, calls=%fused_computation.1 | convolution fusion | flops 1124065280 | bytes 70844416 | tf_op jit(solution)/shard_map/while/body/eval_jaxpr/bqhd,bkhd->bhqk/dot_general | solution.py:166
  237.4 27.7 %multiply_convert_fusion = bf16[16,512,1024]{2,1,0:T(8,128)(2,1)} fusion(f32[16,512,1024]{2,1,0:T(8,128)} %get-tuple-element.137, f32[16,512]{1,0:T(8,128)S(1)} %get-tuple-element.136, f32[16,512]{1,0:T(8,128)S(1)} %log_add_fusion, f32[16,512,1024]{2,1,0:T(8,128)} %get-tuple-element.135, pred[512,1024]{1,0:T(8,128)(4,1)S(1)} %fusion.40), kind=kLoop, calls=%fused_computation | loop fusion | flops 58720256 | bytes 84475904 | tf_op jit(solution)/shard_map/while/body/eval_jaxpr/convert_element_type | solution.py:170
  265.0 10.7 convolution_multiply_fusion
  276.0 17.0 %fusion.2 = f32[16,64,1024]{2,1,0:T(8,128)} fusion(bf16[512,16,64]{0,2,1:T(8,128)(2,1)S(1)} %bitcast.173, f32[16,512,1024]{2,1,0:T(8,128)} %get-tuple-element.135, f32[16,512]{1,0:T(8,128)S(1)} %log_add_fusion, pred[512,1024]{1,0:T(8,128)(4,1)S(1)} %fusion.40), kind=kOutput, calls=%fused_computation.8 | convolution fusion | flops 1115684864 | bytes 39354368 | tf_op jit(solution)/shard_map/while/body/eval_jaxpr/bhqk,bqhd->bkhd/dot_general | solution.py:187
  294.6 15.9 %fusion.41 = bf16[16,64,512]{2,1,0:T(8,128)(2,1)S(1)} fusion(bf16[1024,16,64]{0,2,1:T(8,128)(2,1)} %bitcast.182, f32[16,512,1024]{2,1,0:T(8,128)} %get-tuple-element.135, f32[16,512]{1,0:T(8,128)S(1)} %fusion, f32[16,512]{1,0:T(8,128)S(1)} %get-tuple-element.134, pred[512,1024]{1,0:T(8,128)(4,1)S(1)} %fusion.40), kind=kOutput, calls=%fused_computation.81 | convolution fusion | flops 1124597760 | bytes 37289984 | tf_op jit(solution)/shard_map/while/body/eval_jaxpr/bhqk,bkhd->bqhd/dot_general | solution.py:159
  314.7 12.4 multiply_bitcast_fusion
  333.6 53.3 %reduce-scatter.9.cloned.1.call-done = f32[1,512,1024]{1,2,0:T(8,128)} async-done(((f32[1,1024,1024]{1,2,0:T(8,128)}), f32[1,512,1024]{1,2,0:T(8,128)}) %reduce-scatter.9.cloned.1.call-update) | async-done | bytes 2097168 | tf_op jit(solution)/shard_map/reduce_scatter | solution.py:252
  390.4 6.9 fusion.44
  398.0 67.2 %all-gather = bf16[32,1,128]{2,1,0:T(2,128)(2,1)S(1)} all-gather(bf16[1,1,128]{2,1,0:T(2,128)(2,1)S(1)} %bitcast.180), channel_id=1, replica_groups=mesh['batch'=16,'seq'=2] {'batch','seq'}, dimensions={0}, use_global_device_ids=true | all-gather | bytes 8448 | tf_op jit(solution)/shard_map/all_gather | solution.py:96
  467.3 27.8 %multiply_convert_fusion.1 = (bf16[512,4096]{1,0:T(8,128)(2,1)}, f32[512,4096]{1,0:T(8,128)}, f32[512,4096]{1,0:T(8,128)}) fusion(f32[4096]{0:T(1024)S(1)} %bitcast.178, bf16[1024,4096]{1,0:T(8,128)(2,1)} %all-gather.16.cloned.1.call-done, bf16[1,512,1024]{2,1,0:T(8,128)(2,1)S(1)} %copy-done, f32[1024]{0:T(1024)S(1)} %convert_element_type.199, ...), kind=kOutput, calls=%fused_computation.15 | convolution fusion | flops 4436525056 | bytes 30437376 | tf_op jit(solution)/shard_map/dot_general | solution.py:202
  495.1 51.1 %all-gather.18.cloned.1.call-done = bf16[4096,1024]{1,0:T(8,128)(2,1)} async-done(((bf16[128,1024]{1,0:T(8,128)(2,1)}), bf16[4096,1024]{1,0:T(8,128)(2,1)}) %all-gather.18.cloned.1.call-update) | async-done | bytes 8388624 | tf_op jit(solution)/shard_map/all_gather | solution.py:97
  546.2 13.3 convert_reduce_fusion
  561.5 8.4 fusion.78
  570.2 10.5 fusion.48
  581.4 8.3 fusion.87
  592.1 6.9 fusion.88
  599.1 7.3 fusion.85
  610.8 40.6 %all-reduce.20 = (f32[1024]{0:T(1024)S(1)}, f32[1024]{0:T(1024)S(1)}, f32[3072]{0:T(1024)S(1)}, f32[1024]{0:T(1024)S(1)}, f32[1024]{0:T(1024)S(1)}, /*index=5*/f32[1024]{0:T(1024)S(1)}, f32[4096]{0:T(1024)S(1)}) all-reduce(f32[1024]{0:T(1024)S(1)} %get-tuple-element.92, ...), channel_id=4, replica_groups=mesh['batch'=16,'seq'=2] {'batch','seq'}, use_global_device_ids=true, to_apply=%region_13.14.clone | all-reduce | flops 12288 | bytes 98304
  654.9 34.9 %reduce-scatter.13.cloned.1.call-done = f32[32,1024]{1,0:T(8,128)} async-done(((f32[1024,1024]{1,0:T(8,128)}), f32[32,1024]{1,0:T(8,128)}) %reduce-scatter.13.cloned.1.call-update) | async-done | bytes 131088 | tf_op jit(solution)/shard_map/reduce_scatter | solution.py:275
  689.8 158.5 %reduce-scatter.11.cloned.1.call-done = f32[32,3072]{1,0:T(8,128)} async-done(((f32[1024,3072]{1,0:T(8,128)}), f32[32,3072]{1,0:T(8,128)}) %reduce-scatter.11.cloned.1.call-update) | async-done | bytes 393232 | tf_op jit(solution)/shard_map/reduce_scatter | solution.py:273
  848.4 359.5 %reduce-scatter.15.cloned.1.call-done = f32[32,4096]{1,0:T(8,128)} async-done(((f32[1024,4096]{1,0:T(8,128)}), f32[32,4096]{1,0:T(8,128)}) %reduce-scatter.15.cloned.1.call-update) | async-done | bytes 524304 | tf_op jit(solution)/shard_map/reduce_scatter | solution.py:279
  1207.9 361.5 %reduce-scatter.17.cloned.1.call-done = f32[128,1024]{1,0:T(8,128)} async-done(((f32[4096,1024]{1,0:T(8,128)}), f32[128,1024]{1,0:T(8,128)}) %reduce-scatter.17.cloned.1.call-update) | async-done | bytes 524304 | tf_op jit(solution)/shard_map/reduce_scatter | solution.py:281
  (159 shorter events, 58.5 us)
Async XLA Ops:
  7.2 76.1 %all-gather.8.cloned.1.call-start = ((), (), s32[]{:S(2)}) async-start(), calls=%async_computation.6 | async-start | bytes 6488064 | tf_op jit(solution)/shard_map/all_gather | solution.py:89
  7.9 133.4 %all-gather.14.cloned.1.call-start = ((), (), s32[]{:S(2)}) async-start(), calls=%async_computation.9 | async-start | bytes 2162688 | tf_op jit(solution)/shard_map/all_gather | solution.py:91
  8.7 166.8 %all-gather.12.cloned.1.call-start = ((), (), s32[]{:S(2)}) async-start(), calls=%async_computation.8 | async-start | bytes 3145728 | tf_op jit(solution)/shard_map/all_gather | solution.py:128
  57.5 35.1 %copy-start.13 = (f32[1024]{0:T(1024)}, f32[1024]{0:T(1024)S(1)}, u32[]{:S(2)}) copy-start(f32[1024]{0:T(1024)S(1)} %convert_element_type.183) | copy-start | bytes 12292
  57.5 35.1 %copy-start.22 = (f32[1024]{0:T(1024)}, f32[1024]{0:T(1024)S(1)}, u32[]{:S(2)}) copy-start(f32[1024]{0:T(1024)S(1)} %convert_element_type.184) | copy-start | bytes 12292
  64.8 27.8 %copy-start.15 = (f32[512]{0:T(512)}, f32[512]{0:T(512)S(1)}, u32[]{:S(2)}) copy-start(f32[512]{0:T(512)S(1)} %broadcast_multiply_fusion) | copy-start | bytes 6148
  66.5 26.1 %copy-start.19 = (f32[512]{0:T(512)}, f32[512]{0:T(512)S(1)}, u32[]{:S(2)}) copy-start(f32[512]{0:T(512)S(1)} %fusion.31) | copy-start | bytes 6148
  66.5 26.1 %copy-start.17 = (f32[512]{0:T(512)}, f32[512]{0:T(512)S(1)}, u32[]{:S(2)}) copy-start(f32[512]{0:T(512)S(1)} %fusion.69) | copy-start | bytes 6148
  66.7 35.5 %copy-start.9 = (f32[512,8]{0,1:T(8,128)}, f32[512,8]{0,1:T(8,128)S(1)}, u32[]{:S(2)}) copy-start(f32[512,8]{0,1:T(8,128)S(1)} %get-tuple-element.129) | copy-start | bytes 49156
  66.7 35.5 %copy-start.11 = (f32[512,8]{0,1:T(8,128)}, f32[512,8]{0,1:T(8,128)S(1)}, u32[]{:S(2)}) copy-start(f32[512,8]{0,1:T(8,128)S(1)} %get-tuple-element.130) | copy-start | bytes 49156
  104.1 106.5 %all-gather.10.cloned.1.call-start = ((), (), s32[]{:S(2)}) async-start(), calls=%async_computation.7 | async-start | bytes 3145728 | tf_op jit(solution)/shard_map/all_gather | solution.py:129
  150.9 179.4 %reduce-scatter.7.cloned.1.call-start = ((), (), s32[]{:S(2)}) async-start(), calls=%async_computation.12 | async-start | bytes 6291456 | tf_op jit(solution)/shard_map/reduce_scatter | solution.py:249
  191.7 18.9 %copy-start.5 = (bf16[512,1024]{0,1:T(8,128)(2,1)S(1)}, bf16[512,1024]{0,1:T(8,128)(2,1)}, u32[]{:S(2)}) copy-start(bf16[512,1024]{0,1:T(8,128)(2,1)} %copy.39) | copy-start | bytes 3145732
  237.3 27.7 %copy-start.4 = (bf16[512,16,8]{0,2,1:T(8,128)(2,1)S(1)}, bf16[512,16,8]{0,2,1:T(8,128)(2,1)}, u32[]{:S(2)}) copy-start(bf16[512,16,8]{0,2,1:T(8,128)(2,1)} %get-tuple-element.118) | copy-start | bytes 393220
  275.8 111.0 %reduce-scatter.9.cloned.1.call-start = ((), (), s32[]{:S(2)}) async-start(), calls=%async_computation.13 | async-start | bytes 6291456 | tf_op jit(solution)/shard_map/reduce_scatter | solution.py:252
  293.0 174.2 %all-gather.16.cloned.1.call-start = ((), (), s32[]{:S(2)}) async-start(), calls=%async_computation.10 | async-start | bytes 8650752 | tf_op jit(solution)/shard_map/all_gather | solution.py:95
  293.8 252.4 %all-gather.18.cloned.1.call-start = ((), (), s32[]{:S(2)}) async-start(), calls=%async_computation.11 | async-start | bytes 8650752 | tf_op jit(solution)/shard_map/all_gather | solution.py:97
  294.5 16.9 %copy-start.6 = (bf16[1,512,1024]{2,1,0:T(8,128)(2,1)S(1)}, bf16[1,512,1024]{2,1,0:T(8,128)(2,1)}, u32[]{:S(2)}) copy-start(bf16[1,512,1024]{2,1,0:T(8,128)(2,1)} %param.17) | copy-start | bytes 3145732
  294.5 395.3 %reduce-scatter.13.cloned.1.call-start = ((), (), s32[]{:S(2)}) async-start(), calls=%async_computation.15 | async-start | bytes 4325376 | tf_op jit(solution)/shard_map/reduce_scatter | solution.py:275
  314.7 533.7 %reduce-scatter.11.cloned.1.call-start = ((), (), s32[]{:S(2)}) async-start(), calls=%async_computation.14 | async-start | bytes 12976128 | tf_op jit(solution)/shard_map/reduce_scatter | solution.py:273
  333.2 57.1 %copy-start = (bf16[1,512,1024]{2,1,0:T(8,128)(2,1)S(1)}, bf16[1,512,1024]{2,1,0:T(8,128)(2,1)}, u32[]{:S(2)}) copy-start(bf16[1,512,1024]{2,1,0:T(8,128)(2,1)} %param.15) | copy-start | bytes 3145732
  333.2 57.1 %copy-start.14 = (f32[1024]{0:T(1024)S(1)}, f32[1024]{0:T(1024)}, u32[]{:S(2)}) copy-start(f32[1024]{0:T(1024)} %copy-done.13) | copy-start | bytes 12292
  333.2 57.1 %copy-start.16 = (f32[512]{0:T(512)S(1)}, f32[512]{0:T(512)}, u32[]{:S(2)}) copy-start(f32[512]{0:T(512)} %copy-done.15) | copy-start | bytes 6148
  333.2 57.1 %copy-start.18 = (f32[512]{0:T(512)S(1)}, f32[512]{0:T(512)}, u32[]{:S(2)}) copy-start(f32[512]{0:T(512)} %copy-done.17) | copy-start | bytes 6148
  333.2 57.1 %copy-start.23 = (f32[1024]{0:T(1024)S(1)}, f32[1024]{0:T(1024)}, u32[]{:S(2)}) copy-start(f32[1024]{0:T(1024)} %copy-done.22) | copy-start | bytes 12292
  397.3 810.5 %reduce-scatter.15.cloned.1.call-start = ((), (), s32[]{:S(2)}) async-start(), calls=%async_computation.16 | async-start | bytes 17301504 | tf_op jit(solution)/shard_map/reduce_scatter | solution.py:279
  467.3 78.9 %copy-start.7 = (bf16[1,512,1024]{2,1,0:T(8,128)(2,1)S(1)}, bf16[1,512,1024]{2,1,0:T(8,128)(2,1)}, u32[]{:S(2)}) copy-start(bf16[1,512,1024]{2,1,0:T(8,128)(2,1)} %param.17) | copy-start | bytes 3145732
  570.0 999.4 %reduce-scatter.17.cloned.1.call-start = ((), (), s32[]{:S(2)}) async-start(), calls=%async_computation.17 | async-start | bytes 17301504 | tf_op jit(solution)/shard_map/reduce_scatter | solution.py:281
  581.4 8.3 copy-start.29
  581.4 8.3 copy-start.31
  599.1 9.2 copy-start.8
  651.4 918.4 %copy-start.32 = (f32[32]{0:T(128)}, f32[32]{0:T(128)S(1)}, u32[]{:S(2)}) copy-start(f32[32]{0:T(128)S(1)} %dynamic-slice.6) | copy-start | bytes 388
  (16 other events, 43.2 us)
Sparse Core Ops, SparseCore 0:
  10.9 72.3 all-gather.7
  86.3 54.9 all-gather.13
  143.4 31.9 all-gather.11
  177.4 33.1 all-gather.9
  275.9 54.2 reduce-scatter.6
  332.5 54.3 reduce-scatter.8
  389.8 77.3 all-gather.15
  470.2 75.9 all-gather.17
  549.1 140.7 reduce-scatter.12
  696.3 152.0 reduce-scatter.10
  851.3 356.4 reduce-scatter.14
  1210.7 358.6 reduce-scatter.16
where the time goes:
time: 1590 us; the launch traced here: 1580 us
  waiting for transfers between devices  1110 us (70%)
  matrix products  208 us (13%)
  blocking collectives  156 us (10%)
  other arithmetic  57.8 us (4%)
  local copies, waits for them, and re-layouts  32.5 us (2%)
    reduce_scatter x1, waiting for transfers between devices, local(): lax.psum_scatter(narrow_grad, ('batch', 'seq'), scatter_dimension=0, tile...  362 us
    reduce_scatter x1, waiting for transfers between devices, local(): lax.psum_scatter(widen_grad, ('batch', 'seq'), scatter_dimension=0, tiled...  359 us
    reduce_scatter x1, waiting for transfers between devices, local(): lax.psum_scatter(mixer_grad, ('batch', 'seq'), scatter_dimension=0, tiled...  159 us
    unnamed x2, blocking collectives  83.5 us
    all_gather x1, blocking collectives, local(): lax.all_gather(shards[9], ('batch', 'seq'), axis=0, tiled=True)  67.2 us
    reduce_scatter x1, waiting for transfers between devices, local(): lax.psum_scatter(value_grad.reshape(seqs, length, width), 'seq', scatter_...  53.3 us
    all_gather x1, waiting for transfers between devices, local(): lax.all_gather(shards[10], ('batch', 'seq'), axis=0, tiled=True)  51.1 us
    all_gather x1, waiting for transfers between devices, local(): lax.all_gather(shards[4], ('batch', 'seq'), axis=0, tiled=True)  36.6 us
  transfers between devices with their start and end apart: 12, of which 12 were waited for; matrix products, arithmetic and copies ran while one was open for 14% of the time, Pallas kernels for 0%

commit v1 on v0

v1 whole, which is shorter than its diff:
```python
import functools

import jax
import jax.numpy as jnp
from jax import lax
from jax.experimental import pallas as pl
from jax.experimental.pallas import tpu as pltpu
from jax.sharding import PartitionSpec as P

HD = 64
ROT = 16
EPS = 1e-05
SCALE = 0.125
F32 = jnp.float32
BF = jnp.bfloat16


def dot(left, right, left_dim, right_dim):
    return lax.dot_general(
        left, right, (((left_dim,), (right_dim,)), ((), ())), preferred_element_type=F32
    )


def swap_batch(value, mask):
    count = lax.axis_size("batch")
    return lax.ppermute(value, "batch", [(i, i ^ mask) for i in range(count)])


def swap_seq(value, mask):
    count = lax.axis_size("seq")
    return lax.ppermute(value, "seq", [(i, i ^ mask) for i in range(count)])


def swap_member(value, mask):
    members = 2 * lax.axis_size("seq")
    count = lax.axis_size("batch") * lax.axis_size("seq")
    return lax.ppermute(
        value,
        ("batch", "seq"),
        [(i, (i // members) * members + ((i % members) ^ mask)) for i in range(count)],
    )


def put_kernel(count, first_of, *refs):
    parts, out, sem = refs[:count], refs[count], refs[count + 1]
    copies = []
    for k in range(count):
        copy = pltpu.make_async_copy(parts[k], out.at[first_of(k)], sem.at[k])
        copy.start()
        copies.append(copy)
    for copy in copies:
        copy.wait()


def assemble(parts, place):
    count = len(parts)
    return pl.pallas_call(
        functools.partial(put_kernel, count, place),
        out_shape=jax.ShapeDtypeStruct((count,) + parts[0].shape, parts[0].dtype),
        in_specs=[pl.BlockSpec(memory_space=pl.ANY)] * count,
        out_specs=pl.BlockSpec(memory_space=pl.ANY),
        scratch_shapes=[pltpu.SemaphoreType.DMA((count,))],
    )(*parts)


def gather_groups(chunk):
    groups = lax.axis_size("batch") // 2
    far = [chunk] + [swap_batch(chunk, 4 * k) for k in range(1, groups // 2)]
    near = [swap_batch(part, 2) for part in far]
    parts = [part for pair in zip(far, near) for part in pair]
    return assemble(parts, lambda k: (lax.axis_index("batch") // 2) ^ k)


def reduce_groups(value):
    groups, rows, width = value.shape
    group = lax.axis_index("batch") // 2
    near = group % 2
    far = group // 2
    halves = value.astype(BF).reshape(groups // 2, 2, rows, width)
    other = swap_batch(lax.dynamic_index_in_dim(halves, 1 - near, 1, keepdims=False), 2)
    mine = lax.dynamic_index_in_dim(halves, near, 1, keepdims=False)
    summed = (mine.astype(F32) + other.astype(F32)).astype(BF)
    total = lax.dynamic_index_in_dim(summed, far, 0, keepdims=False).astype(F32)
    for k in range(1, groups // 2):
        piece = lax.dynamic_index_in_dim(summed, far ^ k, 0, keepdims=False)
        total = total + swap_batch(piece, 4 * k).astype(F32)
    return total


def exchange_members(pieces):
    members = pieces.shape[0]
    seq = lax.axis_size("seq")
    me = (lax.axis_index("batch") % 2) * seq + lax.axis_index("seq")
    out = jnp.zeros_like(pieces)
    for k in range(members):
        piece = lax.dynamic_index_in_dim(pieces, me ^ k, 0, keepdims=True)
        got = piece if k == 0 else swap_member(piece, k)
        out = lax.dynamic_update_slice_in_dim(out, got, me ^ k, 0)
    return out


def join_tokens(value):
    seq = lax.axis_size("seq")
    here = lax.axis_index("seq")
    stretch = value.shape[1]
    if seq == 2:
        got = swap_seq(value, 1)
        out = jnp.zeros((value.shape[0], 2 * stretch, value.shape[2]), value.dtype)
        out = lax.dynamic_update_slice_in_dim(out, value, here * stretch, 1)
        whole = lax.dynamic_update_slice_in_dim(out, got, (1 - here) * stretch, 1)
    else:
        whole = lax.all_gather(value, "seq", axis=1, tiled=True)
    return jnp.concatenate([whole, swap_batch(whole, 1)], 0)


def part_tokens(value):
    seqs, length, width = value.shape
    seqs = seqs // 2
    seq = lax.axis_size("seq")
    here = lax.axis_index("seq")
    mine = value[:seqs].astype(F32) + swap_batch(value[seqs:].astype(BF), 1).astype(F32)
    stretch = length // seq
    if seq == 2:
        away = lax.dynamic_slice_in_dim(mine, (1 - here) * stretch, stretch, 1).astype(BF)
        keep = lax.dynamic_slice_in_dim(mine, here * stretch, stretch, 1)
        return keep + swap_seq(away, 1).astype(F32)
    return lax.psum_scatter(mine.astype(BF), "seq", scatter_dimension=1, tiled=True).astype(F32)


def attend_kernel(heads, block, q_ref, k_ref, v_ref, g_ref, c_ref, a_ref, b_ref, col_ref, row_ref, mixed_ref, grad_ref):
    length = q_ref.shape[0]
    half = ROT // 2
    cosine, up, down = c_ref[0], a_ref[0], b_ref[0]

    def roll(value, shift):
        if value.shape[1] % 128:
            return jnp.concatenate([value[:, -shift:], value[:, :-shift]], 1)
        return pltpu.roll(value, shift % value.shape[1], 1)

    def turn(value):
        return value * cosine - roll(value, -half) * up + roll(value, half) * down

    def turn_back(value):
        return value * cosine + roll(value, -half) * up - roll(value, half) * down

    query = (turn(q_ref[...]).astype(BF).astype(F32) * SCALE).astype(BF)
    keys = turn(k_ref[...]).astype(BF)
    values = v_ref[...].astype(BF)
    grads = g_ref[...]
    col = col_ref[0]
    row = row_ref[0]
    dq_all, dk_all, dv_all, mixed_all = [], [], [], []
    for h in range(heads):
        span = slice(h * HD, (h + 1) * HD)
        qh, kh, vh, gh = query[:, span], keys[:, span], values[:, span], grads[:, span]
        dq_parts, mixed_parts = [], []
        dk = jnp.zeros((length, HD), F32)
        dv = jnp.zeros((length, HD), F32)
        for i in range(length // block):
            n = (i + 1) * block
            rows = slice(i * block, n)
            q, g = qh[rows], gh[rows]
            k, v = kh[:n], vh[:n]
            scores = dot(q, k, 1, 1)
            place_q = lax.broadcasted_iota(jnp.int32, (block, n), 0) + i * block
            place_k = lax.broadcasted_iota(jnp.int32, (block, n), 1)
            allowed = (col[rows] == row[:, :n]) & (place_q >= place_k)
            scores = jnp.where(allowed, scores, -1e30)
            expo = jnp.exp(scores - jnp.max(scores, -1, keepdims=True))
            prob = expo * (1.0 / jnp.sum(expo, -1, keepdims=True))
            prob_b = prob.astype(BF)
            mixed_parts.append(dot(prob_b, v, 1, 0))
            prob_grad = dot(g, v, 1, 1)
            center = jnp.sum(prob * prob_grad, -1, keepdims=True)
            score_grad = (prob * (prob_grad - center)).astype(BF)
            dq_parts.append(dot(score_grad, k, 1, 0) * SCALE)
            dk_add = dot(score_grad, q, 0, 0)
            dv_add = dot(prob_b, g, 0, 0)
            if n < length:
                zeros = jnp.zeros((length - n, HD), F32)
                dk_add = jnp.concatenate([dk_add, zeros], 0)
                dv_add = jnp.concatenate([dv_add, zeros], 0)
            dk = dk + dk_add
            dv = dv + dv_add
        dq_all.append(jnp.concatenate(dq_parts, 0))
        mixed_all.append(jnp.concatenate(mixed_parts, 0))
        dk_all.append(dk)
        dv_all.append(dv)
    mixed_ref[...] = jnp.concatenate(mixed_all, 1).astype(BF)
    grad_ref[0] = turn_back(jnp.concatenate(dq_all, 1)).astype(BF)
    grad_ref[1] = turn_back(jnp.concatenate(dk_all, 1)).astype(BF)
    grad_ref[2] = jnp.concatenate(dv_all, 1).astype(BF)


def attend(project, mixed_grad, tables, segs):
    seqs, length = segs.shape
    rows, wide = project.shape
    width = wide // 3
    heads = min(2, width // HD)
    lanes = heads * HD
    steps = width // lanes
    block = min(256, length)

    parts = (project, project, project)
    ahead = steps
    if lanes % 128:
        parts = tuple(jnp.split(project, 3, 1))
        ahead = 0

    def of(part):
        return pl.BlockSpec((length, lanes), lambda s, h: (s, part * ahead + h))

    table = pl.BlockSpec((1, length, lanes), lambda s, h: (s, 0, 0))
    cost = pl.CostEstimate(
        flops=seqs * (width // HD) * length * length * HD * 12,
        bytes_accessed=rows * width * 24,
        transcendentals=seqs * (width // HD) * length * length,
    )
    return pl.pallas_call(
        functools.partial(attend_kernel, heads, block),
        grid=(seqs, steps),
        in_specs=[
            of(0),
            of(1),
            of(2),
            of(0),
            table,
            table,
            table,
            pl.BlockSpec((1, length, 1), lambda s, h: (s, 0, 0)),
            pl.BlockSpec((1, 1, length), lambda s, h: (s, 0, 0)),
        ],
        out_specs=(
            pl.BlockSpec((length, lanes), lambda s, h: (s, h)),
            pl.BlockSpec((3, length, lanes), lambda s, h: (0, s, h)),
        ),
        out_shape=(
            jax.ShapeDtypeStruct((rows, width), BF),
            jax.ShapeDtypeStruct((3, rows, width), BF),
        ),
        cost_estimate=cost,
        compiler_params=pltpu.CompilerParams(vmem_limit_bytes=56 * 1024 * 1024),
    )(*parts, mixed_grad, *tables, segs[:, :, None], segs[:, None, :])


def turn_tables(position, lanes):
    half = ROT // 2
    freq = 10000.0 ** (-(jnp.arange(half).astype(F32) * 2.0) / float(ROT))
    phase = position.astype(F32)[..., None] * freq
    cosine, sine = jnp.cos(phase), jnp.sin(phase)
    rest = phase.shape[:-1] + (HD - ROT,)
    none = jnp.zeros_like(sine)
    heads = lanes // HD

    def lay(*pieces):
        return jnp.tile(jnp.concatenate(pieces, -1), (1, 1, heads))

    return (
        lay(cosine, cosine, jnp.ones(rest, F32)),
        lay(sine, none, jnp.zeros(rest, F32)),
        lay(none, sine, jnp.zeros(rest, F32)),
    )


def local(
    tokens,
    segments,
    cotangent,
    mixer_gain,
    mixer_shift,
    mixer_weight,
    mixer_bias,
    merger_weight,
    merger_bias,
    feeder_gain,
    feeder_shift,
    widen_weight,
    widen_bias,
    narrow_weight,
    narrow_bias,
):
    seqs, stretch, width = tokens.shape
    seq = lax.axis_size("seq")
    groups = lax.axis_size("batch") // 2
    members = 2 * seq
    devices = groups * members
    length = stretch * seq
    here = lax.axis_index("seq")
    me = (lax.axis_index("batch") % 2) * seq + here
    share = mixer_weight.shape[0]
    hidden = widen_weight.shape[1]
    slim = width // members
    unit = hidden // devices
    every = ("batch", "seq")

    vectors = (
        mixer_gain,
        mixer_shift,
        mixer_bias,
        merger_bias,
        feeder_gain,
        feeder_shift,
        widen_bias,
        narrow_bias,
    )
    sizes = [v.shape[0] for v in vectors]
    cuts = [sum(sizes[: i + 1]) for i in range(len(sizes) - 1)]
    gathered = lax.all_gather(jnp.concatenate(vectors), every, axis=0, tiled=False)
    gain_m, shift_m, bias_m, bias_o, gain_f, shift_f, bias_w, bias_n = [
        v.reshape(-1).astype(F32) for v in jnp.split(gathered, cuts, 1)
    ]
    merger_all = lax.all_gather(merger_weight, every, axis=0, tiled=True)
    merger = lax.dynamic_slice_in_dim(merger_all, me * slim, slim, 0)
    mixer_pieces = mixer_weight.reshape(share, 3, members, slim).transpose(2, 0, 1, 3)
    widen_pieces = widen_weight.reshape(share, groups, members, unit).transpose(2, 0, 1, 3)
    pieces = jnp.concatenate(
        [
            mixer_pieces.reshape(members, share, 3 * slim),
            widen_pieces.reshape(members, share, groups * unit),
        ],
        -1,
    )
    chunks = exchange_members(pieces).reshape(members * share, -1)
    mixer = gather_groups(chunks[:, : 3 * slim]).reshape(width, 3 * slim)
    widen = gather_groups(chunks[:, 3 * slim :]).reshape(width, groups * unit)
    narrow = gather_groups(narrow_weight).reshape(groups * unit, width)
    bias_m_mine = lax.dynamic_index_in_dim(bias_m.reshape(3, members, slim), me, 1, keepdims=False)
    bias_w_mine = lax.dynamic_index_in_dim(bias_w.reshape(groups, members, unit), me, 1, keepdims=False)

    inputs = join_tokens(tokens)
    upstream = join_tokens(cotangent).reshape(-1, width)
    segs = join_tokens(segments[:, :, None])[:, :, 0]
    place = jnp.arange(length, dtype=jnp.int32)
    earlier = jnp.sum((segs[:, None, :] < segs[:, :, None]).astype(jnp.int32), -1)
    tables = turn_tables(place[None, :] - earlier, min(2, slim // HD) * HD)

    def centre(rows):
        mean = jnp.mean(rows, -1, keepdims=True)
        centered = rows - mean
        spread = jnp.mean(centered * centered, -1, keepdims=True)
        rstd = lax.rsqrt(spread + EPS)
        return centered * rstd, rstd

    flat = inputs.astype(F32).reshape(-1, width)
    normed, _ = centre(flat)
    first = (normed * gain_m + shift_m).astype(BF)
    second = (normed * gain_f + shift_f).astype(BF)

    project = dot(first, mixer, 1, 0) + bias_m_mine.reshape(-1)
    mixed_grad = dot(upstream, merger, 1, 1).astype(BF)
    mixed, project_grad = attend(project, mixed_grad, tables, segs)

    widened = dot(second, widen, 1, 0) + bias_w_mine.reshape(-1)
    bell = 0.5 * (1.0 + lax.erf(widened * (0.5**0.5)))
    active = (widened * bell).astype(BF)
    slope = bell + widened * jnp.exp(-0.5 * widened * widened) * (0.15915494309189535**0.5)
    narrow_grad = dot(active, upstream, 0, 0).astype(BF)
    narrow_out = reduce_groups(narrow_grad.reshape(groups, unit, width))
    widened_grad = (dot(upstream, narrow, 1, 1) * slope).astype(BF)
    widen_bias_grad = jnp.sum(widened_grad, 0, dtype=F32)
    widen_grad = dot(second, widened_grad, 0, 0).astype(BF)
    widen_sum = reduce_groups(widen_grad.reshape(groups, members * share, groups * unit))
    second_grad = dot(widened_grad, widen, 1, 1)

    partial = dot(mixed, merger, 1, 0) + dot(active, narrow, 1, 0)
    own = tokens.astype(F32)
    layer_output = (own + part_tokens(partial.reshape(2 * seqs, length, width)) + (bias_o + bias_n)).astype(BF)

    merger_grad = dot(mixed, upstream, 0, 0)
    mixer_grad = jnp.concatenate([dot(first, project_grad[i], 0, 0).astype(BF) for i in range(3)], 1)
    mixer_sum = reduce_groups(mixer_grad.reshape(groups, members * share, 3 * slim))
    first_grad = sum(
        dot(project_grad[i], mixer[:, i * slim : (i + 1) * slim], 1, 1) for i in range(3)
    )
    mixer_bias_grad = jnp.sum(project_grad, 1, dtype=F32)
    backs = exchange_members(
        jnp.concatenate([mixer_sum, widen_sum], 1).reshape(members, share, -1).astype(BF)
    ).astype(F32)
    mixer_out = backs[:, :, : 3 * slim].reshape(members, share, 3, slim).transpose(1, 2, 0, 3)
    widen_out = backs[:, :, 3 * slim :].reshape(members, share, groups, unit).transpose(1, 2, 0, 3)
    merger_full = lax.dynamic_update_slice_in_dim(
        jnp.zeros((width, width), BF), merger_grad.astype(BF), me * slim, 0
    )
    merger_out = lax.psum_scatter(merger_full, every, scatter_dimension=0, tiled=True).astype(F32)

    error = first_grad * gain_m + second_grad * gain_f
    error = part_tokens(error.reshape(2 * seqs, length, width))
    normed_own, rstd_own = centre(own)
    back = rstd_own * (
        error
        - jnp.mean(error, -1, keepdims=True)
        - normed_own * jnp.mean(error * normed_own, -1, keepdims=True)
    )
    tokens_grad = (cotangent.astype(F32) + back).astype(BF)

    def spread_out(value, lead):
        shape = (lead, members, value.size // lead)
        return lax.dynamic_update_slice_in_dim(
            jnp.zeros(shape, F32), value.reshape(lead, 1, -1), me, 1
        )

    bias_grad = jnp.sum(cotangent.astype(F32), (0, 1))
    sums = (
        jnp.sum(first_grad * normed, 0),
        jnp.sum(first_grad, 0),
        spread_out(mixer_bias_grad, 3),
        bias_grad,
        jnp.sum(second_grad * normed, 0),
        jnp.sum(second_grad, 0),
        spread_out(widen_bias_grad, groups),
        bias_grad,
    )
    packed = jnp.concatenate([v.reshape(devices, -1) for v in sums], 1)
    owned = lax.psum_scatter(packed, every, scatter_dimension=0, tiled=False)
    gain_m_out, shift_m_out, bias_m_out, bias_o_out, gain_f_out, shift_f_out, bias_w_out, bias_n_out = jnp.split(owned, cuts)
    return (
        layer_output,
        tokens_grad,
        gain_m_out,
        shift_m_out,
        mixer_out.reshape(mixer_weight.shape),
        bias_m_out,
        merger_out,
        bias_o_out,
        gain_f_out,
        shift_f_out,
        widen_out.reshape(widen_weight.shape),
        bias_w_out,
        narrow_out,
        bias_n_out,
    )


def solution(mesh):
    vector = P(("batch", "seq"))
    matrix = P(("batch", "seq"), None)
    rows = P("batch", "seq", None)
    params = (vector, vector, matrix, vector, matrix, vector, vector, vector, matrix, vector, matrix, vector)
    return jax.shard_map(
        local,
        mesh=mesh,
        in_specs=(rows, P("batch", "seq"), rows) + params,
        out_specs=(rows, rows) + params,
        check_vma=False,
    )
```

time: 1590 us -> 763 us (0.48)
  waiting for transfers between devices: 1110 us -> 139 us
  Pallas kernels: 0 us -> 220 us
  matrix products: 208 us -> 91.5 us
  starting transfers between devices: 1.3 us -> 59.5 us
  blocking collectives: 156 us -> 105 us
  local copies, waits for them, and re-layouts: 32.5 us -> 77.5 us
    reduce_scatter x6 -> x1, waiting for transfers between devices: 971 us -> 0.01 us  [local(): lax.psum_scatter(merger_full, every, scatter_dimension=0, tiled=True)]
    pallas_call x0 -> x4, Pallas kernels: none -> 220 us  [the longest x3 178 us: assemble(): pl.pallas_call(functools.partial(put_kernel, count, place), out_shape=jax...]
    ppermute x0 -> x49, waiting for transfers between devices: none -> 139 us  [the longest x38 80.5 us: swap_batch(): return lax.ppermute(value, 'batch', [(i, i ^ mask) for i in range(count)])]
    all_gather x6 -> x1, waiting for transfers between devices: 134 us -> 0.01 us  [local(): merger_all = lax.all_gather(merger_weight, every, axis=0, tiled=True)]
    dot_general x18 -> x16, matrix products: 208 us -> 91.5 us  [dot(): lax.dot_general(left, right, (((left_dim,), (right_dim,)), ((), ())), pre...]
    all_gather x2 -> x0, blocking collectives: 72 us -> none  [the longest x1 67.2 us: local(): lax.all_gather(shards[9], ('batch', 'seq'), axis=0, tiled=True)]
    ppermute x0 -> x49, starting transfers between devices: none -> 59.4 us  [the longest x38 51.3 us: swap_batch(): return lax.ppermute(value, 'batch', [(i, i ^ mask) for i in range(count)])]
    unnamed x2, blocking collectives: 83.5 us -> 105 us
  transfers between devices with their start and end apart: 12 -> 51, of which waited for: 12 -> 21; matrix products, arithmetic and copies ran while one was open for 14% -> 27% of each run, Pallas kernels for 0% -> 29%
where the time goes in v1:
time: 763 us; the launch traced here: 751 us
  Pallas kernels  220 us (29%)
  waiting for transfers between devices  139 us (18%)
  blocking collectives  105 us (14%)
  matrix products  91.5 us (12%)
  local copies, waits for them, and re-layouts  77.5 us (10%)
  starting transfers between devices  59.5 us (8%)
  other arithmetic  43.9 us (6%)
  between operations  15.4 us (2%)
    pallas_call x3, Pallas kernels, assemble(): pl.pallas_call(functools.partial(put_kernel, count, place), out_shape=jax...  178 us
    unnamed x2, blocking collectives  105 us
    dot_general x16, matrix products, dot(): lax.dot_general(left, right, (((left_dim,), (right_dim,)), ((), ())), pre...  91.5 us
    ppermute x38, waiting for transfers between devices, swap_batch(): return lax.ppermute(value, 'batch', [(i, i ^ mask) for i in range(count)])  80.5 us
    ppermute x5, waiting for transfers between devices, swap_seq(): return lax.ppermute(value, 'seq', [(i, i ^ mask) for i in range(count)])  55.2 us
    ppermute x38, starting transfers between devices, swap_batch(): return lax.ppermute(value, 'batch', [(i, i ^ mask) for i in range(count)])  51.3 us
    pallas_call x1, Pallas kernels, attend(): pl.pallas_call(functools.partial(attend_kernel, heads, block), grid=(seqs...  41.4 us
    unnamed x127, local copies, waits for them, and re-layouts  17.9 us
  transfers between devices with their start and end apart: 51, of which 21 were waited for; matrix products, arithmetic and copies ran while one was open for 27% of the time, Pallas kernels for 29%

profile of v1, /device:TPU:0, one launch (start us, length us, event | category | flops | bytes accessed | tf_op | source)
XLA Modules:
  0.0 751.4 jit_solution(5578803085128379715)
XLA Ops:
  21.6 58.0 %all-reduce = bf16[13312]{0:T(1024)(128)(2,1)S(1)} all-reduce(bf16[13312]{0:T(1024)(128)(2,1)S(1)} %dynamic-update-slice), channel_id=2, replica_groups=mesh['batch'=16,'seq'=2] {'batch','seq'}, use_global_device_ids=true, to_apply=%add | all-reduce | flops 13312 | bytes 53248
  112.3 5.4 collective-permute-done.6.refs_2_
  133.2 6.0 collective-permute-done.19.refs_4_
  161.7 5.2 collective-permute-done.27.refs_5_
  167.4 5.0 collective-permute-done.29.refs_7_
  181.9 48.8 %shard_map.254 = bf16[8,128,768]{2,1,0:T(8,128)(2,1)} custom-call(bf16[128,768]{1,0:T(8,128)(2,1)} %copy-done.23, bf16[128,768]{1,0:T(8,128)(2,1)} %copy-done.35, bf16[128,768]{1,0:T(8,128)(2,1)} %copy-done.31, bf16[128,768]{1,0:T(8,128)(2,1)} %copy-done.37, bf16[128,768]{1,0:T(8,128)(2,1)} %copy-done.33, bf16[128,768]{1,0:T(8,128)(2,1)} %copy-done.38, ...), custom_call_target="tpu_custom_call" | custom-call | tf_op jit(solution)/shard_map/pallas_call | solution.py:57
  230.7 64.7 %shard_map.257 = bf16[8,128,1024]{2,1,0:T(8,128)(2,1)} custom-call(bf16[128,1024]{1,0:T(8,128)(2,1)} %refs_0_.1, bf16[128,1024]{1,0:T(8,128)(2,1)} %copy-done.27, bf16[128,1024]{1,0:T(8,128)(2,1)} %collective-permute-done.24.refs_2_, bf16[128,1024]{1,0:T(8,128)(2,1)} %copy-done.29, bf16[128,1024]{1,0:T(8,128)(2,1)} %collective-permute-done.26.refs_4_, ...), custom_call_target="tpu_custom_call" | custom-call | tf_op jit(solution)/shard_map/pallas_call | solution.py:57
  295.5 64.7 %shard_map.256 = bf16[8,128,1024]{2,1,0:T(8,128)(2,1)} custom-call(bf16[128,1024]{1,0:T(8,128)(2,1)} %copy-done.22, bf16[128,1024]{1,0:T(8,128)(2,1)} %copy-done.28, bf16[128,1024]{1,0:T(8,128)(2,1)} %collective-permute-done.17.refs_2_, bf16[128,1024]{1,0:T(8,128)(2,1)} %collective-permute-done.18.refs_3_, ...), custom_call_target="tpu_custom_call" | custom-call | tf_op jit(solution)/shard_map/pallas_call | solution.py:57
  367.5 5.1 add_convert_fusion.1
  372.5 9.7 %multiply_convert_fusion = (bf16[2048,1024]{1,0:T(8,128)(2,1)S(1)}, f32[2048,1024]{1,0:T(8,128)S(1)}) fusion(f32[1024]{0:T(1024)S(1)} %bitcast.208, bf16[2048,1024]{1,0:T(8,128)(2,1)S(1)} %bitcast.180, bf16[1024,1024]{1,0:T(8,128)(2,1)S(1)} %bitcast.195), kind=kOutput, calls=%fused_computation.15 | convolution fusion | flops 4307550208 | bytes 18878464 | tf_op jit(solution)/shard_map/dot_general | solution.py:19
  385.8 5.2 convolution_convert_fusion.1
  394.9 9.1 %convert_reduce_fusion = (f32[1024]{0:T(1024)S(1)}, bf16[2048,1024]{1,0:T(8,128)(2,1)}) fusion(f32[2048,1024]{1,0:T(8,128)S(1)} %get-tuple-element.71, f32[1024]{0:T(1024)S(1)} %bitcast.209, bf16[2048,1024]{1,0:T(8,128)(2,1)S(1)} %bitcast.182, bf16[1024,1024]{1,0:T(8,128)(2,1)S(1)} %bitcast.193), kind=kOutput, calls=%fused_computation.10 | convolution fusion | flops 4322229248 | bytes 18882560 | tf_op jit(solution)/shard_map/dot_general | solution.py:19
  404.1 8.8 %convolution_add_fusion.1.q_ref.k_ref.v_ref = f32[2048,768]{1,0:T(8,128)} fusion(bf16[2048,1024]{1,0:T(8,128)(2,1)} %bitcast.176, bf16[1024,768]{1,0:T(8,128)(2,1)} %bitcast.168, f32[768]{0:T(1024)S(1)} %add.301), kind=kOutput, calls=%fused_computation.32 | convolution fusion | flops 3222798336 | bytes 12061696 | tf_op jit(solution)/shard_map/dot_general | solution.py:19
  412.8 4.6 convolution_convert_fusion.g_ref
  417.4 41.4 %shard_map.255 = (bf16[2048,256]{1,0:T(8,128)(2,1)}, bf16[3,2048,256]{2,1,0:T(8,128)(2,1)}) custom-call(f32[2048,768]{1,0:T(8,128)} %convolution_add_fusion.1.q_ref.k_ref.v_ref, f32[2048,768]{1,0:T(8,128)} %convolution_add_fusion.1.q_ref.k_ref.v_ref, f32[2048,768]{1,0:T(8,128)} %convolution_add_fusion.1.q_ref.k_ref.v_ref, ...), custom_call_target="tpu_custom_call" | custom-call | flops 6442450944 | bytes 12582912 | tf_op jit(solution)/shard_map/pallas_call | solution.py:219
  464.3 4.6 fusion.32
  468.9 4.7 fusion.35
  478.6 6.8 constant_dynamic-slice_fusion.4
  485.4 4.6 copy.81
  490.6 4.7 copy.80
  495.3 7.7 %add_add_fusion = f32[2048,1024]{1,0:T(8,128)S(1)} fusion(f32[2048,1024]{1,0:T(8,128)} %fusion.35, f32[2048,1024]{1,0:T(8,128)} %fusion.32, bf16[3,2048,256]{2,1,0:T(8,128)(2,1)} %get-tuple-element.17, bf16[1024,768]{1,0:T(8,128)(2,1)} %bitcast.169), kind=kOutput, calls=%fused_computation.14 | convolution fusion | flops 1077936128 | bytes 26738688 | tf_op jit(solution)/shard_map/dot_general | solution.py:19
  503.0 13.2 %fusion.64 = (f32[1024]{0:T(1024)S(1)}, f32[1024]{0:T(1024)S(1)}, f32[2048,1024]{1,0:T(8,128)}, f32[1024]{0:T(1024)S(1)}, f32[1024]{0:T(1024)S(1)}, /*index=5*/bf16[2048,1024]{1,0:T(8,128)(2,1)}) fusion(f32[2048]{0:T(1024)S(1)} %get-tuple-element.75, f32[2048]{0:T(1024)S(1)} %get-tuple-element.76, bf16[1,1024,1024]{2,1,0:T(8,128)(2,1)} %collective-permute-done.1, ...), kind=kOutput, calls=%fused_computation.179 | convolution fusion | flops 4328517632 | bytes 31502336 | tf_op jit(solution)/shard_map/dot_general | solution.py:19
  516.2 8.2 %convolution_convert_fusion.2 = bf16[1024,1024]{1,0:T(8,128)(2,1)S(1)} fusion(bf16[2048,1024]{1,0:T(8,128)(2,1)} %get-tuple-element.27, bf16[2048,1024]{1,0:T(8,128)(2,1)} %get-tuple-element.73), kind=kOutput, calls=%fused_computation.60 | convolution fusion | flops 4296015872 | bytes 10485760 | tf_op jit(solution)/shard_map/dot_general | solution.py:19
  530.0 4.6 convolution_add_fusion
  558.7 6.1 collective-permute-done.35
  564.8 5.0 collective-permute-done.36
  573.3 4.9 collective-permute-done.39
  578.2 11.7 %collective-permute-start.46 = (bf16[128,1024]{1,0:T(8,128)(2,1)S(1)}, bf16[128,1024]{1,0:T(8,128)(2,1)S(1)}, u32[]{:S(2)}, u32[]{:S(2)}) collective-permute-start(bf16[128,1024]{1,0:T(8,128)(2,1)S(1)} %get-tuple-element.32), channel_id=1, source_target_pairs={{0,8},{2,10},{4,12},{6,14},{8,0},{10,2},{12,4},{14,6},{16,24},{18,... | collective-permute-start | bytes 786440 | tf_op jit(solution)/shard_map/ppermute | solution.py:26
  597.0 19.9 %collective-permute-done.47 = bf16[128,1024]{1,0:T(8,128)(2,1)S(1)} collective-permute-done((bf16[128,1024]{1,0:T(8,128)(2,1)S(1)}, bf16[128,1024]{1,0:T(8,128)(2,1)S(1)}, u32[]{:S(2)}, u32[]{:S(2)}) %collective-permute-start.47) | collective-permute-done | bytes 262176 | tf_op jit(solution)/shard_map/ppermute | solution.py:26
  632.7 26.6 %collective-permute-done.33 = bf16[1,512,1024]{2,1,0:T(8,128)(2,1)S(1)} collective-permute-done((bf16[1,512,1024]{2,1,0:T(8,128)(2,1)}, bf16[1,512,1024]{2,1,0:T(8,128)(2,1)S(1)}, u32[]{:S(2)}, u32[]{:S(2)}) %collective-permute-start.33) | collective-permute-done | bytes 1048608 | tf_op jit(solution)/shard_map/ppermute | solution.py:31
  661.7 28.6 %collective-permute-done.31 = bf16[1,512,1024]{2,1,0:T(8,128)(2,1)} collective-permute-done((bf16[1,512,1024]{2,1,0:T(8,128)(2,1)}, bf16[1,512,1024]{2,1,0:T(8,128)(2,1)}, u32[]{:S(2)}, u32[]{:S(2)}) %collective-permute-start.31) | collective-permute-done | bytes 1048608 | tf_op jit(solution)/shard_map/ppermute | solution.py:31
  694.3 46.7 %all-reduce.1 = f32[32,416]{1,0:T(8,128)S(1)} all-reduce(f32[32,416]{1,0:T(8,128)S(1)} %concatenate.42), channel_id=3, replica_groups=mesh['batch'=16,'seq'=2] {'batch','seq'}, use_global_device_ids=true, to_apply=%region_14.15.clone | all-reduce | flops 13312 | bytes 106496
  (346 shorter events, 185.6 us)
Async XLA Ops:
  7.3 405.6 %all-gather.3.cloned.1.call-start = ((), (), s32[]{:S(2)}) async-start(), calls=%async_computation.1 | async-start | bytes 2162688 | tf_op jit(solution)/shard_map/all_gather | solution.py:312
  7.3 93.8 %collective-permute-start.24 = (bf16[128,1024]{1,0:T(8,128)(2,1)}, bf16[128,1024]{1,0:T(8,128)(2,1)}, u32[]{:S(2)}, u32[]{:S(2)}) collective-permute-start(bf16[128,1024]{1,0:T(8,128)(2,1)} %refs_0_.1), channel_id=1, source_target_pairs={{0,8},{2,10},{4,12},{6,14},{8,0},{10,2},{12,4},{14,6},{16,24},{18,... | collective-permute-start | bytes 786440 | tf_op jit(solution)/shard_map/ppermute | solution.py:26
  10.4 92.4 %collective-permute-start.26 = (bf16[128,1024]{1,0:T(8,128)(2,1)}, bf16[128,1024]{1,0:T(8,128)(2,1)}, u32[]{:S(2)}, u32[]{:S(2)}) collective-permute-start(bf16[128,1024]{1,0:T(8,128)(2,1)} %refs_0_.1), channel_id=1, source_target_pairs={{0,16},{2,18},{4,20},{6,22},{8,24},{10,26},{12,28},{14,30},{16,0},... | collective-permute-start | bytes 786440 | tf_op jit(solution)/shard_map/ppermute | solution.py:26
  17.3 71.3 %collective-permute-start.2 = (bf16[1,32,1792]{2,1,0:T(8,128)(2,1)}, bf16[1,32,1792]{2,1,0:T(8,128)(2,1)}, u32[]{:S(2)}, u32[]{:S(2)}) collective-permute-start(bf16[1,32,1792]{2,1,0:T(8,128)(2,1)} %get-tuple-element.50), channel_id=1, source_target_pairs={{0,1},{1,0},{2,3},{3,2},{4,5},{5,4},{6,7},{7,6},{8,9},{9,8},{10,11... | collective-permute-start | bytes 344072 | tf_op jit(solution)/shard_map/ppermute | solution.py:37
  18.8 75.2 %collective-permute-start = (bf16[1,512,1024]{2,1,0:T(8,128)(2,1)S(1)}, bf16[1,512,1024]{2,1,0:T(8,128)(2,1)}, u32[]{:S(2)}, u32[]{:S(2)}) collective-permute-start(bf16[1,512,1024]{2,1,0:T(8,128)(2,1)S(1)} %copy-done), channel_id=1, source_target_pairs={{0,1},{1,0},{2,3},{3,2},{4,5},{5,4},{6,7},{7,6},{8,9},{9,8},{10,11... | collective-permute-start | bytes 3145736 | tf_op jit(solution)/shard_map/ppermute | solution.py:31
  19.4 723.5 %reduce-scatter.2.cloned.1.call-start = ((), (), s32[]{:S(2)}) async-start(), calls=%async_computation.2 | async-start | bytes 2162688 | tf_op jit(solution)/shard_map/reduce_scatter | solution.py:384
  19.4 65.6 %collective-permute-start.14 = (s32[1,512,1]{1,2,0:T(1,128)}, s32[1,512,1]{1,2,0:T(1,128)}, u32[]{:S(2)}, u32[]{:S(2)}) collective-permute-start(s32[1,512,1]{1,2,0:T(1,128)} %bitcast.6), channel_id=1, source_target_pairs={{0,1},{1,0},{2,3},{3,2},{4,5},{5,4},{6,7},{7,6},{8,9},{9,8},{10,11... | collective-permute-start | bytes 6152 | tf_op jit(solution)/shard_map/ppermute | solution.py:31
  85.0 17.8 %collective-permute-start.28 = (bf16[128,1024]{1,0:T(8,128)(2,1)S(1)}, bf16[128,1024]{1,0:T(8,128)(2,1)S(1)}, u32[]{:S(2)}, u32[]{:S(2)}) collective-permute-start(bf16[128,1024]{1,0:T(8,128)(2,1)S(1)} %copy-done.24), channel_id=1, source_target_pairs={{0,24},{2,26},{4,28},{6,30},{8,16},{10,18},{12,20},{14,22},{16,8},... | collective-permute-start | bytes 786440 | tf_op jit(solution)/shard_map/ppermute | solution.py:26
  99.2 263.4 %collective-permute-start.1 = (bf16[1,1024,1024]{2,1,0:T(8,128)(2,1)S(1)}, bf16[1,1024,1024]{2,1,0:T(8,128)(2,1)}, u32[]{:S(2)}, u32[]{:S(2)}) collective-permute-start(bf16[1,1024,1024]{2,1,0:T(8,128)(2,1)S(1)} %constant_dynamic-update-slice_fusion.10), channel_id=1, source_target_pairs={{0,2},{2,0},{4,6},{6,4},{8,10},{10,8},{12,14},{14,12},{16,18},{18,... | collective-permute-start | bytes 6291464 | tf_op jit(solution)/shard_map/ppermute | solution.py:26
  110.8 20.2 %collective-permute-start.17 = (bf16[128,1024]{1,0:T(8,128)(2,1)S(1)}, bf16[128,1024]{1,0:T(8,128)(2,1)}, u32[]{:S(2)}, u32[]{:S(2)}) collective-permute-start(bf16[128,1024]{1,0:T(8,128)(2,1)S(1)} %slice.80.refs_0_), channel_id=1, source_target_pairs={{0,8},{2,10},{4,12},{6,14},{8,0},{10,2},{12,4},{14,6},{16,24},{18,... | collective-permute-start | bytes 786440 | tf_op jit(solution)/shard_map/ppermute | solution.py:26
  117.8 21.5 %collective-permute-start.19 = (bf16[128,1024]{1,0:T(8,128)(2,1)S(1)}, bf16[128,1024]{1,0:T(8,128)(2,1)}, u32[]{:S(2)}, u32[]{:S(2)}) collective-permute-start(bf16[128,1024]{1,0:T(8,128)(2,1)S(1)} %slice.80.refs_0_), channel_id=1, source_target_pairs={{0,16},{2,18},{4,20},{6,22},{8,24},{10,26},{12,28},{14,30},{16,0},... | collective-permute-start | bytes 786440 | tf_op jit(solution)/shard_map/ppermute | solution.py:26
  119.5 20.3 %collective-permute-start.21 = (bf16[128,1024]{1,0:T(8,128)(2,1)S(1)}, bf16[128,1024]{1,0:T(8,128)(2,1)}, u32[]{:S(2)}, u32[]{:S(2)}) collective-permute-start(bf16[128,1024]{1,0:T(8,128)(2,1)S(1)} %slice.80.refs_0_), channel_id=1, source_target_pairs={{0,24},{2,26},{4,28},{6,30},{8,16},{10,18},{12,20},{14,22},{16,8},... | collective-permute-start | bytes 786440 | tf_op jit(solution)/shard_map/ppermute | solution.py:26
  120.9 20.4 %collective-permute-start.16 = (bf16[128,1024]{1,0:T(8,128)(2,1)S(1)}, bf16[128,1024]{1,0:T(8,128)(2,1)S(1)}, u32[]{:S(2)}, u32[]{:S(2)}) collective-permute-start(bf16[128,1024]{1,0:T(8,128)(2,1)S(1)} %slice.80.refs_0_), channel_id=1, source_target_pairs={{0,4},{2,6},{4,0},{6,2},{8,12},{10,14},{12,8},{14,10},{16,20},{18,... | collective-permute-start | bytes 786440 | tf_op jit(solution)/shard_map/ppermute | solution.py:26
  131.0 229.2 %collective-permute-start.12 = (bf16[1,512,1024]{2,1,0:T(8,128)(2,1)}, bf16[1,512,1024]{2,1,0:T(8,128)(2,1)}, u32[]{:S(2)}, u32[]{:S(2)}) collective-permute-start(bf16[1,512,1024]{2,1,0:T(8,128)(2,1)} %param.17), channel_id=1, source_target_pairs={{0,1},{1,0},{2,3},{3,2},{4,5},{5,4},{6,7},{7,6},{8,9},{9,8},{10,11... | collective-permute-start | bytes 3145736 | tf_op jit(solution)/shard_map/ppermute | solution.py:31
  161.1 134.3 %collective-permute-start.18 = (bf16[128,1024]{1,0:T(8,128)(2,1)}, bf16[128,1024]{1,0:T(8,128)(2,1)}, u32[]{:S(2)}, u32[]{:S(2)}) collective-permute-start(bf16[128,1024]{1,0:T(8,128)(2,1)} %collective-permute-done.17.refs_2_), channel_id=1, source_target_pairs={{0,4},{2,6},{4,0},{6,2},{8,12},{10,14},{12,8},{14,10},{16,20},{18,... | collective-permute-start | bytes 786440 | tf_op jit(solution)/shard_map/ppermute | solution.py:26
  166.8 128.6 %collective-permute-start.20 = (bf16[128,1024]{1,0:T(8,128)(2,1)}, bf16[128,1024]{1,0:T(8,128)(2,1)}, u32[]{:S(2)}, u32[]{:S(2)}) collective-permute-start(bf16[128,1024]{1,0:T(8,128)(2,1)} %collective-permute-done.19.refs_4_), channel_id=1, source_target_pairs={{0,4},{2,6},{4,0},{6,2},{8,12},{10,14},{12,8},{14,10},{16,20},{18,... | collective-permute-start | bytes 786440 | tf_op jit(solution)/shard_map/ppermute | solution.py:26
  172.5 123.0 %collective-permute-start.22 = (bf16[128,1024]{1,0:T(8,128)(2,1)}, bf16[128,1024]{1,0:T(8,128)(2,1)}, u32[]{:S(2)}, u32[]{:S(2)}) collective-permute-start(bf16[128,1024]{1,0:T(8,128)(2,1)} %collective-permute-done.21.refs_6_), channel_id=1, source_target_pairs={{0,4},{2,6},{4,0},{6,2},{8,12},{10,14},{12,8},{14,10},{16,20},{18,... | collective-permute-start | bytes 786440 | tf_op jit(solution)/shard_map/ppermute | solution.py:26
  362.6 19.7 %collective-permute-start.13 = (bf16[1,1024,1024]{2,1,0:T(8,128)(2,1)}, bf16[1,1024,1024]{2,1,0:T(8,128)(2,1)S(1)}, u32[]{:S(2)}, u32[]{:S(2)}) collective-permute-start(bf16[1,1024,1024]{2,1,0:T(8,128)(2,1)} %constant_dynamic-update-slice_fusion.5), channel_id=1, source_target_pairs={{0,2},{2,0},{4,6},{6,4},{8,10},{10,8},{12,14},{14,12},{16,18},{18,... | collective-permute-start | bytes 6291464 | tf_op jit(solution)/shard_map/ppermute | solution.py:26
  393.4 155.5 %collective-permute-start.45 = (bf16[4,128,1024]{2,1,0:T(8,128)(2,1)}, bf16[4,128,1024]{2,1,0:T(8,128)(2,1)}, u32[]{:S(2)}, u32[]{:S(2)}) collective-permute-start(bf16[4,128,1024]{2,1,0:T(8,128)(2,1)} %dynamic-slice_bitcast_fusion), channel_id=1, source_target_pairs={{0,4},{2,6},{4,0},{6,2},{8,12},{10,14},{12,8},{14,10},{16,20},{18,... | collective-permute-start | bytes 3145736 | tf_op jit(solution)/shard_map/ppermute | solution.py:26
  490.1 60.9 %collective-permute-start.34 = (bf16[4,128,768]{2,1,0:T(8,128)(2,1)}, bf16[4,128,768]{2,1,0:T(8,128)(2,1)}, u32[]{:S(2)}, u32[]{:S(2)}) collective-permute-start(bf16[4,128,768]{2,1,0:T(8,128)(2,1)} %bitcast.29), channel_id=1, source_target_pairs={{0,4},{2,6},{4,0},{6,2},{8,12},{10,14},{12,8},{14,10},{16,20},{18,... | collective-permute-start | bytes 2359304 | tf_op jit(solution)/shard_map/ppermute | solution.py:26
  525.5 29.4 %collective-permute-start.38 = (bf16[4,128,1024]{2,1,0:T(8,128)(2,1)}, bf16[4,128,1024]{2,1,0:T(8,128)(2,1)}, u32[]{:S(2)}, u32[]{:S(2)}) collective-permute-start(bf16[4,128,1024]{2,1,0:T(8,128)(2,1)} %dynamic-slice_bitcast_fusion.1), channel_id=1, source_target_pairs={{0,4},{2,6},{4,0},{6,2},{8,12},{10,14},{12,8},{14,10},{16,20},{18,... | collective-permute-start | bytes 3145736 | tf_op jit(solution)/shard_map/ppermute | solution.py:26
  536.3 87.9 %collective-permute-start.30 = (bf16[1,1024,1024]{2,1,0:T(8,128)(2,1)}, bf16[1,1024,1024]{2,1,0:T(8,128)(2,1)}, u32[]{:S(2)}, u32[]{:S(2)}) collective-permute-start(bf16[1,1024,1024]{2,1,0:T(8,128)(2,1)} %fusion.20), channel_id=1, source_target_pairs={{0,2},{2,0},{4,6},{6,4},{8,10},{10,8},{12,14},{14,12},{16,18},{18,... | collective-permute-start | bytes 6291464 | tf_op jit(solution)/shard_map/ppermute | solution.py:26
  543.2 74.7 %collective-permute-start.32 = (bf16[1,1024,1024]{2,1,0:T(8,128)(2,1)}, bf16[1,1024,1024]{2,1,0:T(8,128)(2,1)}, u32[]{:S(2)}, u32[]{:S(2)}) collective-permute-start(bf16[1,1024,1024]{2,1,0:T(8,128)(2,1)} %fusion.21), channel_id=1, source_target_pairs={{0,2},{2,0},{4,6},{6,4},{8,10},{10,8},{12,14},{14,12},{16,18},{18,... | collective-permute-start | bytes 6291464 | tf_op jit(solution)/shard_map/ppermute | solution.py:26
  552.6 17.1 %collective-permute-start.36 = (bf16[128,768]{1,0:T(8,128)(2,1)S(1)}, bf16[128,768]{1,0:T(8,128)(2,1)S(1)}, u32[]{:S(2)}, u32[]{:S(2)}) collective-permute-start(bf16[128,768]{1,0:T(8,128)(2,1)S(1)} %get-tuple-element.43), channel_id=1, source_target_pairs={{0,16},{2,18},{4,20},{6,22},{8,24},{10,26},{12,28},{14,30},{16,0},... | collective-permute-start | bytes 589832 | tf_op jit(solution)/shard_map/ppermute | solution.py:26
  569.8 23.0 %collective-permute-start.40 = (bf16[128,1024]{1,0:T(8,128)(2,1)S(1)}, bf16[128,1024]{1,0:T(8,128)(2,1)S(1)}, u32[]{:S(2)}, u32[]{:S(2)}) collective-permute-start(bf16[128,1024]{1,0:T(8,128)(2,1)S(1)} %get-tuple-element.37), channel_id=1, source_target_pairs={{0,16},{2,18},{4,20},{6,22},{8,24},{10,26},{12,28},{14,30},{16,0},... | collective-permute-start | bytes 786440 | tf_op jit(solution)/shard_map/ppermute | solution.py:26
  570.5 22.2 %collective-permute-start.41 = (bf16[128,1024]{1,0:T(8,128)(2,1)S(1)}, bf16[128,1024]{1,0:T(8,128)(2,1)S(1)}, u32[]{:S(2)}, u32[]{:S(2)}) collective-permute-start(bf16[128,1024]{1,0:T(8,128)(2,1)S(1)} %get-tuple-element.36), channel_id=1, source_target_pairs={{0,24},{2,26},{4,28},{6,30},{8,16},{10,18},{12,20},{14,22},{16,8},... | collective-permute-start | bytes 786440 | tf_op jit(solution)/shard_map/ppermute | solution.py:26
  578.2 18.8 %collective-permute-start.46 = (bf16[128,1024]{1,0:T(8,128)(2,1)S(1)}, bf16[128,1024]{1,0:T(8,128)(2,1)S(1)}, u32[]{:S(2)}, u32[]{:S(2)}) collective-permute-start(bf16[128,1024]{1,0:T(8,128)(2,1)S(1)} %get-tuple-element.32), channel_id=1, source_target_pairs={{0,8},{2,10},{4,12},{6,14},{8,0},{10,2},{12,4},{14,6},{16,24},{18,... | collective-permute-start | bytes 786440 | tf_op jit(solution)/shard_map/ppermute | solution.py:26
  592.7 24.2 %collective-permute-start.47 = (bf16[128,1024]{1,0:T(8,128)(2,1)S(1)}, bf16[128,1024]{1,0:T(8,128)(2,1)S(1)}, u32[]{:S(2)}, u32[]{:S(2)}) collective-permute-start(bf16[128,1024]{1,0:T(8,128)(2,1)S(1)} %get-tuple-element.34), channel_id=1, source_target_pairs={{0,16},{2,18},{4,20},{6,22},{8,24},{10,26},{12,28},{14,30},{16,0},... | collective-permute-start | bytes 786440 | tf_op jit(solution)/shard_map/ppermute | solution.py:26
  592.7 24.2 %collective-permute-start.48 = (bf16[128,1024]{1,0:T(8,128)(2,1)S(1)}, bf16[128,1024]{1,0:T(8,128)(2,1)S(1)}, u32[]{:S(2)}, u32[]{:S(2)}) collective-permute-start(bf16[128,1024]{1,0:T(8,128)(2,1)S(1)} %get-tuple-element.33), channel_id=1, source_target_pairs={{0,24},{2,26},{4,28},{6,30},{8,16},{10,18},{12,20},{14,22},{16,8},... | collective-permute-start | bytes 786440 | tf_op jit(solution)/shard_map/ppermute | solution.py:26
  597.0 20.9 %collective-permute-start.42 = (bf16[1,32,1792]{2,1,0:T(8,128)(2,1)S(1)}, bf16[1,32,1792]{2,1,0:T(8,128)(2,1)S(1)}, u32[]{:S(2)}, u32[]{:S(2)}) collective-permute-start(bf16[1,32,1792]{2,1,0:T(8,128)(2,1)S(1)} %get-tuple-element.46), channel_id=1, source_target_pairs={{0,1},{1,0},{2,3},{3,2},{4,5},{5,4},{6,7},{7,6},{8,9},{9,8},{10,11... | collective-permute-start | bytes 344072 | tf_op jit(solution)/shard_map/ppermute | solution.py:37
  622.1 37.3 %collective-permute-start.33 = (bf16[1,512,1024]{2,1,0:T(8,128)(2,1)}, bf16[1,512,1024]{2,1,0:T(8,128)(2,1)S(1)}, u32[]{:S(2)}, u32[]{:S(2)}) collective-permute-start(bf16[1,512,1024]{2,1,0:T(8,128)(2,1)} %dynamic-slice_convert_fusion), channel_id=1, source_target_pairs={{0,1},{1,0},{2,3},{3,2},{4,5},{5,4},{6,7},{7,6},{8,9},{9,8},{10,11... | collective-permute-start | bytes 3145736 | tf_op jit(solution)/shard_map/ppermute | solution.py:31
  629.2 61.0 %collective-permute-start.31 = (bf16[1,512,1024]{2,1,0:T(8,128)(2,1)}, bf16[1,512,1024]{2,1,0:T(8,128)(2,1)}, u32[]{:S(2)}, u32[]{:S(2)}) collective-permute-start(bf16[1,512,1024]{2,1,0:T(8,128)(2,1)} %dynamic-slice_convert_fusion.1), channel_id=1, source_target_pairs={{0,1},{1,0},{2,3},{3,2},{4,5},{5,4},{6,7},{7,6},{8,9},{9,8},{10,11... | collective-permute-start | bytes 3145736 | tf_op jit(solution)/shard_map/ppermute | solution.py:31
  (79 other events, 1298.8 us)
Sparse Core Ops, SparseCore 0:
  19.5 54.9 all-gather.2
  549.0 140.8 reduce-scatter.1

commit v2 on v1

v2 whole, which is shorter than its diff:
```python
import functools

import jax
import jax.numpy as jnp
from jax import lax
from jax.experimental import pallas as pl
from jax.experimental.pallas import tpu as pltpu
from jax.sharding import PartitionSpec as P

HD = 64
ROT = 16
EPS = 1e-05
SCALE = 0.125
F32 = jnp.float32
BF = jnp.bfloat16


def dot(left, right, left_dim, right_dim):
    return lax.dot_general(
        left, right, (((left_dim,), (right_dim,)), ((), ())), preferred_element_type=F32
    )


def swap_batch(value, mask):
    count = lax.axis_size("batch")
    return lax.ppermute(value, "batch", [(i, i ^ mask) for i in range(count)])


def swap_seq(value, mask):
    count = lax.axis_size("seq")
    return lax.ppermute(value, "seq", [(i, i ^ mask) for i in range(count)])


def swap_member(value, mask):
    members = 2 * lax.axis_size("seq")
    count = lax.axis_size("batch") * lax.axis_size("seq")
    return lax.ppermute(
        value,
        ("batch", "seq"),
        [(i, (i // members) * members + ((i % members) ^ mask)) for i in range(count)],
    )


def after(value, *others):
    return lax.optimization_barrier((value,) + others)[0]


def gather_groups(chunk):
    groups = lax.axis_size("batch") // 2
    far = [chunk] + [swap_batch(chunk, 4 * k) for k in range(1, groups // 2)]
    near = [swap_batch(part, 2) for part in far]
    return [part for pair in zip(far, near) for part in pair]


def sort_groups(value):
    groups = value.shape[0]
    me = lax.axis_index("batch") // 2
    bit = 1
    while bit < groups:
        paired = value.reshape((groups // (2 * bit), 2, bit) + value.shape[1:])
        flipped = jnp.concatenate([paired[:, 1:], paired[:, :1]], 1)
        value = jnp.where((me & bit) > 0, flipped, paired).reshape(value.shape)
        bit = 2 * bit
    return value


def reduce_groups(send, keep):
    got = swap_batch(send, 2)
    total = keep[0].astype(F32) + got[0].astype(F32)
    pieces = [
        (keep[k].astype(F32) + got[k].astype(F32)).astype(send.dtype) for k in range(1, send.shape[0])
    ]
    for k, piece in enumerate(pieces):
        total = total + swap_batch(piece, 4 * (k + 1)).astype(F32)
    return total


def member():
    return (lax.axis_index("batch") % 2) * lax.axis_size("seq") + lax.axis_index("seq")


def exchange_members(pieces):
    me = member()
    out = jnp.zeros_like(pieces)
    for k in range(pieces.shape[0]):
        piece = lax.dynamic_index_in_dim(pieces, me ^ k, 0, keepdims=True)
        got = piece if k == 0 else swap_member(piece, k)
        out = lax.dynamic_update_slice_in_dim(out, got, me ^ k, 0)
    return out


def gather_merger(weight):
    seq = lax.axis_size("seq")
    batch = lax.axis_size("batch")
    members = 2 * seq
    groups = batch // 2
    lows = groups // members
    share = weight.shape[0]
    every = ("batch", "seq")
    group = lax.axis_index("batch") // 2
    root = group // lows
    me = member()
    block = jnp.zeros((members,) + weight.shape, weight.dtype)
    block = lax.dynamic_update_slice_in_dim(block, weight[None], me, 0)
    for k in range(1, members):
        pairs = [
            (g * members + t, g * members + (t ^ k))
            for g in range(groups)
            for t in range(members)
            if t ^ k == g // lows
        ]
        block = lax.dynamic_update_slice_in_dim(block, lax.ppermute(weight, every, pairs)[None], me ^ k, 0)
    block = block.reshape(members * share, -1)
    found = jnp.where(me == root, block, jnp.zeros_like(block))
    for k in range(1, members):
        pairs = [
            (g * members + g // lows, (g ^ (k * lows)) * members + g // lows) for g in range(groups)
        ]
        found = found + lax.ppermute(block, every, pairs)
    whole = found[None]
    bit = 1
    while bit < lows:
        got = swap_batch(whole, 2 * bit)
        swapped = (group & bit) > 0
        whole = jnp.where(swapped, jnp.concatenate([got, whole]), jnp.concatenate([whole, got]))
        bit = 2 * bit
    return whole.reshape(-1, weight.shape[1])


def reduce_merger(grad):
    seq = lax.axis_size("seq")
    batch = lax.axis_size("batch")
    members = 2 * seq
    groups = batch // 2
    lows = groups // members
    every = ("batch", "seq")
    group = lax.axis_index("batch") // 2
    root = group // lows
    me = member()
    whole = grad.reshape((lows, -1, grad.shape[1]))
    bit = lows // 2
    while bit:
        halves = whole.reshape((2, -1) + whole.shape[1:])
        side = ((group & bit) > 0).astype(jnp.int32)
        away = lax.dynamic_index_in_dim(halves, 1 - side, 0, keepdims=False).astype(BF)
        whole = lax.dynamic_index_in_dim(halves, side, 0, keepdims=False)
        whole = whole + swap_batch(away, 2 * bit).astype(F32)
        bit = bit // 2
    block = whole[0].astype(BF)
    total = whole[0]
    for k in range(1, members):
        pairs = [
            ((g ^ (k * lows)) * members + g // lows, g * members + g // lows) for g in range(groups)
        ]
        total = total + lax.ppermute(block, every, pairs).astype(F32)
    rows = total.reshape(members, -1, grad.shape[1]).astype(BF)
    mine = lax.dynamic_index_in_dim(rows, me, 0, keepdims=False).astype(F32)
    out = jnp.where(me == root, mine, jnp.zeros_like(mine))
    for k in range(1, members):
        pairs = [
            (g * members + g // lows, g * members + ((g // lows) ^ k)) for g in range(groups)
        ]
        piece = lax.dynamic_index_in_dim(rows, me ^ k, 0, keepdims=False)
        out = out + lax.ppermute(piece, every, pairs).astype(F32)
    return out


def join_tokens(value):
    if lax.axis_size("seq") == 2:
        far = swap_seq(value, 1)
        return jnp.concatenate(
            [
                jnp.concatenate([value, far], 1),
                jnp.concatenate([swap_batch(value, 1), swap_batch(far, 1)], 1),
            ],
            0,
        )
    whole = lax.all_gather(value, "seq", axis=1, tiled=True)
    return jnp.concatenate([whole, swap_batch(whole, 1)], 0)


def part_tokens(value):
    seqs, length, _ = value.shape
    seqs = seqs // 2
    mine = value[:seqs].astype(F32) + swap_batch(value[seqs:], 1).astype(F32)
    if lax.axis_size("seq") == 2:
        stretch = length // 2
        return mine[:, :stretch] + swap_seq(mine[:, stretch:].astype(BF), 1).astype(F32)
    return lax.psum_scatter(mine.astype(BF), "seq", scatter_dimension=1, tiled=True).astype(F32)


def centre(rows):
    mean = jnp.mean(rows, -1, keepdims=True)
    centered = rows - mean
    spread = jnp.mean(centered * centered, -1, keepdims=True)
    rstd = lax.rsqrt(spread + EPS)
    return centered * rstd, rstd


def lay(parts, out_ref, group, rows):
    for k, part in enumerate(parts):
        out_ref[pl.ds(pl.multiple_of((group ^ k) * rows, rows), rows), :] = part[:rows, :]


def split_out(total_ref, send_ref, keep_ref, group, rows):
    for k in range(send_ref.shape[0]):
        keep = pl.multiple_of((group ^ (2 * k)) * rows, rows)
        send = pl.multiple_of((group ^ (2 * k + 1)) * rows, rows)
        keep_ref[k] = total_ref[pl.ds(keep, rows), :].astype(BF)
        send_ref[k] = total_ref[pl.ds(send, rows), :].astype(BF)


def add_rows(out_ref, i, row, value):
    total = jnp.sum(value, 0, keepdims=True)

    @pl.when(i == 0)
    def _():
        out_ref[row : row + 1, :] = total

    @pl.when(i > 0)
    def _():
        out_ref[row : row + 1, :] += total


def add_to(total_ref, i, value):
    @pl.when(i == 0)
    def _():
        total_ref[...] = value

    @pl.when(i > 0)
    def _():
        total_ref[...] += value


def feed_kernel(groups, info, x_ref, g_ref, gain_ref, shift_ref, bias_ref, *refs):
    widen_parts, narrow_parts = refs[:groups], refs[groups : 2 * groups]
    out_ref, e_ref, sums_ref, bsum_ref, ns_ref, nk_ref, ws_ref, wk_ref = refs[2 * groups : 2 * groups + 8]
    widen, narrow, narrow_total, widen_total = refs[2 * groups + 8 :]
    i = pl.program_id(0)
    group = info[0]
    wide_rows = widen.shape[0] // groups
    unit = narrow.shape[0] // groups

    @pl.when(i == 0)
    def _():
        lay(widen_parts, widen, group, wide_rows)
        lay(narrow_parts, narrow, group, unit)

    normed, _ = centre(x_ref[...].astype(F32))
    second = (normed * gain_ref[...] + shift_ref[...]).astype(BF)
    upstream = g_ref[...]
    widened = dot(second, widen[...], 1, 0) + bias_ref[...]
    bell = 0.5 + 0.5 * lax.erf(widened * (0.5**0.5))
    active = (widened * bell).astype(BF)
    slope = bell + widened * jnp.exp(-0.5 * widened * widened) * (0.15915494309189535**0.5)
    add_to(narrow_total, i, dot(active, upstream, 0, 0))
    out_ref[...] = dot(active, narrow[...], 1, 0).astype(BF)
    widened_grad_f = dot(upstream, narrow[...], 1, 1) * slope
    widened_grad = widened_grad_f.astype(BF)
    add_rows(bsum_ref, i, 0, widened_grad.astype(F32))
    add_to(widen_total, i, dot(second, widened_grad, 0, 0))
    second_grad = dot(widened_grad, widen[...], 1, 1)
    add_rows(sums_ref, i, 0, second_grad * normed)
    add_rows(sums_ref, i, 1, second_grad)
    e_ref[...] = (second_grad * gain_ref[...]).astype(BF)

    @pl.when(i == pl.num_programs(0) - 1)
    def _():
        split_out(narrow_total, ns_ref, nk_ref, group, unit)
        split_out(widen_total, ws_ref, wk_ref, group, wide_rows)


def whole(shape):
    return pl.BlockSpec(shape, lambda *_: (0,) * len(shape), pipeline_mode=pl.Buffered(1))


def feed(info, inputs, upstream, gain, shift, bias, widen_parts, narrow_parts):
    rows, width = inputs.shape
    groups = len(widen_parts)
    unit = narrow_parts[0].shape[0]
    hidden = groups * unit
    block = min(512, rows)
    share = width // groups
    tile = pl.BlockSpec((block, width), lambda i, _: (i, 0))
    half = groups // 2
    shapes = [(half, unit, width), (half, unit, width), (half, share, hidden), (half, share, hidden)]
    return pl.pallas_call(
        functools.partial(feed_kernel, groups),
        grid_spec=pltpu.PrefetchScalarGridSpec(
            num_scalar_prefetch=1,
            grid=(rows // block,),
            in_specs=[tile, tile, whole((1, width)), whole((1, width)), whole((1, hidden))]
            + [whole(part.shape) for part in widen_parts]
            + [whole(part.shape) for part in narrow_parts],
            out_specs=[tile, tile, whole((2, width)), whole((1, hidden))] + [whole(s) for s in shapes],
            scratch_shapes=[
                pltpu.VMEM((width, hidden), BF),
                pltpu.VMEM((hidden, width), BF),
                pltpu.VMEM((hidden, width), F32),
                pltpu.VMEM((width, hidden), F32),
            ],
        ),
        out_shape=[
            jax.ShapeDtypeStruct((rows, width), BF),
            jax.ShapeDtypeStruct((rows, width), BF),
            jax.ShapeDtypeStruct((2, width), F32),
            jax.ShapeDtypeStruct((1, hidden), F32),
        ]
        + [jax.ShapeDtypeStruct(s, BF) for s in shapes],
        cost_estimate=pl.CostEstimate(
            flops=12 * rows * width * hidden, bytes_accessed=8 * rows * width, transcendentals=2 * rows * hidden
        ),
        compiler_params=pltpu.CompilerParams(vmem_limit_bytes=60 * 1024 * 1024),
    )(info, inputs, upstream, gain, shift, bias, *widen_parts, *narrow_parts)


def project_kernel(groups, info, x_ref, g_ref, gain_ref, shift_ref, bias_ref, merger_ref, *refs):
    parts = refs[:groups]
    first_ref, project_ref, mg_ref, mixer = refs[groups:]

    @pl.when(pl.program_id(0) == 0)
    def _():
        lay(parts, mixer, info[0], mixer.shape[0] // groups)

    normed, _ = centre(x_ref[...].astype(F32))
    first = (normed * gain_ref[...] + shift_ref[...]).astype(BF)
    first_ref[...] = first
    project_ref[...] = dot(first, mixer[...], 1, 0) + bias_ref[...]
    mg_ref[...] = dot(g_ref[...], merger_ref[...], 1, 1).astype(BF)


def project_all(info, inputs, upstream, gain, shift, bias, merger, parts):
    rows, width = inputs.shape
    groups = len(parts)
    wide = parts[0].shape[1]
    slim = wide // 3
    block = min(512, rows)

    def tile(n):
        return pl.BlockSpec((block, n), lambda i, _: (i, 0))

    return pl.pallas_call(
        functools.partial(project_kernel, groups),
        grid_spec=pltpu.PrefetchScalarGridSpec(
            num_scalar_prefetch=1,
            grid=(rows // block,),
            in_specs=[tile(width), tile(width), whole((1, width)), whole((1, width)), whole((1, wide)), whole(merger.shape)]
            + [whole(part.shape) for part in parts],
            out_specs=[tile(width), tile(wide), tile(slim)],
            scratch_shapes=[pltpu.VMEM((width, wide), BF)],
        ),
        out_shape=[
            jax.ShapeDtypeStruct((rows, width), BF),
            jax.ShapeDtypeStruct((rows, wide), F32),
            jax.ShapeDtypeStruct((rows, slim), BF),
        ],
        cost_estimate=pl.CostEstimate(
            flops=2 * rows * width * (wide + slim), bytes_accessed=10 * rows * width, transcendentals=0
        ),
        compiler_params=pltpu.CompilerParams(vmem_limit_bytes=56 * 1024 * 1024),
    )(info, inputs, upstream, gain, shift, bias, merger, *parts)


def merge_kernel(m_ref, g_ref, f_ref, w_ref, out_ref, grad_ref):
    mixed = m_ref[...]
    out_ref[...] = (dot(mixed, w_ref[...], 1, 0) + f_ref[...].astype(F32)).astype(BF)
    add_to(grad_ref, pl.program_id(0), dot(mixed, g_ref[...], 0, 0))


def merge(mixed, upstream, partial, merger):
    rows, slim = mixed.shape
    width = upstream.shape[1]
    block = min(512, rows)

    def tile(n):
        return pl.BlockSpec((block, n), lambda i: (i, 0))

    return pl.pallas_call(
        merge_kernel,
        grid=(rows // block,),
        in_specs=[tile(slim), tile(width), tile(width), whole(merger.shape)],
        out_specs=[tile(width), whole((slim, width))],
        out_shape=[jax.ShapeDtypeStruct((rows, width), BF), jax.ShapeDtypeStruct((slim, width), F32)],
        cost_estimate=pl.CostEstimate(
            flops=4 * rows * width * slim, bytes_accessed=6 * rows * width, transcendentals=0
        ),
        compiler_params=pltpu.CompilerParams(vmem_limit_bytes=40 * 1024 * 1024),
    )(mixed, upstream, partial, merger)


def mixer_kernel(groups, info, x_ref, first_ref, e_ref, p_ref, gain_ref, *refs):
    parts = refs[:groups]
    out_ref, sums_ref, bsum_ref, s_ref, k_ref, mixer, total = refs[groups:]
    i = pl.program_id(0)
    group = info[0]
    share = mixer.shape[0] // groups

    @pl.when(i == 0)
    def _():
        lay(parts, mixer, group, share)

    grad = jnp.concatenate([p_ref[0], p_ref[1], p_ref[2]], 1)
    add_to(total, i, dot(first_ref[...], grad, 0, 0))
    first_grad = dot(grad, mixer[...], 1, 1)
    normed, _ = centre(x_ref[...].astype(F32))
    out_ref[...] = (first_grad * gain_ref[...] + e_ref[...].astype(F32)).astype(BF)
    add_rows(sums_ref, i, 0, first_grad * normed)
    add_rows(sums_ref, i, 1, first_grad)
    add_rows(bsum_ref, i, 0, grad.astype(F32))

    @pl.when(i == pl.num_programs(0) - 1)
    def _():
        split_out(total, s_ref, k_ref, group, share)


def mixer_back(info, inputs, first, error, grads, gain, parts):
    rows, width = inputs.shape
    groups = len(parts)
    wide = parts[0].shape[1]
    slim = wide // 3
    block = min(512, rows)
    shape = (groups // 2, width // groups, wide)
    tile = pl.BlockSpec((block, width), lambda i, _: (i, 0))
    return pl.pallas_call(
        functools.partial(mixer_kernel, groups),
        grid_spec=pltpu.PrefetchScalarGridSpec(
            num_scalar_prefetch=1,
            grid=(rows // block,),
            in_specs=[tile, tile, tile, pl.BlockSpec((3, block, slim), lambda i, _: (0, i, 0)), whole((1, width))]
            + [whole(part.shape) for part in parts],
            out_specs=[tile, whole((2, width)), whole((1, wide)), whole(shape), whole(shape)],
            scratch_shapes=[pltpu.VMEM((width, wide), BF), pltpu.VMEM((width, wide), F32)],
        ),
        out_shape=[
            jax.ShapeDtypeStruct((rows, width), BF),
            jax.ShapeDtypeStruct((2, width), F32),
            jax.ShapeDtypeStruct((1, wide), F32),
            jax.ShapeDtypeStruct(shape, BF),
            jax.ShapeDtypeStruct(shape, BF),
        ],
        cost_estimate=pl.CostEstimate(
            flops=4 * rows * width * wide, bytes_accessed=10 * rows * width, transcendentals=0
        ),
        compiler_params=pltpu.CompilerParams(vmem_limit_bytes=56 * 1024 * 1024),
    )(info, inputs, first, error, grads, gain, *parts)


def attend_kernel(heads, block, info, q_ref, k_ref, v_ref, g_ref, c_ref, s_ref, col_ref, row_ref, mixed_ref, grad_ref):
    length = q_ref.shape[0]
    half = ROT // 2
    cosine, sine = c_ref[0], s_ref[0]
    middle = length // 2
    low = pl.ds(pl.multiple_of(info[1] * middle, middle), middle)
    high = pl.ds(pl.multiple_of((1 - info[1]) * middle, middle), middle)

    def take(ref):
        return jnp.concatenate([ref[low, :], ref[high, :]], 0)

    def put(ref, value):
        ref[low, :] = value[:middle]
        ref[high, :] = value[middle:]

    def put_grad(part, value):
        grad_ref[part, low, :] = value[:middle]
        grad_ref[part, high, :] = value[middle:]

    lane = lax.broadcasted_iota(jnp.int32, cosine.shape, 1) % HD
    leading = lane < half

    def roll(value, shift):
        if value.shape[1] % 128:
            return jnp.concatenate([value[:, -shift:], value[:, :-shift]], 1)
        return pltpu.roll(value, shift % value.shape[1], 1)

    def turn(value):
        return value * cosine + jnp.where(leading, -roll(value, -half), roll(value, half)) * sine

    def turn_back(value):
        return value * cosine + jnp.where(leading, roll(value, -half), -roll(value, half)) * sine

    query = (turn(take(q_ref)).astype(BF).astype(F32) * SCALE).astype(BF)
    keys = turn(take(k_ref)).astype(BF)
    values = take(v_ref).astype(BF)
    grads = take(g_ref)
    col = col_ref[0]
    row = row_ref[0]
    dq_all, dk_all, dv_all, mixed_all = [], [], [], []
    for h in range(heads):
        span = slice(h * HD, (h + 1) * HD)
        qh, kh, vh, gh = query[:, span], keys[:, span], values[:, span], grads[:, span]
        dq_parts, mixed_parts = [], []
        dk = jnp.zeros((length, HD), F32)
        dv = jnp.zeros((length, HD), F32)
        for i in range(length // block):
            n = (i + 1) * block
            rows = slice(i * block, n)
            q, g = qh[rows], gh[rows]
            k, v = kh[:n], vh[:n]
            scores = dot(q, k, 1, 1)
            place_q = lax.broadcasted_iota(jnp.int32, (block, n), 0) + i * block
            place_k = lax.broadcasted_iota(jnp.int32, (block, n), 1)
            allowed = (col[rows] == row[:, :n]) & (place_q >= place_k)
            scores = jnp.where(allowed, scores, -1e30)
            expo = jnp.exp(scores - jnp.max(scores, -1, keepdims=True))
            prob = expo * (1.0 / jnp.sum(expo, -1, keepdims=True))
            prob_b = prob.astype(BF)
            mixed_parts.append(dot(prob_b, v, 1, 0))
            prob_grad = dot(g, v, 1, 1)
            center = jnp.sum(prob * prob_grad, -1, keepdims=True)
            score_grad = (prob * (prob_grad - center)).astype(BF)
            dq_parts.append(dot(score_grad, k, 1, 0) * SCALE)
            dk_add = dot(score_grad, q, 0, 0)
            dv_add = dot(prob_b, g, 0, 0)
            if n < length:
                zeros = jnp.zeros((length - n, HD), F32)
                dk_add = jnp.concatenate([dk_add, zeros], 0)
                dv_add = jnp.concatenate([dv_add, zeros], 0)
            dk = dk + dk_add
            dv = dv + dv_add
        dq_all.append(jnp.concatenate(dq_parts, 0))
        mixed_all.append(jnp.concatenate(mixed_parts, 0))
        dk_all.append(dk)
        dv_all.append(dv)
    put(mixed_ref, jnp.concatenate(mixed_all, 1).astype(BF))
    put_grad(0, turn_back(jnp.concatenate(dq_all, 1)).astype(BF))
    put_grad(1, turn_back(jnp.concatenate(dk_all, 1)).astype(BF))
    put_grad(2, jnp.concatenate(dv_all, 1).astype(BF))


def attend(info, project, mixed_grad, tables, segs):
    seqs, length = segs.shape
    rows, wide = project.shape
    width = wide // 3
    heads = min(2, width // HD)
    lanes = heads * HD
    steps = width // lanes
    block = min(256, length)

    parts = (project, project, project)
    ahead = steps
    if lanes % 128:
        parts = tuple(jnp.split(project, 3, 1))
        ahead = 0

    def of(part):
        return pl.BlockSpec((length, lanes), lambda s, h, _: (s, part * ahead + h))

    table = pl.BlockSpec((1, length, lanes), lambda s, h, _: (s, 0, 0))
    cost = pl.CostEstimate(
        flops=seqs * (width // HD) * length * length * HD * 12,
        bytes_accessed=rows * width * 24,
        transcendentals=seqs * (width // HD) * length * length,
    )
    return pl.pallas_call(
        functools.partial(attend_kernel, heads, block),
        grid_spec=pltpu.PrefetchScalarGridSpec(
            num_scalar_prefetch=1,
            grid=(seqs, steps),
            in_specs=[
                of(0),
                of(1),
                of(2),
                of(0),
                table,
                table,
                pl.BlockSpec((1, length, 1), lambda s, h, _: (s, 0, 0)),
                pl.BlockSpec((1, 1, length), lambda s, h, _: (s, 0, 0)),
            ],
            out_specs=[
                pl.BlockSpec((length, lanes), lambda s, h, _: (s, h)),
                pl.BlockSpec((3, length, lanes), lambda s, h, _: (0, s, h)),
            ],
        ),
        out_shape=[
            jax.ShapeDtypeStruct((rows, width), BF),
            jax.ShapeDtypeStruct((3, rows, width), BF),
        ],
        cost_estimate=cost,
        compiler_params=pltpu.CompilerParams(vmem_limit_bytes=56 * 1024 * 1024),
    )(info, *parts, mixed_grad, *tables, segs[:, :, None], segs[:, None, :])


def turn_tables(position, lanes):
    half = ROT // 2
    lane = jnp.arange(lanes) % HD
    freq = 10000.0 ** (-((lane % half).astype(F32) * 2.0) / float(ROT))
    freq = jnp.where(lane < ROT, freq, 0.0)
    phase = position.astype(F32)[..., None] * freq
    return jnp.cos(phase), jnp.sin(phase)


def local(
    tokens,
    segments,
    cotangent,
    mixer_gain,
    mixer_shift,
    mixer_weight,
    mixer_bias,
    merger_weight,
    merger_bias,
    feeder_gain,
    feeder_shift,
    widen_weight,
    widen_bias,
    narrow_weight,
    narrow_bias,
):
    seqs, stretch, width = tokens.shape
    seq = lax.axis_size("seq")
    groups = lax.axis_size("batch") // 2
    members = 2 * seq
    devices = groups * members
    length = stretch * seq
    here = lax.axis_index("seq")
    me = member()
    group = lax.axis_index("batch") // 2
    share = mixer_weight.shape[0]
    hidden = widen_weight.shape[1]
    slim = width // members
    unit = hidden // devices
    mine_h = groups * unit
    block = members * share
    turned = here if seq == 2 else jnp.zeros_like(here)
    info = jnp.stack([group, turned]).astype(jnp.int32)

    vectors = (mixer_gain, mixer_shift, mixer_bias, merger_bias, feeder_gain, feeder_shift, widen_bias, narrow_bias)
    sizes = [v.shape[0] for v in vectors]
    cuts = [sum(sizes[: i + 1]) for i in range(len(sizes) - 1)]
    packed = jnp.pad(jnp.concatenate(vectors), (0, mine_h - sum(sizes)))
    narrow_parts = gather_groups(narrow_weight)
    mixer_pieces = mixer_weight.reshape(share, 3, members, slim).transpose(2, 0, 1, 3)
    widen_pieces = widen_weight.reshape(share, groups, members, unit).transpose(2, 0, 1, 3)
    widen_pieces = jnp.concatenate(
        [
            widen_pieces.reshape(members, share, mine_h),
            jnp.broadcast_to(packed, (members, 1, mine_h)),
        ],
        1,
    )
    widen_got = exchange_members(widen_pieces)
    pad = (-members) % 16
    widen_chunk = jnp.concatenate(
        [widen_got[:, :share].reshape(block, mine_h), jnp.pad(widen_got[:, share], ((0, pad), (0, 0)))], 0
    )
    widen_parts = gather_groups(widen_chunk)
    mixer_chunk = exchange_members(mixer_pieces.reshape(members, share, 3 * slim)).reshape(block, -1)
    mixer_parts = gather_groups(after(mixer_chunk, widen_parts[-2]))
    merger = gather_merger(after(merger_weight, widen_parts[-2]))
    gathered = sort_groups(jnp.stack([p[block : block + members, : sum(sizes)] for p in widen_parts]))
    gathered = gathered.reshape(devices, -1).astype(F32)
    gain_m, shift_m, bias_m, bias_o, gain_f, shift_f, bias_w, bias_n = [
        v.reshape(1, -1) for v in jnp.split(gathered, cuts, 1)
    ]
    bias_m_mine = lax.dynamic_index_in_dim(bias_m.reshape(3, members, slim), me, 1).reshape(1, -1)
    bias_w_mine = lax.dynamic_index_in_dim(bias_w.reshape(groups, members, unit), me, 1).reshape(1, -1)

    inputs = join_tokens(tokens).reshape(-1, width)
    upstream = join_tokens(cotangent).reshape(-1, width)
    segs = join_tokens(segments)
    if seq == 2:
        flipped = jnp.concatenate([segs[:, stretch:], segs[:, :stretch]], 1)
        segs = jnp.where(here == 0, segs, flipped)
    place = jnp.arange(length, dtype=jnp.int32)
    earlier = jnp.sum((segs[:, None, :] < segs[:, :, None]).astype(jnp.int32), -1)
    tables = turn_tables(place[None, :] - earlier, min(2, slim // HD) * HD)

    partial, error, feed_sums, widen_bias_grad, n_send, n_keep, w_send, w_keep = feed(
        info, inputs, upstream, gain_f, shift_f, bias_w_mine, widen_parts, narrow_parts
    )
    narrow_out = reduce_groups(n_send, n_keep)
    widen_sum = reduce_groups(w_send, w_keep)
    widen_back = exchange_members(widen_sum.reshape(members, share, mine_h).astype(BF))
    widen_out = widen_back.reshape(members, share, groups, unit).transpose(1, 2, 0, 3).astype(F32)

    first, project, mixed_grad = project_all(
        info, inputs, after(upstream, partial), gain_m, shift_m, bias_m_mine, merger, mixer_parts
    )
    mixed, project_grad = attend(info, project, mixed_grad, tables, segs)
    partial, merger_grad = merge(mixed, upstream, partial, merger)
    merger_out = reduce_merger(merger_grad)
    own = tokens.astype(F32)
    layer_output = part_tokens(partial.reshape(2 * seqs, length, width))
    layer_output = (own + layer_output + (bias_o + bias_n)).astype(BF)
    error, mixer_sums, mixer_bias_grad, m_send, m_keep = mixer_back(
        info, inputs, first, error, project_grad, gain_m, mixer_parts
    )
    mixer_sum = reduce_groups(m_send, m_keep)
    mixer_back_rows = exchange_members(mixer_sum.reshape(members, share, 3 * slim).astype(BF))
    mixer_out = mixer_back_rows.reshape(members, share, 3, slim).transpose(1, 2, 0, 3).astype(F32)

    error = part_tokens(error.reshape(2 * seqs, length, width))
    normed, rstd = centre(own)
    back = rstd * (
        error
        - jnp.mean(error, -1, keepdims=True)
        - normed * jnp.mean(error * normed, -1, keepdims=True)
    )
    tokens_grad = (cotangent.astype(F32) + back).astype(BF)

    def spread_out(value, lead):
        shape = (lead, members, value.size // lead)
        return lax.dynamic_update_slice_in_dim(jnp.zeros(shape, F32), value.reshape(lead, 1, -1), me, 1)

    bias_grad = jnp.sum(cotangent.astype(F32), (0, 1))
    sums = (
        mixer_sums[0],
        mixer_sums[1],
        spread_out(mixer_bias_grad, 3),
        bias_grad,
        feed_sums[0],
        feed_sums[1],
        spread_out(widen_bias_grad, groups),
        bias_grad,
    )
    packed = jnp.concatenate([v.reshape(devices, -1) for v in sums], 1).reshape(groups, members, -1)
    relative = sort_groups(packed).reshape(groups // 2, 2, members, -1)
    owned = reduce_groups(relative[:, 1], relative[:, 0])
    owned = jnp.sum(exchange_members(owned), 0)
    gain_m_out, shift_m_out, bias_m_out, bias_o_out, gain_f_out, shift_f_out, bias_w_out, bias_n_out = jnp.split(owned, cuts)
    return (
        layer_output,
        tokens_grad,
        gain_m_out,
        shift_m_out,
        mixer_out.reshape(mixer_weight.shape),
        bias_m_out,
        merger_out,
        bias_o_out,
        gain_f_out,
        shift_f_out,
        widen_out.reshape(widen_weight.shape),
        bias_w_out,
        narrow_out,
        bias_n_out,
    )


def solution(mesh):
    vector = P(("batch", "seq"))
    matrix = P(("batch", "seq"), None)
    rows = P("batch", "seq", None)
    params = (vector, vector, matrix, vector, matrix, vector, vector, vector, matrix, vector, matrix, vector)
    return jax.shard_map(
        local,
        mesh=mesh,
        in_specs=(rows, P("batch", "seq"), rows) + params,
        out_specs=(rows, rows) + params,
        check_vma=False,
    )
```

time: 763 us -> 515 us (0.67)
  blocking collectives: 105 us -> 0 us
  Pallas kernels: 220 us -> 122 us
  matrix products: 91.5 us -> 0 us
  starting transfers between devices: 59.5 us -> 109 us
  waiting for transfers between devices: 139 us -> 179 us
  local copies, waits for them, and re-layouts: 77.5 us -> 54.3 us
  between operations: 15.4 us -> 2.46 us
    unnamed x2 -> x0, blocking collectives: 105 us -> none
    pallas_call x4 -> x5, Pallas kernels: 220 us -> 122 us  [the longest x1 43.8 us: feed(): pl.pallas_call(functools.partial(feed_kernel, groups), grid_spec=pltpu.Pr...]
    dot_general x16 -> x0, matrix products: 91.5 us -> none  [dot(): lax.dot_general(left, right, (((left_dim,), (right_dim,)), ((), ())), pre...]
    ppermute x5, waiting for transfers between devices: 55.2 us -> 20 us  [swap_seq(): return lax.ppermute(value, 'seq', [(i, i ^ mask) for i in range(count)])]
    ppermute x6 -> x15, waiting for transfers between devices: 3.36 us -> 38.3 us  [swap_member(): lax.ppermute(value, ('batch', 'seq'), [(i, i // members * members + (i %...]
    ppermute x38 -> x47, starting transfers between devices: 51.3 us -> 75 us  [swap_batch(): return lax.ppermute(value, 'batch', [(i, i ^ mask) for i in range(count)])]
    ppermute x38 -> x47, waiting for transfers between devices: 80.5 us -> 102 us  [swap_batch(): return lax.ppermute(value, 'batch', [(i, i ^ mask) for i in range(count)])]
    ppermute x0 -> x12, starting transfers between devices: none -> 19.2 us  [the longest x3 5.78 us: reduce_merger(): out = out + lax.ppermute(piece, every, pairs).astype(F32)]
  transfers between devices with their start and end apart: 51 -> 79, of which waited for: 21 -> 34; matrix products, arithmetic and copies ran while one was open for 27% -> 17% of each run, Pallas kernels for 29% -> 9%
where the time goes in v2:
time: 515 us; the launch traced here: 508 us
  waiting for transfers between devices  179 us (35%)
  Pallas kernels  122 us (24%)
  starting transfers between devices  109 us (21%)
  local copies, waits for them, and re-layouts  54.3 us (11%)
  other arithmetic  40.8 us (8%)
    ppermute x47, waiting for transfers between devices, swap_batch(): return lax.ppermute(value, 'batch', [(i, i ^ mask) for i in range(count)])  102 us
    ppermute x47, starting transfers between devices, swap_batch(): return lax.ppermute(value, 'batch', [(i, i ^ mask) for i in range(count)])  75 us
    pallas_call x1, Pallas kernels, feed(): pl.pallas_call(functools.partial(feed_kernel, groups), grid_spec=pltpu.Pr...  43.8 us
    pallas_call x1, Pallas kernels, attend(): pl.pallas_call(functools.partial(attend_kernel, heads, block), grid_spec=...  41.8 us
    ppermute x15, waiting for transfers between devices, swap_member(): lax.ppermute(value, ('batch', 'seq'), [(i, i // members * members + (i %...  38.3 us
    ppermute x5, waiting for transfers between devices, swap_seq(): return lax.ppermute(value, 'seq', [(i, i ^ mask) for i in range(count)])  20 us
    pallas_call x1, Pallas kernels, mixer_back(): pl.pallas_call(functools.partial(mixer_kernel, groups), grid_spec=pltpu.P...  19.4 us
    pallas_call x1, Pallas kernels, project_all(): pl.pallas_call(functools.partial(project_kernel, groups), grid_spec=pltpu...  12 us
  transfers between devices with their start and end apart: 79, of which 34 were waited for; matrix products, arithmetic and copies ran while one was open for 17% of the time, Pallas kernels for 9%

profile of v2, /device:TPU:0, one launch (start us, length us, event | category | flops | bytes accessed | tf_op | source)
XLA Modules:
  0.0 507.6 jit_solution(18068773446523811197)
XLA Ops:
  4.9 5.4 %concatenate.247 = bf16[416]{0:T(512)(128)(2,1)S(1)} concatenate(bf16[32]{0:T(256)(128)(2,1)} %param.18, bf16[32]{0:T(256)(128)(2,1)} %param.19, bf16[96]{0:T(256)(128)(2,1)} %param.21, bf16[32]{0:T(256)(128)(2,1)} %param.23, bf16[32]{0:T(256)(128)(2,1)} %param.24, bf16[32]{0:T(256)(128)(2,1)} %param.25, bf16[128]{0:T(256)(128)(2,1)} %param.27, bf16[32]{0:T(256)(128)(2,1)} %param.29), dimensions={0} | concatenate | bytes 1664 | tf_op jit(solution)/shard_map/concatenate | solution.py:630
  25.6 5.6 %multiply_sine_fusion = (f32[2,1024,128]{2,1,0:T(8,128)}, f32[2,1024,128]{2,1,0:T(8,128)}) fusion(f32[128]{0:T(128)S(1)} %compare_select_fusion.2, f32[2,1024]{1,0:T(2,128)S(1)} %subtract_convert_fusion), kind=kLoop, calls=%fused_computation.27 | loop fusion | flops 262144 | bytes 2105856 | tf_op jit(solution)/shard_map/sin | solution.py:589
  33.1 10.4 %collective-permute-done.30 = bf16[1,32,768]{2,1,0:T(8,128)(2,1)S(1)} collective-permute-done((bf16[1,32,768]{2,1,0:T(8,128)(2,1)}, bf16[1,32,768]{2,1,0:T(8,128)(2,1)S(1)}, u32[]{:S(2)}, u32[]{:S(2)}) %collective-permute-start.30) | collective-permute-done | bytes 49184 | tf_op jit(solution)/shard_map/ppermute | solution.py:37
  55.2 3.6 collective-permute-start.14
  58.9 11.5 %collective-permute-done.32 = bf16[1,32,768]{2,1,0:T(8,128)(2,1)S(1)} collective-permute-done((bf16[1,32,768]{2,1,0:T(8,128)(2,1)}, bf16[1,32,768]{2,1,0:T(8,128)(2,1)S(1)}, u32[]{:S(2)}, u32[]{:S(2)}) %collective-permute-start.32) | collective-permute-done | bytes 49184 | tf_op jit(solution)/shard_map/ppermute | solution.py:37
  76.8 9.2 %collective-permute-done.10.refs_2_ = bf16[144,1024]{1,0:T(8,128)(2,1)S(1)} collective-permute-done((bf16[144,1024]{1,0:T(8,128)(2,1)S(1)}, bf16[144,1024]{1,0:T(8,128)(2,1)S(1)}, u32[]{:S(2)}, u32[]{:S(2)}) %collective-permute-start.10) | collective-permute-done | bytes 294944 | tf_op jit(solution)/shard_map/ppermute | solution.py:26
  94.7 4.6 collective-permute-done.11.refs_3_
  100.6 10.5 %collective-permute-done.13.refs_5_ = bf16[144,1024]{1,0:T(8,128)(2,1)S(1)} collective-permute-done((bf16[144,1024]{1,0:T(8,128)(2,1)S(1)}, bf16[144,1024]{1,0:T(8,128)(2,1)S(1)}, u32[]{:S(2)}, u32[]{:S(2)}) %collective-permute-start.13) | collective-permute-done | bytes 294944 | tf_op jit(solution)/shard_map/ppermute | solution.py:26
  127.1 5.1 %collective-permute-done.29 = bf16[1,128,1024]{2,1,0:T(8,128)(2,1)S(1)} collective-permute-done((bf16[1,128,1024]{2,1,0:T(8,128)(2,1)S(1)}, bf16[1,128,1024]{2,1,0:T(8,128)(2,1)S(1)}, u32[]{:S(2)}, u32[]{:S(2)}) %collective-permute-start.29) | collective-permute-done | bytes 262176 | tf_op jit(solution)/shard_map/ppermute | solution.py:26
  138.7 6.5 %collective-permute-done.19.refs_12_ = bf16[128,1024]{1,0:T(8,128)(2,1)S(1)} collective-permute-done((bf16[128,1024]{1,0:T(8,128)(2,1)}, bf16[128,1024]{1,0:T(8,128)(2,1)S(1)}, u32[]{:S(2)}, u32[]{:S(2)}) %collective-permute-start.19) | collective-permute-done | bytes 262176 | tf_op jit(solution)/shard_map/ppermute | solution.py:26
  145.3 3.5 collective-permute-start.21
  150.9 3.7 maximum_maximum_fusion.1
  159.8 4.1 collective-permute-done.18.refs_11_
  164.7 3.6 collective-permute-start.38
  168.3 3.6 maximum_maximum_fusion
  174.0 5.8 %collective-permute-done.36.refs_4_ = bf16[128,768]{1,0:T(8,128)(2,1)S(1)} collective-permute-done((bf16[128,768]{1,0:T(8,128)(2,1)S(1)}, bf16[128,768]{1,0:T(8,128)(2,1)S(1)}, u32[]{:S(2)}, u32[]{:S(2)}) %collective-permute-start.36) | collective-permute-done | bytes 196640 | tf_op jit(solution)/shard_map/ppermute | solution.py:26
  182.6 43.8 %shard_map.254 = (bf16[2048,1024]{1,0:T(8,128)(2,1)}, bf16[2048,1024]{1,0:T(8,128)(2,1)}, f32[2,1024]{1,0:T(2,128)}, f32[1,1024]{1,0:T(1,128)}, bf16[4,128,1024]...) custom-call(s32[2]{0:T(128)} %pad_add_fusion.1.info, ...), custom_call_target="tpu_custom_call" | custom-call | flops 25769803776 | bytes 16777216 | tf_op jit(solution)/shard_map/pallas_call | solution.py:287
  227.3 12.0 %shard_map.255 = (bf16[2048,1024]{1,0:T(8,128)(2,1)}, f32[2048,768]{1,0:T(8,128)}, bf16[2048,256]{1,0:T(8,128)(2,1)}) custom-call(s32[2]{0:T(128)} %pad_add_fusion.1.info, bf16[2048,1024]{1,0:T(8,128)(2,1)} %bitcast.254, bf16[2048,1024]{1,0:T(8,128)(2,1)} %bitcast.246, f32[1,1024]{1,0:T(1,128)} %reshape.768.gain_ref, f32[1,1024]{1,0:T(1,128)} %reshape.769.shift_ref, ...), custom_call_target="tpu_custom_call" | custom-call | flops 4294967296 | bytes 20971520 | tf_op jit(solution)/shard_map/pallas_call | solution.py:342
  239.3 41.8 %shard_map.256 = (bf16[2048,256]{1,0:T(8,128)(2,1)}, bf16[3,2048,256]{2,1,0:T(8,128)(2,1)}) custom-call(s32[2]{0:T(128)} %pad_add_fusion.1.info, f32[2048,768]{1,0:T(8,128)} %get-tuple-element.41.q_ref.k_ref.v_ref, f32[2048,768]{1,0:T(8,128)} %get-tuple-element.41.q_ref.k_ref.v_ref, f32[2048,768]{1,0:T(8,128)} %get-tuple-element.41.q_ref.k_ref.v_ref, ...), custom_call_target="tpu_custom_call" | custom-call | flops 6442450944 | bytes 12582912 | tf_op jit(solution)/shard_map/pallas_call | solution.py:554
  281.1 19.4 %shard_map.258 = (bf16[2048,1024]{1,0:T(8,128)(2,1)}, f32[2,1024]{1,0:T(2,128)}, f32[1,768]{1,0:T(1,128)}, bf16[4,128,768]{2,1,0:T(8,128)(2,1)}, bf16[4,128,768]{2,1,0:T(8,128)(2,1)}) custom-call(s32[2]{0:T(128)} %pad_add_fusion.1.info, bf16[2048,1024]{1,0:T(8,128)(2,1)} %bitcast.255, bf16[2048,1024]{1,0:T(8,128)(2,1)} %get-tuple-element.45.first_ref, ...), custom_call_target="tpu_custom_call" | custom-call | flops 6442450944 | bytes 20971520 | tf_op jit(solution)/shard_map/pallas_call | solution.py:424
  304.9 5.0 shard_map.257
  331.8 8.2 %collective-permute-done.62 = bf16[128,1024]{1,0:T(8,128)(2,1)S(1)} collective-permute-done((bf16[128,1024]{1,0:T(8,128)(2,1)S(1)}, bf16[128,1024]{1,0:T(8,128)(2,1)S(1)}, u32[]{:S(2)}, u32[]{:S(2)}) %collective-permute-start.62) | collective-permute-done | bytes 262176 | tf_op jit(solution)/shard_map/ppermute | solution.py:155
  341.7 11.6 %collective-permute-done.54 = bf16[4,128,768]{2,1,0:T(8,128)(2,1)} collective-permute-done((bf16[4,128,768]{2,1,0:T(8,128)(2,1)}, bf16[4,128,768]{2,1,0:T(8,128)(2,1)}, u32[]{:S(2)}, u32[]{:S(2)}) %collective-permute-start.54) | collective-permute-done | bytes 786464 | tf_op jit(solution)/shard_map/ppermute | solution.py:26
  354.8 6.2 %collective-permute-start.55 = (bf16[128,768]{1,0:T(8,128)(2,1)S(1)}, bf16[128,768]{1,0:T(8,128)(2,1)S(1)}, u32[]{:S(2)}, u32[]{:S(2)}) collective-permute-start(bf16[128,768]{1,0:T(8,128)(2,1)S(1)} %get-tuple-element.72), channel_id=1, source_target_pairs={{0,8},{2,10},{4,12},{6,14},{8,0},{10,2},{12,4},{14,6},{16,24},{18,... | collective-permute-start | bytes 589832 | tf_op jit(solution)/shard_map/ppermute | solution.py:26
  368.4 6.9 %collective-permute-done.56 = bf16[128,768]{1,0:T(8,128)(2,1)S(1)} collective-permute-done((bf16[128,768]{1,0:T(8,128)(2,1)S(1)}, bf16[128,768]{1,0:T(8,128)(2,1)S(1)}, u32[]{:S(2)}, u32[]{:S(2)}) %collective-permute-start.56) | collective-permute-done | bytes 196640 | tf_op jit(solution)/shard_map/ppermute | solution.py:26
  383.8 3.7 collective-permute-done.58
  399.7 6.4 %collective-permute-done.69 = bf16[128,1024]{1,0:T(8,128)(2,1)} collective-permute-done((bf16[128,1024]{1,0:T(8,128)(2,1)}, bf16[128,1024]{1,0:T(8,128)(2,1)}, u32[]{:S(2)}, u32[]{:S(2)}) %collective-permute-start.69) | collective-permute-done | bytes 262176 | tf_op jit(solution)/shard_map/ppermute | solution.py:26
  406.1 9.2 %collective-permute-done.70 = bf16[128,1024]{1,0:T(8,128)(2,1)} collective-permute-done((bf16[128,1024]{1,0:T(8,128)(2,1)}, bf16[128,1024]{1,0:T(8,128)(2,1)}, u32[]{:S(2)}, u32[]{:S(2)}) %collective-permute-start.70) | collective-permute-done | bytes 262176 | tf_op jit(solution)/shard_map/ppermute | solution.py:26
  428.2 9.4 %collective-permute-done.77 = bf16[128,1024]{1,0:T(8,128)(2,1)S(1)} collective-permute-done((bf16[128,1024]{1,0:T(8,128)(2,1)S(1)}, bf16[128,1024]{1,0:T(8,128)(2,1)S(1)}, u32[]{:S(2)}, u32[]{:S(2)}) %collective-permute-start.77) | collective-permute-done | bytes 262176 | tf_op jit(solution)/shard_map/ppermute | solution.py:26
  440.6 10.2 %collective-permute-done.72 = bf16[1,32,1024]{2,1,0:T(8,128)(2,1)S(1)} collective-permute-done((bf16[1,32,1024]{2,1,0:T(8,128)(2,1)S(1)}, bf16[1,32,1024]{2,1,0:T(8,128)(2,1)S(1)}, u32[]{:S(2)}, u32[]{:S(2)}) %collective-permute-start.72) | collective-permute-done | bytes 65568 | tf_op jit(solution)/shard_map/ppermute | solution.py:37
  451.7 20.0 %collective-permute-done.44 = bf16[1,512,1024]{2,1,0:T(8,128)(2,1)S(1)} collective-permute-done((bf16[1,512,1024]{2,1,0:T(8,128)(2,1)S(1)}, bf16[1,512,1024]{2,1,0:T(8,128)(2,1)S(1)}, u32[]{:S(2)}, u32[]{:S(2)}) %collective-permute-start.44) | collective-permute-done | bytes 1048608 | tf_op jit(solution)/shard_map/ppermute | solution.py:31
  479.8 16.6 %collective-permute-start.48 = (f32[4,416]{1,0:T(4,128)S(1)}, f32[4,416]{1,0:T(4,128)S(1)}, u32[]{:S(2)}, u32[]{:S(2)}) collective-permute-start(f32[4,416]{1,0:T(4,128)S(1)} %get-tuple-element.114), channel_id=1, source_target_pairs={{0,8},{2,10},{4,12},{6,14},{8,0},{10,2},{12,4},{14,6},{16,24},{18,... | collective-permute-start | bytes 19976 | tf_op jit(solution)/shard_map/ppermute | solution.py:26
  (442 shorter events, 178.0 us)
Async XLA Ops:
  11.1 34.0 %collective-permute-start.6 = (bf16[1,33,1024]{2,0,1:T(2,128)(2,1)S(1)}, bf16[1,33,1024]{2,0,1:T(2,128)(2,1)}, u32[]{:S(2)}, u32[]{:S(2)}) collective-permute-start(bf16[1,33,1024]{2,0,1:T(2,128)(2,1)S(1)} %get-tuple-element.80), channel_id=1, source_target_pairs={{0,1},{1,0},{2,3},{3,2},{4,5},{5,4},{6,7},{7,6},{8,9},{9,8},{10,11... | collective-permute-start | bytes 202760 | tf_op jit(solution)/shard_map/ppermute | solution.py:37
  11.4 38.2 %collective-permute-start.7 = (bf16[1,33,1024]{2,0,1:T(2,128)(2,1)S(1)}, bf16[1,33,1024]{2,0,1:T(2,128)(2,1)S(1)}, u32[]{:S(2)}, u32[]{:S(2)}) collective-permute-start(bf16[1,33,1024]{2,0,1:T(2,128)(2,1)S(1)} %get-tuple-element.81), channel_id=1, source_target_pairs={{0,2},{1,3},{2,0},{3,1},{4,6},{5,7},{6,4},{7,5},{8,10},{9,11},{10,... | collective-permute-start | bytes 202760 | tf_op jit(solution)/shard_map/ppermute | solution.py:37
  11.7 115.1 %collective-permute-start = (bf16[1,512,1024]{2,1,0:T(8,128)(2,1)}, bf16[1,512,1024]{2,1,0:T(8,128)(2,1)}, u32[]{:S(2)}, u32[]{:S(2)}) collective-permute-start(bf16[1,512,1024]{2,1,0:T(8,128)(2,1)} %param.15), channel_id=1, source_target_pairs={{0,1},{1,0},{2,3},{3,2},{4,5},{5,4},{6,7},{7,6},{8,9},{9,8},{10,11... | collective-permute-start | bytes 3145736 | tf_op jit(solution)/shard_map/ppermute | solution.py:31
  21.3 30.2 %collective-permute-start.8 = (bf16[1,33,1024]{2,0,1:T(2,128)(2,1)S(1)}, bf16[1,33,1024]{2,0,1:T(2,128)(2,1)S(1)}, u32[]{:S(2)}, u32[]{:S(2)}) collective-permute-start(bf16[1,33,1024]{2,0,1:T(2,128)(2,1)S(1)} %get-tuple-element.78), channel_id=1, source_target_pairs={{0,3},{1,2},{2,1},{3,0},{4,7},{5,6},{6,5},{7,4},{8,11},{9,10},{10,... | collective-permute-start | bytes 202760 | tf_op jit(solution)/shard_map/ppermute | solution.py:37
  22.7 20.9 %collective-permute-start.30 = (bf16[1,32,768]{2,1,0:T(8,128)(2,1)}, bf16[1,32,768]{2,1,0:T(8,128)(2,1)S(1)}, u32[]{:S(2)}, u32[]{:S(2)}) collective-permute-start(bf16[1,32,768]{2,1,0:T(8,128)(2,1)} %get-tuple-element.95), channel_id=1, source_target_pairs={{0,1},{1,0},{2,3},{3,2},{4,5},{5,4},{6,7},{7,6},{8,9},{9,8},{10,11... | collective-permute-start | bytes 147464 | tf_op jit(solution)/shard_map/ppermute | solution.py:37
  44.8 77.6 %collective-permute-start.3 = (bf16[1,512,1024]{2,1,0:T(8,128)(2,1)S(1)}, bf16[1,512,1024]{2,1,0:T(8,128)(2,1)}, u32[]{:S(2)}, u32[]{:S(2)}) collective-permute-start(bf16[1,512,1024]{2,1,0:T(8,128)(2,1)S(1)} %copy-done.8), channel_id=1, source_target_pairs={{0,1},{1,0},{2,3},{3,2},{4,5},{5,4},{6,7},{7,6},{8,9},{9,8},{10,11... | collective-permute-start | bytes 3145736 | tf_op jit(solution)/shard_map/ppermute | solution.py:31
  45.1 25.2 %collective-permute-start.32 = (bf16[1,32,768]{2,1,0:T(8,128)(2,1)}, bf16[1,32,768]{2,1,0:T(8,128)(2,1)S(1)}, u32[]{:S(2)}, u32[]{:S(2)}) collective-permute-start(bf16[1,32,768]{2,1,0:T(8,128)(2,1)} %get-tuple-element.93), channel_id=1, source_target_pairs={{0,3},{1,2},{2,1},{3,0},{4,7},{5,6},{6,5},{7,4},{8,11},{9,10},{10,... | collective-permute-start | bytes 147464 | tf_op jit(solution)/shard_map/ppermute | solution.py:37
  53.7 21.0 %collective-permute-start.9 = (bf16[144,1024]{1,0:T(8,128)(2,1)S(1)}, bf16[144,1024]{1,0:T(8,128)(2,1)S(1)}, u32[]{:S(2)}, u32[]{:S(2)}) collective-permute-start(bf16[144,1024]{1,0:T(8,128)(2,1)S(1)} %fusion.24.refs_0_), channel_id=1, source_target_pairs={{0,4},{2,6},{4,0},{6,2},{8,12},{10,14},{12,8},{14,10},{16,20},{18,... | collective-permute-start | bytes 884744 | tf_op jit(solution)/shard_map/ppermute | solution.py:26
  90.9 22.3 %collective-permute-start.15 = (bf16[144,1024]{1,0:T(8,128)(2,1)S(1)}, bf16[144,1024]{1,0:T(8,128)(2,1)S(1)}, u32[]{:S(2)}, u32[]{:S(2)}) collective-permute-start(bf16[144,1024]{1,0:T(8,128)(2,1)S(1)} %collective-permute-done.14.refs_6_), channel_id=1, source_target_pairs={{0,4},{2,6},{4,0},{6,2},{8,12},{10,14},{12,8},{14,10},{16,20},{18,... | collective-permute-start | bytes 884744 | tf_op jit(solution)/shard_map/ppermute | solution.py:26
  119.6 29.2 %collective-permute-start.4 = (bf16[1,512,1024]{2,1,0:T(8,128)(2,1)S(1)}, bf16[1,512,1024]{2,1,0:T(8,128)(2,1)}, u32[]{:S(2)}, u32[]{:S(2)}) collective-permute-start(bf16[1,512,1024]{2,1,0:T(8,128)(2,1)S(1)} %copy-done.8), channel_id=1, source_target_pairs={{0,2},{2,0},{4,6},{6,4},{8,10},{10,8},{12,14},{14,12},{16,18},{18,... | collective-permute-start | bytes 3145736 | tf_op jit(solution)/shard_map/ppermute | solution.py:26
  122.4 41.4 %collective-permute-start.1 = (bf16[1,512,1024]{2,1,0:T(8,128)(2,1)S(1)}, bf16[1,512,1024]{2,1,0:T(8,128)(2,1)}, u32[]{:S(2)}, u32[]{:S(2)}) collective-permute-start(bf16[1,512,1024]{2,1,0:T(8,128)(2,1)S(1)} %copy-done.6), channel_id=1, source_target_pairs={{0,2},{2,0},{4,6},{6,4},{8,10},{10,8},{12,14},{14,12},{16,18},{18,... | collective-permute-start | bytes 3145736 | tf_op jit(solution)/shard_map/ppermute | solution.py:26
  122.4 27.9 %collective-permute-start.5 = (bf16[1,512,1024]{2,1,0:T(8,128)(2,1)}, bf16[1,512,1024]{2,1,0:T(8,128)(2,1)}, u32[]{:S(2)}, u32[]{:S(2)}) collective-permute-start(bf16[1,512,1024]{2,1,0:T(8,128)(2,1)} %collective-permute-done.3), channel_id=1, source_target_pairs={{0,2},{2,0},{4,6},{6,4},{8,10},{10,8},{12,14},{14,12},{16,18},{18,... | collective-permute-start | bytes 3145736 | tf_op jit(solution)/shard_map/ppermute | solution.py:26
  126.9 37.8 %collective-permute-start.2 = (bf16[1,512,1024]{2,1,0:T(8,128)(2,1)}, bf16[1,512,1024]{2,1,0:T(8,128)(2,1)}, u32[]{:S(2)}, u32[]{:S(2)}) collective-permute-start(bf16[1,512,1024]{2,1,0:T(8,128)(2,1)} %collective-permute-done), channel_id=1, source_target_pairs={{0,2},{2,0},{4,6},{6,4},{8,10},{10,8},{12,14},{14,12},{16,18},{18,... | collective-permute-start | bytes 3145736 | tf_op jit(solution)/shard_map/ppermute | solution.py:26
  158.2 23.6 %collective-permute-start.22 = (bf16[128,1024]{1,0:T(8,128)(2,1)S(1)}, bf16[128,1024]{1,0:T(8,128)(2,1)S(1)}, u32[]{:S(2)}, u32[]{:S(2)}) collective-permute-start(bf16[128,1024]{1,0:T(8,128)(2,1)S(1)} %collective-permute-done.21.refs_14_), channel_id=1, source_target_pairs={{0,4},{2,6},{4,0},{6,2},{8,12},{10,14},{12,8},{14,10},{16,20},{18,... | collective-permute-start | bytes 786440 | tf_op jit(solution)/shard_map/ppermute | solution.py:26
  171.9 54.5 %collective-permute-start.33 = (bf16[128,768]{1,0:T(8,128)(2,1)S(1)}, bf16[128,768]{1,0:T(8,128)(2,1)S(1)}, u32[]{:S(2)}, u32[]{:S(2)}) collective-permute-start(bf16[128,768]{1,0:T(8,128)(2,1)S(1)} %bitcast.289), channel_id=1, source_target_pairs={{0,4},{2,6},{4,0},{6,2},{8,12},{10,14},{12,8},{14,10},{16,20},{18,... | collective-permute-start | bytes 589832 | tf_op jit(solution)/shard_map/ppermute | solution.py:26
  173.5 53.0 %collective-permute-start.35 = (bf16[128,768]{1,0:T(8,128)(2,1)S(1)}, bf16[128,768]{1,0:T(8,128)(2,1)S(1)}, u32[]{:S(2)}, u32[]{:S(2)}) collective-permute-start(bf16[128,768]{1,0:T(8,128)(2,1)S(1)} %collective-permute-done.34.refs_2_), channel_id=1, source_target_pairs={{0,4},{2,6},{4,0},{6,2},{8,12},{10,14},{12,8},{14,10},{16,20},{18,... | collective-permute-start | bytes 589832 | tf_op jit(solution)/shard_map/ppermute | solution.py:26
  179.8 46.7 %collective-permute-start.37 = (bf16[128,768]{1,0:T(8,128)(2,1)S(1)}, bf16[128,768]{1,0:T(8,128)(2,1)S(1)}, u32[]{:S(2)}, u32[]{:S(2)}) collective-permute-start(bf16[128,768]{1,0:T(8,128)(2,1)S(1)} %collective-permute-done.36.refs_4_), channel_id=1, source_target_pairs={{0,4},{2,6},{4,0},{6,2},{8,12},{10,14},{12,8},{14,10},{16,20},{18,... | collective-permute-start | bytes 589832 | tf_op jit(solution)/shard_map/ppermute | solution.py:26
  181.3 45.2 %collective-permute-start.39 = (bf16[128,768]{1,0:T(8,128)(2,1)S(1)}, bf16[128,768]{1,0:T(8,128)(2,1)S(1)}, u32[]{:S(2)}, u32[]{:S(2)}) collective-permute-start(bf16[128,768]{1,0:T(8,128)(2,1)S(1)} %collective-permute-done.38.refs_6_), channel_id=1, source_target_pairs={{0,4},{2,6},{4,0},{6,2},{8,12},{10,14},{12,8},{14,10},{16,20},{18,... | collective-permute-start | bytes 589832 | tf_op jit(solution)/shard_map/ppermute | solution.py:26
  315.6 73.7 %collective-permute-start.68 = (bf16[4,128,1024]{2,1,0:T(8,128)(2,1)}, bf16[4,128,1024]{2,1,0:T(8,128)(2,1)}, u32[]{:S(2)}, u32[]{:S(2)}) collective-permute-start(bf16[4,128,1024]{2,1,0:T(8,128)(2,1)} %get-tuple-element.57), channel_id=1, source_target_pairs={{0,4},{2,6},{4,0},{6,2},{8,12},{10,14},{12,8},{14,10},{16,20},{18,... | collective-permute-start | bytes 3145736 | tf_op jit(solution)/shard_map/ppermute | solution.py:26
  316.1 37.2 %collective-permute-start.54 = (bf16[4,128,768]{2,1,0:T(8,128)(2,1)}, bf16[4,128,768]{2,1,0:T(8,128)(2,1)}, u32[]{:S(2)}, u32[]{:S(2)}) collective-permute-start(bf16[4,128,768]{2,1,0:T(8,128)(2,1)} %get-tuple-element.54), channel_id=1, source_target_pairs={{0,4},{2,6},{4,0},{6,2},{8,12},{10,14},{12,8},{14,10},{16,20},{18,... | collective-permute-start | bytes 2359304 | tf_op jit(solution)/shard_map/ppermute | solution.py:26
  340.1 79.7 %collective-permute-start.45 = (bf16[1,1024,1024]{2,1,0:T(8,128)(2,1)S(1)}, bf16[1,1024,1024]{2,1,0:T(8,128)(2,1)}, u32[]{:S(2)}, u32[]{:S(2)}) collective-permute-start(bf16[1,1024,1024]{2,1,0:T(8,128)(2,1)S(1)} %slice_bitcast_fusion), channel_id=1, source_target_pairs={{0,2},{2,0},{4,6},{6,4},{8,10},{10,8},{12,14},{14,12},{16,18},{18,... | collective-permute-start | bytes 6291464 | tf_op jit(solution)/shard_map/ppermute | solution.py:26
  368.4 26.7 %collective-permute-start.75 = (bf16[4,128,1024]{2,1,0:T(8,128)(2,1)S(1)}, bf16[4,128,1024]{2,1,0:T(8,128)(2,1)S(1)}, u32[]{:S(2)}, u32[]{:S(2)}) collective-permute-start(bf16[4,128,1024]{2,1,0:T(8,128)(2,1)S(1)} %copy-done.43), channel_id=1, source_target_pairs={{0,4},{2,6},{4,0},{6,2},{8,12},{10,14},{12,8},{14,10},{16,20},{18,... | collective-permute-start | bytes 3145736 | tf_op jit(solution)/shard_map/ppermute | solution.py:26
  375.3 48.2 %collective-permute-start.43 = (bf16[1,1024,1024]{2,1,0:T(8,128)(2,1)}, bf16[1,1024,1024]{2,1,0:T(8,128)(2,1)}, u32[]{:S(2)}, u32[]{:S(2)}) collective-permute-start(bf16[1,1024,1024]{2,1,0:T(8,128)(2,1)} %slice_bitcast_fusion.1), channel_id=1, source_target_pairs={{0,2},{2,0},{4,6},{6,4},{8,10},{10,8},{12,14},{14,12},{16,18},{18,... | collective-permute-start | bytes 6291464 | tf_op jit(solution)/shard_map/ppermute | solution.py:26
  393.6 21.7 %collective-permute-start.70 = (bf16[128,1024]{1,0:T(8,128)(2,1)}, bf16[128,1024]{1,0:T(8,128)(2,1)}, u32[]{:S(2)}, u32[]{:S(2)}) collective-permute-start(bf16[128,1024]{1,0:T(8,128)(2,1)} %get-tuple-element.71), channel_id=1, source_target_pairs={{0,16},{2,18},{4,20},{6,22},{8,24},{10,26},{12,28},{14,30},{16,0},... | collective-permute-start | bytes 786440 | tf_op jit(solution)/shard_map/ppermute | solution.py:26
  406.1 22.1 %collective-permute-start.76 = (bf16[128,1024]{1,0:T(8,128)(2,1)S(1)}, bf16[128,1024]{1,0:T(8,128)(2,1)S(1)}, u32[]{:S(2)}, u32[]{:S(2)}) collective-permute-start(bf16[128,1024]{1,0:T(8,128)(2,1)S(1)} %get-tuple-element.66), channel_id=1, source_target_pairs={{0,8},{2,10},{4,12},{6,14},{8,0},{10,2},{12,4},{14,6},{16,24},{18,... | collective-permute-start | bytes 786440 | tf_op jit(solution)/shard_map/ppermute | solution.py:26
  415.3 22.4 %collective-permute-start.77 = (bf16[128,1024]{1,0:T(8,128)(2,1)S(1)}, bf16[128,1024]{1,0:T(8,128)(2,1)S(1)}, u32[]{:S(2)}, u32[]{:S(2)}) collective-permute-start(bf16[128,1024]{1,0:T(8,128)(2,1)S(1)} %get-tuple-element.68), channel_id=1, source_target_pairs={{0,16},{2,18},{4,20},{6,22},{8,24},{10,26},{12,28},{14,30},{16,0},... | collective-permute-start | bytes 786440 | tf_op jit(solution)/shard_map/ppermute | solution.py:26
  415.3 22.4 %collective-permute-start.78 = (bf16[128,1024]{1,0:T(8,128)(2,1)S(1)}, bf16[128,1024]{1,0:T(8,128)(2,1)S(1)}, u32[]{:S(2)}, u32[]{:S(2)}) collective-permute-start(bf16[128,1024]{1,0:T(8,128)(2,1)S(1)} %get-tuple-element.67), channel_id=1, source_target_pairs={{0,24},{2,26},{4,28},{6,30},{8,16},{10,18},{12,20},{14,22},{16,8},... | collective-permute-start | bytes 786440 | tf_op jit(solution)/shard_map/ppermute | solution.py:26
  423.2 27.6 %collective-permute-start.46 = (bf16[1,512,1024]{2,1,0:T(8,128)(2,1)S(1)}, bf16[1,512,1024]{2,1,0:T(8,128)(2,1)S(1)}, u32[]{:S(2)}, u32[]{:S(2)}) collective-permute-start(bf16[1,512,1024]{2,1,0:T(8,128)(2,1)S(1)} %slice.448), channel_id=1, source_target_pairs={{0,1},{1,0},{2,3},{3,2},{4,5},{5,4},{6,7},{7,6},{8,9},{9,8},{10,11... | collective-permute-start | bytes 3145736 | tf_op jit(solution)/shard_map/ppermute | solution.py:31
  423.6 27.2 %collective-permute-start.72 = (bf16[1,32,1024]{2,1,0:T(8,128)(2,1)S(1)}, bf16[1,32,1024]{2,1,0:T(8,128)(2,1)S(1)}, u32[]{:S(2)}, u32[]{:S(2)}) collective-permute-start(bf16[1,32,1024]{2,1,0:T(8,128)(2,1)S(1)} %get-tuple-element.84), channel_id=1, source_target_pairs={{0,1},{1,0},{2,3},{3,2},{4,5},{5,4},{6,7},{7,6},{8,9},{9,8},{10,11... | collective-permute-start | bytes 196616 | tf_op jit(solution)/shard_map/ppermute | solution.py:37
  428.2 22.6 %collective-permute-start.73 = (bf16[1,32,1024]{2,1,0:T(8,128)(2,1)S(1)}, bf16[1,32,1024]{2,1,0:T(8,128)(2,1)S(1)}, u32[]{:S(2)}, u32[]{:S(2)}) collective-permute-start(bf16[1,32,1024]{2,1,0:T(8,128)(2,1)S(1)} %get-tuple-element.83), channel_id=1, source_target_pairs={{0,2},{1,3},{2,0},{3,1},{4,6},{5,7},{6,4},{7,5},{8,10},{9,11},{10,... | collective-permute-start | bytes 196616 | tf_op jit(solution)/shard_map/ppermute | solution.py:37
  437.6 61.2 %collective-permute-start.74 = (bf16[1,32,1024]{2,1,0:T(8,128)(2,1)S(1)}, bf16[1,32,1024]{2,1,0:T(8,128)(2,1)S(1)}, u32[]{:S(2)}, u32[]{:S(2)}) collective-permute-start(bf16[1,32,1024]{2,1,0:T(8,128)(2,1)S(1)} %get-tuple-element.82), channel_id=1, source_target_pairs={{0,3},{1,2},{2,1},{3,0},{4,7},{5,6},{6,5},{7,4},{8,11},{9,10},{10,... | collective-permute-start | bytes 196616 | tf_op jit(solution)/shard_map/ppermute | solution.py:37
  437.7 34.0 %collective-permute-start.44 = (bf16[1,512,1024]{2,1,0:T(8,128)(2,1)S(1)}, bf16[1,512,1024]{2,1,0:T(8,128)(2,1)S(1)}, u32[]{:S(2)}, u32[]{:S(2)}) collective-permute-start(bf16[1,512,1024]{2,1,0:T(8,128)(2,1)S(1)} %slice.449), channel_id=1, source_target_pairs={{0,1},{1,0},{2,3},{3,2},{4,5},{5,4},{6,7},{7,6},{8,9},{9,8},{10,11... | collective-permute-start | bytes 3145736 | tf_op jit(solution)/shard_map/ppermute | solution.py:31
  (104 other events, 1535.3 us)

commit v3 on v2

v3 whole, which is shorter than its diff:
```python
import functools

import jax
import jax.numpy as jnp
from jax import lax
from jax.experimental import pallas as pl
from jax.experimental.pallas import tpu as pltpu
from jax.sharding import PartitionSpec as P

HD = 64
ROT = 16
EPS = 1e-05
SCALE = 0.125
F32 = jnp.float32
BF = jnp.bfloat16


def dot(left, right, left_dim, right_dim):
    return lax.dot_general(
        left, right, (((left_dim,), (right_dim,)), ((), ())), preferred_element_type=F32
    )


def swap_batch(value, mask):
    count = lax.axis_size("batch")
    return lax.ppermute(value, "batch", [(i, i ^ mask) for i in range(count)])


def swap_seq(value, mask):
    count = lax.axis_size("seq")
    return lax.ppermute(value, "seq", [(i, i ^ mask) for i in range(count)])


def swap_member(value, mask):
    members = 2 * lax.axis_size("seq")
    count = lax.axis_size("batch") * lax.axis_size("seq")
    return lax.ppermute(
        value,
        ("batch", "seq"),
        [(i, (i // members) * members + ((i % members) ^ mask)) for i in range(count)],
    )


def after(value, *others):
    return lax.optimization_barrier((value,) + others)[0]


def sort_groups(value):
    groups = value.shape[0]
    me = lax.axis_index("batch") // 2
    bit = 1
    while bit < groups:
        paired = value.reshape((groups // (2 * bit), 2, bit) + value.shape[1:])
        flipped = jnp.concatenate([paired[:, 1:], paired[:, :1]], 1)
        value = jnp.where((me & bit) > 0, flipped, paired).reshape(value.shape)
        bit = 2 * bit
    return value


LIGHT = pl.CostEstimate(flops=1000, bytes_accessed=1000, transcendentals=0)


def far_groups(chunk):
    groups = lax.axis_size("batch") // 2
    return jnp.stack([chunk] + [swap_batch(chunk, 4 * k) for k in range(1, groups // 2)])


def near_groups(stack):
    return swap_batch(stack, 2)


def fold_near(send, keep):
    return send.shape[0], keep, swap_batch(send, 2), send.dtype


def fold_far(state, *others):
    half, keep, got, dtype = state
    total = keep[0].astype(F32) + got[0].astype(F32)
    for k in range(1, half):
        piece = (keep[k].astype(F32) + got[k].astype(F32)).astype(dtype)
        total = total + swap_batch(after(piece, *others), 4 * k).astype(F32)
    return total


def member():
    return (lax.axis_index("batch") % 2) * lax.axis_size("seq") + lax.axis_index("seq")


def exchange_members(pieces):
    me = member()
    out = jnp.zeros_like(pieces)
    for k in range(pieces.shape[0]):
        piece = lax.dynamic_index_in_dim(pieces, me ^ k, 0, keepdims=True)
        got = piece if k == 0 else swap_member(piece, k)
        out = lax.dynamic_update_slice_in_dim(out, got, me ^ k, 0)
    return out


def gather_merger(block):
    seq = lax.axis_size("seq")
    batch = lax.axis_size("batch")
    members = 2 * seq
    groups = batch // 2
    lows = groups // members
    every = ("batch", "seq")
    group = lax.axis_index("batch") // 2
    root = group // lows
    found = jnp.where(member() == root, block, jnp.zeros_like(block))
    for k in range(1, members):
        pairs = [
            (g * members + g // lows, (g ^ (k * lows)) * members + g // lows) for g in range(groups)
        ]
        found = found + lax.ppermute(block, every, pairs)
    whole = found[None]
    bit = 1
    while bit < lows:
        got = swap_batch(whole, 2 * bit)
        swapped = (group & bit) > 0
        whole = jnp.where(swapped, jnp.concatenate([got, whole]), jnp.concatenate([whole, got]))
        bit = 2 * bit
    return whole.reshape(-1, block.shape[1])


def far_tokens(value, *others):
    if lax.axis_size("seq") == 2:
        return jnp.concatenate([value, swap_seq(after(value, *others), 1)], 1)
    return lax.all_gather(value, "seq", axis=1, tiled=True)


def near_tokens(value, *others):
    seqs = value.shape[0] // 2
    return value[:seqs].astype(F32) + swap_batch(value[seqs:], 1).astype(F32)


def part_tokens(mine, *others):
    if lax.axis_size("seq") == 2:
        stretch = mine.shape[1] // 2
        return mine[:, :stretch] + swap_seq(after(mine[:, stretch:].astype(BF), *others), 1).astype(F32)
    return lax.psum_scatter(mine.astype(BF), "seq", scatter_dimension=1, tiled=True).astype(F32)


def reduce_merger(grad):
    seq = lax.axis_size("seq")
    batch = lax.axis_size("batch")
    members = 2 * seq
    groups = batch // 2
    lows = groups // members
    every = ("batch", "seq")
    group = lax.axis_index("batch") // 2
    root = group // lows
    me = member()
    whole = grad.reshape((lows, -1, grad.shape[1]))
    bit = lows // 2
    while bit:
        halves = whole.reshape((2, -1) + whole.shape[1:])
        side = ((group & bit) > 0).astype(jnp.int32)
        away = lax.dynamic_index_in_dim(halves, 1 - side, 0, keepdims=False).astype(BF)
        whole = lax.dynamic_index_in_dim(halves, side, 0, keepdims=False)
        whole = whole + swap_batch(away, 2 * bit).astype(F32)
        bit = bit // 2
    block = whole[0].astype(BF)
    total = whole[0]
    for k in range(1, members):
        pairs = [
            ((g ^ (k * lows)) * members + g // lows, g * members + g // lows) for g in range(groups)
        ]
        total = total + lax.ppermute(block, every, pairs).astype(F32)
    rows = total.reshape(members, -1, grad.shape[1]).astype(BF)
    mine = lax.dynamic_index_in_dim(rows, me, 0, keepdims=False).astype(F32)
    out = jnp.where(me == root, mine, jnp.zeros_like(mine))
    for k in range(1, members):
        pairs = [
            (g * members + g // lows, g * members + ((g // lows) ^ k)) for g in range(groups)
        ]
        piece = lax.dynamic_index_in_dim(rows, me ^ k, 0, keepdims=False)
        out = out + lax.ppermute(piece, every, pairs).astype(F32)
    return out


def centre(rows):
    mean = jnp.mean(rows, -1, keepdims=True)
    centered = rows - mean
    spread = jnp.mean(centered * centered, -1, keepdims=True)
    rstd = lax.rsqrt(spread + EPS)
    return centered * rstd, rstd


def lay(far, near, out_ref, group, rows):
    for k in range(far.shape[0]):
        out_ref[pl.ds(pl.multiple_of((group ^ (2 * k)) * rows, rows), rows), :] = far[k, :rows, :]
        out_ref[pl.ds(pl.multiple_of((group ^ (2 * k + 1)) * rows, rows), rows), :] = near[k, :rows, :]


def pick(own, peer):
    return jnp.where(pl.program_id(0) < pl.num_programs(0) // 2, own[...], peer[...])


def split_out(total_ref, send_ref, keep_ref, group, rows):
    for k in range(send_ref.shape[0]):
        keep = pl.multiple_of((group ^ (2 * k)) * rows, rows)
        send = pl.multiple_of((group ^ (2 * k + 1)) * rows, rows)
        keep_ref[k] = total_ref[pl.ds(keep, rows), :].astype(BF)
        send_ref[k] = total_ref[pl.ds(send, rows), :].astype(BF)


def add_rows(out_ref, i, row, value):
    total = jnp.sum(value, 0, keepdims=True)

    @pl.when(i == 0)
    def _():
        out_ref[row : row + 1, :] = total

    @pl.when(i > 0)
    def _():
        out_ref[row : row + 1, :] += total


def add_to(total_ref, i, value):
    @pl.when(i == 0)
    def _():
        total_ref[...] = value

    @pl.when(i > 0)
    def _():
        total_ref[...] += value


def whole(shape):
    return pl.BlockSpec(shape, lambda *_: (0,) * len(shape), pipeline_mode=pl.Buffered(1))


def widen_kernel(info, xo_ref, xp_ref, go_ref, gp_ref, gain_ref, shift_ref, bias_ref, far_ref, near_ref, *refs):
    active_ref, slope_ref, send_ref, keep_ref, widen, total = refs
    i = pl.program_id(0)
    group = info[0]
    share = widen.shape[0] // (2 * far_ref.shape[0])

    @pl.when(i == 0)
    def _():
        lay(far_ref, near_ref, widen, group, share)

    normed, _ = centre(pick(xo_ref, xp_ref).astype(F32))
    second = (normed * gain_ref[...] + shift_ref[...]).astype(BF)
    widened = dot(second, widen[...], 1, 0) + bias_ref[...]
    bell = 0.5 + 0.5 * lax.erf(widened * (0.5**0.5))
    active = (widened * bell).astype(BF)
    slope = bell + widened * jnp.exp(-0.5 * widened * widened) * (0.15915494309189535**0.5)
    active_ref[...] = active
    slope_ref[...] = slope.astype(BF)
    add_to(total, i, dot(active, pick(go_ref, gp_ref), 0, 0))

    @pl.when(i == pl.num_programs(0) - 1)
    def _():
        split_out(total, send_ref, keep_ref, group, total.shape[0] // (2 * far_ref.shape[0]))


def narrow_kernel(info, xo_ref, xp_ref, go_ref, gp_ref, a_ref, s_ref, gain_ref, shift_ref, *refs):
    wf_ref, wn_ref, nf_ref, nn_ref, out_ref, e_ref, sums_ref, bsum_ref, send_ref, keep_ref, widen, narrow, total = refs
    i = pl.program_id(0)
    group = info[0]
    groups = 2 * wf_ref.shape[0]
    share = widen.shape[0] // groups

    @pl.when(i == 0)
    def _():
        lay(wf_ref, wn_ref, widen, group, share)
        lay(nf_ref, nn_ref, narrow, group, narrow.shape[0] // groups)

    out_ref[...] = dot(a_ref[...], narrow[...], 1, 0).astype(BF)
    active_grad = dot(pick(go_ref, gp_ref), narrow[...], 1, 1)
    widened_grad = (active_grad * s_ref[...].astype(F32)).astype(BF)
    add_rows(bsum_ref, i, 0, widened_grad.astype(F32))
    normed, _ = centre(pick(xo_ref, xp_ref).astype(F32))
    second = (normed * gain_ref[...] + shift_ref[...]).astype(BF)
    add_to(total, i, dot(second, widened_grad, 0, 0))
    second_grad = dot(widened_grad, widen[...], 1, 1)
    add_rows(sums_ref, i, 0, second_grad * normed)
    add_rows(sums_ref, i, 1, second_grad)
    e_ref[...] = (second_grad * gain_ref[...]).astype(BF)

    @pl.when(i == pl.num_programs(0) - 1)
    def _():
        split_out(total, send_ref, keep_ref, group, share)


def tiles(rows):
    block = min(512, rows)
    steps = 2 * rows // block

    def own(n):
        return pl.BlockSpec((block, n), lambda i, *_: (jnp.minimum(i, steps // 2 - 1), 0))

    def peer(n):
        return pl.BlockSpec((block, n), lambda i, *_: (jnp.maximum(i - steps // 2, 0), 0))

    def every(n):
        return pl.BlockSpec((block, n), lambda i, *_: (i, 0))

    return block, steps, own, peer, every


def call(kernel, steps, in_specs, out_specs, out_shape, scratch, *operands):
    return pl.pallas_call(
        kernel,
        grid_spec=pltpu.PrefetchScalarGridSpec(
            num_scalar_prefetch=1, grid=(steps,), in_specs=in_specs, out_specs=out_specs, scratch_shapes=scratch
        ),
        out_shape=out_shape,
        cost_estimate=LIGHT,
        compiler_params=pltpu.CompilerParams(vmem_limit_bytes=58 * 1024 * 1024),
    )(*operands)


def feed_widen(info, inputs, upstream, gain, shift, bias, far, near):
    rows, width = inputs[0].shape
    half, _, hidden = far.shape
    _, steps, own, peer, every = tiles(rows)
    shape = (half, hidden // (2 * half), width)
    return call(
        widen_kernel,
        steps,
        [own(width), peer(width), own(width), peer(width), whole((1, width)), whole((1, width)), whole((1, hidden))]
        + [whole(far.shape), whole(near.shape)],
        [every(hidden), every(hidden), whole(shape), whole(shape)],
        [jax.ShapeDtypeStruct((2 * rows, hidden), BF)] * 2 + [jax.ShapeDtypeStruct(shape, BF)] * 2,
        [pltpu.VMEM((width, hidden), BF), pltpu.VMEM((hidden, width), F32)],
        info, *inputs, *upstream, gain, shift, bias, far, near,
    )


def feed_narrow(info, inputs, upstream, active, slope, gain, shift, widen, narrow):
    rows, width = inputs[0].shape
    half, _, hidden = widen[0].shape
    _, steps, own, peer, every = tiles(rows)
    shape = (half, width // (2 * half), hidden)
    return call(
        narrow_kernel,
        steps,
        [own(width), peer(width), own(width), peer(width), every(hidden), every(hidden), whole((1, width)), whole((1, width))]
        + [whole(part.shape) for part in widen + narrow],
        [every(width), every(width), whole((2, width)), whole((1, hidden)), whole(shape), whole(shape)],
        [
            jax.ShapeDtypeStruct((2 * rows, width), BF),
            jax.ShapeDtypeStruct((2 * rows, width), BF),
            jax.ShapeDtypeStruct((2, width), F32),
            jax.ShapeDtypeStruct((1, hidden), F32),
            jax.ShapeDtypeStruct(shape, BF),
            jax.ShapeDtypeStruct(shape, BF),
        ],
        [pltpu.VMEM((width, hidden), BF), pltpu.VMEM((hidden, width), BF), pltpu.VMEM((width, hidden), F32)],
        info, *inputs, *upstream, active, slope, gain, shift, *widen, *narrow,
    )


def project_kernel(info, xo_ref, xp_ref, go_ref, gp_ref, gain_ref, shift_ref, bias_ref, merger_ref, far_ref, near_ref, *refs):
    first_ref, project_ref, mg_ref, mixer = refs

    @pl.when(pl.program_id(0) == 0)
    def _():
        lay(far_ref, near_ref, mixer, info[0], mixer.shape[0] // (2 * far_ref.shape[0]))

    normed, _ = centre(pick(xo_ref, xp_ref).astype(F32))
    first = (normed * gain_ref[...] + shift_ref[...]).astype(BF)
    first_ref[...] = first
    project_ref[...] = dot(first, mixer[...], 1, 0) + bias_ref[...]
    mg_ref[...] = dot(pick(go_ref, gp_ref), merger_ref[...], 1, 1).astype(BF)


def project_all(info, inputs, upstream, gain, shift, bias, merger, far, near):
    rows, width = inputs[0].shape
    wide = far.shape[2]
    slim = wide // 3
    _, steps, own, peer, every = tiles(rows)
    return call(
        project_kernel,
        steps,
        [own(width), peer(width), own(width), peer(width), whole((1, width)), whole((1, width)), whole((1, wide))]
        + [whole(merger.shape), whole(far.shape), whole(near.shape)],
        [every(width), every(wide), every(slim)],
        [
            jax.ShapeDtypeStruct((2 * rows, width), BF),
            jax.ShapeDtypeStruct((2 * rows, wide), F32),
            jax.ShapeDtypeStruct((2 * rows, slim), BF),
        ],
        [pltpu.VMEM((width, wide), BF)],
        info, *inputs, *upstream, gain, shift, bias, merger, far, near,
    )


def merge_kernel(info, m_ref, go_ref, gp_ref, f_ref, w_ref, out_ref, grad_ref):
    mixed = m_ref[...]
    out_ref[...] = (dot(mixed, w_ref[...], 1, 0) + f_ref[...].astype(F32)).astype(BF)
    add_to(grad_ref, pl.program_id(0), dot(mixed, pick(go_ref, gp_ref), 0, 0))


def merge(info, mixed, upstream, partial, merger):
    rows, width = upstream[0].shape
    slim = mixed.shape[1]
    _, steps, own, peer, every = tiles(rows)
    return call(
        merge_kernel,
        steps,
        [every(slim), own(width), peer(width), every(width), whole(merger.shape)],
        [every(width), whole((slim, width))],
        [jax.ShapeDtypeStruct((2 * rows, width), BF), jax.ShapeDtypeStruct((slim, width), F32)],
        [],
        info, mixed, *upstream, partial, merger,
    )


def mixer_kernel(info, xo_ref, xp_ref, first_ref, e_ref, p_ref, gain_ref, far_ref, near_ref, *refs):
    out_ref, sums_ref, bsum_ref, send_ref, keep_ref, mixer, total = refs
    i = pl.program_id(0)
    group = info[0]
    share = mixer.shape[0] // (2 * far_ref.shape[0])

    @pl.when(i == 0)
    def _():
        lay(far_ref, near_ref, mixer, group, share)

    grad = jnp.concatenate([p_ref[0], p_ref[1], p_ref[2]], 1)
    add_to(total, i, dot(first_ref[...], grad, 0, 0))
    first_grad = dot(grad, mixer[...], 1, 1)
    normed, _ = centre(pick(xo_ref, xp_ref).astype(F32))
    out_ref[...] = (first_grad * gain_ref[...] + e_ref[...].astype(F32)).astype(BF)
    add_rows(sums_ref, i, 0, first_grad * normed)
    add_rows(sums_ref, i, 1, first_grad)
    add_rows(bsum_ref, i, 0, grad.astype(F32))

    @pl.when(i == pl.num_programs(0) - 1)
    def _():
        split_out(total, send_ref, keep_ref, group, share)


def mixer_back(info, inputs, first, error, grads, gain, far, near):
    rows, width = inputs[0].shape
    half, _, wide = far.shape
    block, steps, own, peer, every = tiles(rows)
    shape = (half, width // (2 * half), wide)
    return call(
        mixer_kernel,
        steps,
        [own(width), peer(width), every(width), every(width)]
        + [pl.BlockSpec((3, block, wide // 3), lambda i, _: (0, i, 0)), whole((1, width))]
        + [whole(far.shape), whole(near.shape)],
        [every(width), whole((2, width)), whole((1, wide)), whole(shape), whole(shape)],
        [
            jax.ShapeDtypeStruct((2 * rows, width), BF),
            jax.ShapeDtypeStruct((2, width), F32),
            jax.ShapeDtypeStruct((1, wide), F32),
            jax.ShapeDtypeStruct(shape, BF),
            jax.ShapeDtypeStruct(shape, BF),
        ],
        [pltpu.VMEM((width, wide), BF), pltpu.VMEM((width, wide), F32)],
        info, *inputs, first, error, grads, gain, far, near,
    )


def attend_kernel(heads, block, info, q_ref, k_ref, v_ref, g_ref, c_ref, s_ref, col_ref, row_ref, mixed_ref, grad_ref):
    length = q_ref.shape[0]
    half = ROT // 2
    cosine, sine = c_ref[0], s_ref[0]
    middle = length // 2
    low = pl.ds(pl.multiple_of(info[1] * middle, middle), middle)
    high = pl.ds(pl.multiple_of((1 - info[1]) * middle, middle), middle)

    def take(ref):
        return jnp.concatenate([ref[low, :], ref[high, :]], 0)

    def put(ref, value):
        ref[low, :] = value[:middle]
        ref[high, :] = value[middle:]

    def put_grad(part, value):
        grad_ref[part, low, :] = value[:middle]
        grad_ref[part, high, :] = value[middle:]

    lane = lax.broadcasted_iota(jnp.int32, cosine.shape, 1) % HD
    leading = lane < half

    def roll(value, shift):
        if value.shape[1] % 128:
            return jnp.concatenate([value[:, -shift:], value[:, :-shift]], 1)
        return pltpu.roll(value, shift % value.shape[1], 1)

    def turn(value):
        return value * cosine + jnp.where(leading, -roll(value, -half), roll(value, half)) * sine

    def turn_back(value):
        return value * cosine + jnp.where(leading, roll(value, -half), -roll(value, half)) * sine

    query = (turn(take(q_ref)).astype(BF).astype(F32) * SCALE).astype(BF)
    keys = turn(take(k_ref)).astype(BF)
    values = take(v_ref).astype(BF)
    grads = take(g_ref)
    col = col_ref[0]
    row = row_ref[0]
    dq_all, dk_all, dv_all, mixed_all = [], [], [], []
    for h in range(heads):
        span = slice(h * HD, (h + 1) * HD)
        qh, kh, vh, gh = query[:, span], keys[:, span], values[:, span], grads[:, span]
        dq_parts, mixed_parts = [], []
        dk = jnp.zeros((length, HD), F32)
        dv = jnp.zeros((length, HD), F32)
        for i in range(length // block):
            n = (i + 1) * block
            rows = slice(i * block, n)
            q, g = qh[rows], gh[rows]
            k, v = kh[:n], vh[:n]
            scores = dot(q, k, 1, 1)
            place_q = lax.broadcasted_iota(jnp.int32, (block, n), 0) + i * block
            place_k = lax.broadcasted_iota(jnp.int32, (block, n), 1)
            allowed = (col[rows] == row[:, :n]) & (place_q >= place_k)
            scores = jnp.where(allowed, scores, -1e30)
            expo = jnp.exp(scores - jnp.max(scores, -1, keepdims=True))
            prob = expo * (1.0 / jnp.sum(expo, -1, keepdims=True))
            prob_b = prob.astype(BF)
            mixed_parts.append(dot(prob_b, v, 1, 0))
            prob_grad = dot(g, v, 1, 1)
            center = jnp.sum(prob * prob_grad, -1, keepdims=True)
            score_grad = (prob * (prob_grad - center)).astype(BF)
            dq_parts.append(dot(score_grad, k, 1, 0) * SCALE)
            dk_add = dot(score_grad, q, 0, 0)
            dv_add = dot(prob_b, g, 0, 0)
            if n < length:
                zeros = jnp.zeros((length - n, HD), F32)
                dk_add = jnp.concatenate([dk_add, zeros], 0)
                dv_add = jnp.concatenate([dv_add, zeros], 0)
            dk = dk + dk_add
            dv = dv + dv_add
        dq_all.append(jnp.concatenate(dq_parts, 0))
        mixed_all.append(jnp.concatenate(mixed_parts, 0))
        dk_all.append(dk)
        dv_all.append(dv)
    put(mixed_ref, jnp.concatenate(mixed_all, 1).astype(BF))
    put_grad(0, turn_back(jnp.concatenate(dq_all, 1)).astype(BF))
    put_grad(1, turn_back(jnp.concatenate(dk_all, 1)).astype(BF))
    put_grad(2, jnp.concatenate(dv_all, 1).astype(BF))


def attend(info, side, project, mixed_grad, tables, segs):
    seqs, length = segs.shape
    seqs = seqs // 2
    skip = side * seqs
    wide = project.shape[1]
    rows = seqs * length
    width = wide // 3
    heads = min(2, width // HD)
    lanes = heads * HD
    steps = width // lanes
    block = min(256, length)

    parts = (project, project, project)
    ahead = steps
    if lanes % 128:
        parts = tuple(jnp.split(project, 3, 1))
        ahead = 0

    def of(part):
        return pl.BlockSpec((length, lanes), lambda s, h, _: (s + skip, part * ahead + h))

    table = pl.BlockSpec((1, length, lanes), lambda s, h, _: (s + skip, 0, 0))
    return pl.pallas_call(
        functools.partial(attend_kernel, heads, block),
        grid_spec=pltpu.PrefetchScalarGridSpec(
            num_scalar_prefetch=1,
            grid=(seqs, steps),
            in_specs=[
                of(0),
                of(1),
                of(2),
                of(0),
                table,
                table,
                pl.BlockSpec((1, length, 1), lambda s, h, _: (s + skip, 0, 0)),
                pl.BlockSpec((1, 1, length), lambda s, h, _: (s + skip, 0, 0)),
            ],
            out_specs=[
                pl.BlockSpec((length, lanes), lambda s, h, _: (s, h)),
                pl.BlockSpec((3, length, lanes), lambda s, h, _: (0, s, h)),
            ],
        ),
        out_shape=[
            jax.ShapeDtypeStruct((rows, width), BF),
            jax.ShapeDtypeStruct((3, rows, width), BF),
        ],
        cost_estimate=LIGHT,
        compiler_params=pltpu.CompilerParams(vmem_limit_bytes=56 * 1024 * 1024),
    )(info, *parts, mixed_grad, *tables, segs[:, :, None], segs[:, None, :])


def turn_tables(position, lanes):
    half = ROT // 2
    lane = jnp.arange(lanes) % HD
    freq = 10000.0 ** (-((lane % half).astype(F32) * 2.0) / float(ROT))
    freq = jnp.where(lane < ROT, freq, 0.0)
    phase = position.astype(F32)[..., None] * freq
    return jnp.cos(phase), jnp.sin(phase)


def local(
    tokens,
    segments,
    cotangent,
    mixer_gain,
    mixer_shift,
    mixer_weight,
    mixer_bias,
    merger_weight,
    merger_bias,
    feeder_gain,
    feeder_shift,
    widen_weight,
    widen_bias,
    narrow_weight,
    narrow_bias,
):
    seqs, stretch, width = tokens.shape
    seq = lax.axis_size("seq")
    groups = lax.axis_size("batch") // 2
    members = 2 * seq
    devices = groups * members
    length = stretch * seq
    here = lax.axis_index("seq")
    me = member()
    group = lax.axis_index("batch") // 2
    share = mixer_weight.shape[0]
    hidden = widen_weight.shape[1]
    slim = width // members
    unit = hidden // devices
    mine_h = groups * unit
    block = members * share
    wide = 3 * slim
    turned = here if seq == 2 else jnp.zeros_like(here)
    info = jnp.stack([group, turned]).astype(jnp.int32)

    vectors = (mixer_gain, mixer_shift, mixer_bias, merger_bias, feeder_gain, feeder_shift, widen_bias, narrow_bias)
    sizes = [v.shape[0] for v in vectors]
    cuts = [sum(sizes[: i + 1]) for i in range(len(sizes) - 1)]
    span = wide + mine_h + width
    packed = jnp.concatenate(vectors)
    small = jnp.stack(
        [
            jnp.pad(packed, (0, span - packed.size)),
            jnp.pad(segments.reshape(-1).astype(BF), (0, span - segments.size)),
        ]
    )
    mixer_pieces = mixer_weight.reshape(share, 3, members, slim).transpose(2, 0, 1, 3)
    widen_pieces = widen_weight.reshape(share, groups, members, unit).transpose(2, 0, 1, 3)
    pieces = jnp.concatenate(
        [
            jnp.concatenate(
                [
                    mixer_pieces.reshape(members, share, wide),
                    widen_pieces.reshape(members, share, mine_h),
                    jnp.broadcast_to(merger_weight, (members, share, width)),
                ],
                2,
            ),
            jnp.broadcast_to(small, (members, 2, span)),
        ],
        1,
    )
    got = exchange_members(pieces)
    pad = (-members) % 16
    notes = jnp.pad(got[:, share, : sum(sizes)], ((0, pad), (0, 0)))
    columns = max(wide, sum(sizes))
    notes = jnp.pad(notes, ((0, 0), (0, columns - sum(sizes))))
    mixer_chunk = got[:, :share, :wide].reshape(block, wide)
    widen_chunk = got[:, :share, wide : wide + mine_h].reshape(block, mine_h)
    merger_block = got[:, :share, wide + mine_h :].reshape(block, width)
    segs = got[:, share + 1, : segments.size].astype(jnp.int32).reshape(2, seq, seqs, stretch)
    segs = segs.transpose(0, 2, 1, 3).reshape(2, seqs, length)
    segs = jnp.where(lax.axis_index("batch") % 2 == 0, segs, segs[::-1]).reshape(2 * seqs, length)

    mixer_far = far_groups(jnp.concatenate([mixer_chunk, notes[:, :wide]], 0))
    inputs_own = far_tokens(tokens, got).reshape(-1, width)
    merger = gather_merger(merger_block)
    mixer_near = near_groups(mixer_far)
    widen_far = far_groups(after(widen_chunk, mixer_far))
    inputs = (inputs_own, swap_batch(inputs_own, 1))
    upstream_own = far_tokens(cotangent, inputs_own).reshape(-1, width)
    upstream = (upstream_own, swap_batch(upstream_own, 1))
    widen_near = near_groups(after(widen_far, mixer_near))
    narrow_far = far_groups(after(narrow_weight, widen_far))
    narrow_near = near_groups(after(narrow_far, widen_near))
    widen = (widen_far, widen_near)
    narrow = (narrow_far, narrow_near)

    both = jnp.stack([mixer_far[:, block : block + members], mixer_near[:, block : block + members]], 1)
    gathered = sort_groups(both.reshape(groups, members, -1)[:, :, : sum(sizes)])
    gathered = gathered.reshape(devices, -1).astype(F32)
    gain_m, shift_m, bias_m, bias_o, gain_f, shift_f, bias_w, bias_n = [
        v.reshape(1, -1) for v in jnp.split(gathered, cuts, 1)
    ]
    bias_m_mine = lax.dynamic_index_in_dim(bias_m.reshape(3, members, slim), me, 1).reshape(1, -1)
    bias_w_mine = lax.dynamic_index_in_dim(bias_w.reshape(groups, members, unit), me, 1).reshape(1, -1)
    place = jnp.arange(length, dtype=jnp.int32)
    earlier = jnp.sum((segs[:, None, :] < segs[:, :, None]).astype(jnp.int32), -1)
    tables = turn_tables(place[None, :] - earlier, min(2, slim // HD) * HD)

    first, project, mixed_grad = project_all(
        info, inputs, upstream, gain_m, shift_m, bias_m_mine, merger, mixer_far, mixer_near
    )
    mixed_a, grad_a = attend(info, 0, project, mixed_grad, tables, segs)

    active, slope, n_send, n_keep = feed_widen(
        after(info, mixed_a, narrow_far), inputs, upstream, gain_f, shift_f, bias_w_mine, widen_far, widen_near
    )
    narrow_state = fold_near(n_send, n_keep)

    mixed_b, grad_b = attend(after(info, active), 1, project, mixed_grad, tables, segs)

    partial, error, feed_sums, widen_bias_grad, w_send, w_keep = feed_narrow(
        after(info, mixed_b, narrow_state[2]), inputs, upstream, active, slope, gain_f, shift_f, widen, narrow
    )
    narrow_out = fold_far(narrow_state)
    widen_state = fold_near(after(w_send, narrow_state[2]), w_keep)

    mixed = jnp.concatenate([mixed_a, mixed_b], 0)
    project_grad = jnp.concatenate([grad_a, grad_b], 1)
    partial, merger_grad = merge(info, mixed, upstream, partial, merger)
    error, mixer_sums, mixer_bias_grad, m_send, m_keep = mixer_back(
        after(info, partial), inputs, first, error, project_grad, gain_m, mixer_far, mixer_near
    )
    own = tokens.astype(F32)
    layer_output = part_tokens(near_tokens(partial.reshape(2 * seqs, length, width)))
    mixer_state = fold_near(after(m_send, widen_state[2]), m_keep)
    widen_sum = fold_far(widen_state, narrow_out)
    merger_out = reduce_merger(merger_grad)
    widen_back = exchange_members(widen_sum.reshape(members, share, mine_h).astype(BF))
    widen_out = widen_back.reshape(members, share, groups, unit).transpose(1, 2, 0, 3).astype(F32)
    mixer_sum = fold_far(mixer_state, widen_sum)
    mixer_back_rows = exchange_members(mixer_sum.reshape(members, share, wide).astype(BF))
    mixer_out = mixer_back_rows.reshape(members, share, 3, slim).transpose(1, 2, 0, 3).astype(F32)

    error = part_tokens(near_tokens(error.reshape(2 * seqs, length, width)), layer_output)
    layer_output = (own + layer_output + (bias_o + bias_n)).astype(BF)
    normed, rstd = centre(own)
    back = rstd * (
        error
        - jnp.mean(error, -1, keepdims=True)
        - normed * jnp.mean(error * normed, -1, keepdims=True)
    )
    tokens_grad = (cotangent.astype(F32) + back).astype(BF)

    def spread_out(value, lead):
        shape = (lead, members, value.size // lead)
        return lax.dynamic_update_slice_in_dim(jnp.zeros(shape, F32), value.reshape(lead, 1, -1), me, 1)

    bias_grad = jnp.sum(cotangent.astype(F32), (0, 1))
    sums = (
        mixer_sums[0],
        mixer_sums[1],
        spread_out(mixer_bias_grad, 3),
        bias_grad,
        feed_sums[0],
        feed_sums[1],
        spread_out(widen_bias_grad, groups),
        bias_grad,
    )
    packed = jnp.concatenate([v.reshape(devices, -1) for v in sums], 1).reshape(groups, members, -1)
    relative = sort_groups(packed).reshape(groups // 2, 2, members, -1)
    owned = fold_far(fold_near(relative[:, 1], relative[:, 0]))
    owned = jnp.sum(exchange_members(owned), 0)
    gain_m_out, shift_m_out, bias_m_out, bias_o_out, gain_f_out, shift_f_out, bias_w_out, bias_n_out = jnp.split(owned, cuts)
    return (
        layer_output,
        tokens_grad,
        gain_m_out,
        shift_m_out,
        mixer_out.reshape(mixer_weight.shape),
        bias_m_out,
        merger_out,
        bias_o_out,
        gain_f_out,
        shift_f_out,
        widen_out.reshape(widen_weight.shape),
        bias_w_out,
        narrow_out,
        bias_n_out,
    )


def solution(mesh):
    vector = P(("batch", "seq"))
    matrix = P(("batch", "seq"), None)
    rows = P("batch", "seq", None)
    params = (vector, vector, matrix, vector, matrix, vector, vector, vector, matrix, vector, matrix, vector)
    return jax.shard_map(
        local,
        mesh=mesh,
        in_specs=(rows, P("batch", "seq"), rows) + params,
        out_specs=(rows, rows) + params,
        check_vma=False,
    )
```

time: 515 us -> 502 us (0.975)
  waiting for transfers between devices: 179 us -> 124 us
  local copies, waits for them, and re-layouts: 54.3 us -> 91.3 us
  Pallas kernels: 122 us -> 142 us
  starting transfers between devices: 109 us -> 91.2 us
    ppermute x15 -> x12, waiting for transfers between devices: 38.3 us -> 15 us  [swap_member(): lax.ppermute(value, ('batch', 'seq'), [(i, i // members * members + (i %...]
    concatenate x43, local copies, waits for them, and re-layouts: 11.6 us -> 33.8 us  [local(): jnp.concatenate([v.reshape(devices, -1) for v in sums], 1)]
    ppermute x5 -> x4, waiting for transfers between devices: 20 us -> 0.42 us  [swap_seq(): return lax.ppermute(value, 'seq', [(i, i ^ mask) for i in range(count)])]
    dynamic_update_slice x17 -> x14, local copies, waits for them, and re-layouts: 9.14 us -> 26.5 us  [exchange_members(): out = lax.dynamic_update_slice_in_dim(out, got, me ^ k, 0)]
    pallas_call x4 -> x5, Pallas kernels: 80.2 us -> 96 us  [call(): pl.pallas_call(kernel, grid_spec=pltpu.PrefetchScalarGridSpec(num_scalar_...]
    ppermute x47 -> x34, starting transfers between devices: 75 us -> 63.2 us  [swap_batch(): return lax.ppermute(value, 'batch', [(i, i ^ mask) for i in range(count)])]
    ppermute x3, waiting for transfers between devices: 6.03 us -> 0.01 us  [gather_merger(): found = found + lax.ppermute(block, every, pairs)]
    concatenate x5 -> x2, local copies, waits for them, and re-layouts: 5.46 us -> 0.12 us  [the longest x1 0.11 us: local(): packed = jnp.concatenate(vectors)]
  transfers between devices with their start and end apart: 79 -> 59, of which waited for: 34 -> 20; matrix products, arithmetic and copies ran while one was open for 17% -> 23% of each run, Pallas kernels for 9% -> 9%
where the time goes in v3:
time: 502 us; the launch traced here: 494 us
  Pallas kernels  142 us (28%)
  waiting for transfers between devices  124 us (25%)
  local copies, waits for them, and re-layouts  91.3 us (18%)
  starting transfers between devices  91.2 us (18%)
  other arithmetic  44.1 us (9%)
    ppermute x34, waiting for transfers between devices, swap_batch(): return lax.ppermute(value, 'batch', [(i, i ^ mask) for i in range(count)])  102 us
    pallas_call x5, Pallas kernels, call(): pl.pallas_call(kernel, grid_spec=pltpu.PrefetchScalarGridSpec(num_scalar_...  96 us
    ppermute x34, starting transfers between devices, swap_batch(): return lax.ppermute(value, 'batch', [(i, i ^ mask) for i in range(count)])  63.2 us
    pallas_call x2, Pallas kernels, attend(): pl.pallas_call(functools.partial(attend_kernel, heads, block), grid_spec=...  45.8 us
    concatenate x43, local copies, waits for them, and re-layouts, local(): jnp.concatenate([v.reshape(devices, -1) for v in sums], 1)  33.8 us
    dynamic_update_slice x14, local copies, waits for them, and re-layouts, exchange_members(): out = lax.dynamic_update_slice_in_dim(out, got, me ^ k, 0)  26.5 us
    ppermute x12, waiting for transfers between devices, swap_member(): lax.ppermute(value, ('batch', 'seq'), [(i, i // members * members + (i %...  15 us
  transfers between devices with their start and end apart: 59, of which 20 were waited for; matrix products, arithmetic and copies ran while one was open for 23% of the time, Pallas kernels for 9%

profile of v3, /device:TPU:0, one launch (start us, length us, event | category | flops | bytes accessed | tf_op | source)
XLA Modules:
  0.0 494.5 jit_solution(17304370565962699036)
XLA Ops:
  9.4 5.5 %dynamic_update_slice.54 = bf16[4,34,2816]{2,0,1:T(4,128)(2,1)S(1)} dynamic-update-slice(bf16[4,34,2816]{2,0,1:T(4,128)(2,1)S(1)} %broadcast_in_dim.45, bf16[1,34,2816]{2,0,1:T(2,128)(2,1)S(1)} %get-tuple-element.125, s32[]{:T(128)S(6)} %select_n.280, s32[]{:T(128)} %constant.172.clone.1, s32[]{:T(128)} %constant.172.clone.1) | dynamic-update-slice | bytes 382980 | tf_op jit(solution)/shard_map/dynamic_update_slice | solution.py:95
  18.8 7.3 %dynamic_update_slice.55 = bf16[4,34,2816]{2,0,1:T(4,128)(2,1)S(1)} dynamic-update-slice(bf16[4,34,2816]{2,0,1:T(4,128)(2,1)S(1)} %dynamic_update_slice.54, bf16[1,34,2816]{2,0,1:T(2,128)(2,1)} %collective-permute-done, s32[]{:T(128)S(6)} %select_n.281, s32[]{:T(128)} %constant.172.clone.1, s32[]{:T(128)} %constant.172.clone.1) | dynamic-update-slice | bytes 382980 | tf_op jit(solution)/shard_map/dynamic_update_slice | solution.py:95
  26.2 5.5 %dynamic_update_slice.56 = bf16[4,34,2816]{2,0,1:T(4,128)(2,1)S(1)} dynamic-update-slice(bf16[4,34,2816]{2,0,1:T(4,128)(2,1)S(1)} %dynamic_update_slice.55, bf16[1,34,2816]{2,0,1:T(2,128)(2,1)S(1)} %collective-permute-done.1, s32[]{:T(128)S(6)} %select_n.282, s32[]{:T(128)} %constant.172.clone.1, s32[]{:T(128)} %constant.172.clone.1) | dynamic-update-slice | bytes 382980 | tf_op jit(solution)/shard_map/dynamic_update_slice | solution.py:95
  31.8 5.5 %dynamic_update_slice.57 = bf16[4,34,2816]{2,0,1:T(4,128)(2,1)S(1)} dynamic-update-slice(bf16[4,34,2816]{2,0,1:T(4,128)(2,1)S(1)} %dynamic_update_slice.56, bf16[1,34,2816]{2,0,1:T(2,128)(2,1)S(1)} %collective-permute-done.2, s32[]{:T(128)S(6)} %select_n.283, s32[]{:T(128)} %constant.172.clone.1, s32[]{:T(128)} %constant.172.clone.1) | dynamic-update-slice | bytes 382980 | tf_op jit(solution)/shard_map/dynamic_update_slice | solution.py:95
  47.6 7.2 %collective-permute-done.8 = bf16[144,768]{1,0:T(8,128)(2,1)S(1)} collective-permute-done((bf16[144,768]{1,0:T(8,128)(2,1)S(1)}, bf16[144,768]{1,0:T(8,128)(2,1)S(1)}, u32[]{:S(2)}, u32[]{:S(2)}) %collective-permute-start.8) | collective-permute-done | bytes 221216 | tf_op jit(solution)/shard_map/ppermute | solution.py:26
  56.2 3.8 collective-permute-start.13
  60.1 5.5 %multiply_sine_fusion = (f32[2,1024,128]{2,1,0:T(8,128)}, f32[2,1024,128]{2,1,0:T(8,128)}) fusion(f32[128]{0:T(128)S(1)} %compare_select_fusion.2, f32[2,1024]{1,0:T(2,128)S(1)} %subtract_convert_fusion), kind=kLoop, calls=%fused_computation.28 | loop fusion | flops 262144 | bytes 2105856 | tf_op jit(solution)/shard_map/sin | solution.py:598
  67.3 4.6 collective-permute-start.16
  81.8 9.8 %collective-permute-done.17 = bf16[128,1024]{1,0:T(8,128)(2,1)} collective-permute-done((bf16[128,1024]{1,0:T(8,128)(2,1)S(1)}, bf16[128,1024]{1,0:T(8,128)(2,1)}, u32[]{:S(2)}, u32[]{:S(2)}) %collective-permute-start.17) | collective-permute-done | bytes 262176 | tf_op jit(solution)/shard_map/ppermute | solution.py:26
  93.7 5.2 %collective-permute-start.18 = (bf16[128,1024]{1,0:T(8,128)(2,1)S(1)}, bf16[128,1024]{1,0:T(8,128)(2,1)S(1)}, u32[]{:S(2)}, u32[]{:S(2)}) collective-permute-start(bf16[128,1024]{1,0:T(8,128)(2,1)S(1)} %copy-done.18), channel_id=1, source_target_pairs={{0,8},{2,10},{4,12},{6,14},{8,0},{10,2},{12,4},{14,6},{16,24},{18,... | collective-permute-start | bytes 786440 | tf_op jit(solution)/shard_map/ppermute | solution.py:26
  105.0 5.7 %collective-permute-done.18 = bf16[128,1024]{1,0:T(8,128)(2,1)S(1)} collective-permute-done((bf16[128,1024]{1,0:T(8,128)(2,1)S(1)}, bf16[128,1024]{1,0:T(8,128)(2,1)S(1)}, u32[]{:S(2)}, u32[]{:S(2)}) %collective-permute-start.18) | collective-permute-done | bytes 262176 | tf_op jit(solution)/shard_map/ppermute | solution.py:26
  110.7 9.6 %collective-permute-done.19 = bf16[128,1024]{1,0:T(8,128)(2,1)S(1)} collective-permute-done((bf16[128,1024]{1,0:T(8,128)(2,1)S(1)}, bf16[128,1024]{1,0:T(8,128)(2,1)S(1)}, u32[]{:S(2)}, u32[]{:S(2)}) %collective-permute-start.19) | collective-permute-done | bytes 262176 | tf_op jit(solution)/shard_map/ppermute | solution.py:26
  130.0 17.3 %collective-permute-done.21.near_ref.refs_1_ = bf16[4,128,1024]{2,1,0:T(8,128)(2,1)} collective-permute-done((bf16[4,128,1024]{2,1,0:T(8,128)(2,1)}, bf16[4,128,1024]{2,1,0:T(8,128)(2,1)}, u32[]{:S(2)}, u32[]{:S(2)}) %collective-permute-start.21) | collective-permute-done | bytes 1048608 | tf_op jit(solution)/shard_map/ppermute | solution.py:26
  147.3 12.9 %shard_map.254 = (bf16[2048,1024]{1,0:T(8,128)(2,1)}, f32[2048,768]{1,0:T(8,128)}, bf16[2048,256]{1,0:T(8,128)(2,1)}) custom-call(s32[2]{0:T(128)} %pad_add_fusion.info, bf16[1024,1024]{1,0:T(8,128)(2,1)} %maximum_bitcast_fusion.xo_ref, bf16[1024,1024]{1,0:T(8,128)(2,1)} %collective-permute-done.4.xp_ref, bf16[1024,1024]{1,0:T(8,128)(2,1)} %copy-done, ...), custom_call_target="tpu_custom_call" | custom-call | flops 1000 | bytes 1000 | tf_op jit(solution)/shard_map/pallas_call | solution.py:303
  160.2 23.1 %shard_map.255 = (bf16[1024,256]{1,0:T(8,128)(2,1)}, bf16[3,1024,256]{2,1,0:T(8,128)(2,1)}) custom-call(s32[2]{0:T(128)} %pad_add_fusion.info, f32[2048,768]{1,0:T(8,128)} %get-tuple-element.59.q_ref.k_ref.v_ref, f32[2048,768]{1,0:T(8,128)} %get-tuple-element.59.q_ref.k_ref.v_ref, f32[2048,768]{1,0:T(8,128)} %get-tuple-element.59.q_ref.k_ref.v_ref, ...), custom_call_target="tpu_custom_call" | custom-call | flops 1000 | bytes 1000 | tf_op jit(solution)/shard_map/pallas_call | solution.py:563
  183.3 21.7 %shard_map.256 = (bf16[2048,1024]{1,0:T(8,128)(2,1)}, bf16[2048,1024]{1,0:T(8,128)(2,1)}, bf16[4,128,1024]{2,1,0:T(8,128)(2,1)}, bf16[4,128,1024]{2,1,0:T(8,128)(2,1)}) custom-call(s32[2]{0:T(128)} %pad_add_fusion.info, bf16[1024,1024]{1,0:T(8,128)(2,1)} %maximum_bitcast_fusion.xo_ref, bf16[1024,1024]{1,0:T(8,128)(2,1)} %collective-permute-done.4.xp_ref, ...), custom_call_target="tpu_custom_call" | custom-call | flops 1000 | bytes 1000 | tf_op jit(solution)/shard_map/pallas_call | solution.py:303
  208.5 22.7 %shard_map.257 = (bf16[1024,256]{1,0:T(8,128)(2,1)}, bf16[3,1024,256]{2,1,0:T(8,128)(2,1)}) custom-call(s32[2]{0:T(128)} %pad_add_fusion.info, f32[2048,768]{1,0:T(8,128)} %get-tuple-element.59.q_ref.k_ref.v_ref, f32[2048,768]{1,0:T(8,128)} %get-tuple-element.59.q_ref.k_ref.v_ref, f32[2048,768]{1,0:T(8,128)} %get-tuple-element.59.q_ref.k_ref.v_ref, ...), custom_call_target="tpu_custom_call" | custom-call | flops 1000 | bytes 1000 | tf_op jit(solution)/shard_map/pallas_call | solution.py:563
  236.7 15.8 %collective-permute-done.23.refs_3_ = bf16[4,128,1024]{2,1,0:T(8,128)(2,1)S(1)} collective-permute-done((bf16[4,128,1024]{2,1,0:T(8,128)(2,1)S(1)}, bf16[4,128,1024]{2,1,0:T(8,128)(2,1)S(1)}, u32[]{:S(2)}, u32[]{:S(2)}) %collective-permute-start.23) | collective-permute-done | bytes 1048608 | tf_op jit(solution)/shard_map/ppermute | solution.py:26
  253.5 32.5 %shard_map.258 = (bf16[2048,1024]{1,0:T(8,128)(2,1)}, bf16[2048,1024]{1,0:T(8,128)(2,1)}, f32[2,1024]{1,0:T(2,128)}, f32[1,1024]{1,0:T(1,128)}, bf16[4,128,1024]...) custom-call(s32[2]{0:T(128)} %pad_add_fusion.info, bf16[1024,1024]{1,0:T(8,128)(2,1)} %maximum_bitcast_fusion.xo_ref, ...), custom_call_target="tpu_custom_call" | custom-call | flops 1000 | bytes 1000 | tf_op jit(solution)/shard_map/pallas_call | solution.py:303
  286.0 9.0 %shard_map.259 = (bf16[2048,1024]{1,0:T(8,128)(2,1)}, f32[256,1024]{1,0:T(8,128)}) custom-call(s32[2]{0:T(128)} %pad_add_fusion.info, bf16[2048,256]{1,0:T(8,128)(2,1)} %pad_maximum_fusion.3.m_ref, bf16[1024,1024]{1,0:T(8,128)(2,1)} %copy-done, bf16[1024,1024]{1,0:T(8,128)(2,1)} %collective-permute-done.6.gp_ref, ...), custom_call_target="tpu_custom_call" | custom-call | flops 1000 | bytes 1000 | tf_op jit(solution)/shard_map/pallas_call | solution.py:303
  300.3 4.9 collective-permute-start.37
  310.2 19.9 %shard_map.260 = (bf16[2048,1024]{1,0:T(8,128)(2,1)}, f32[2,1024]{1,0:T(2,128)}, f32[1,768]{1,0:T(1,128)}, bf16[4,128,768]{2,1,0:T(8,128)(2,1)}, bf16[4,128,768]{2,1,0:T(8,128)(2,1)}) custom-call(s32[2]{0:T(128)} %pad_add_fusion.info, bf16[1024,1024]{1,0:T(8,128)(2,1)} %maximum_bitcast_fusion.xo_ref, bf16[1024,1024]{1,0:T(8,128)(2,1)} %collective-permute-done.4.xp_ref, ...), custom_call_target="tpu_custom_call" | custom-call | flops 1000 | bytes 1000 | tf_op jit(solution)/shard_map/pallas_call | solution.py:303
  377.8 6.3 %collective-permute-done.50 = bf16[128,1024]{1,0:T(8,128)(2,1)S(1)} collective-permute-done((bf16[128,1024]{1,0:T(8,128)(2,1)S(1)}, bf16[128,1024]{1,0:T(8,128)(2,1)S(1)}, u32[]{:S(2)}, u32[]{:S(2)}) %collective-permute-start.50) | collective-permute-done | bytes 262176 | tf_op jit(solution)/shard_map/ppermute | solution.py:167
  384.1 4.4 collective-permute-start.42
  388.7 3.9 collective-permute-done.40
  393.9 9.8 %collective-permute-done.41 = bf16[128,1024]{1,0:T(8,128)(2,1)S(1)} collective-permute-done((bf16[128,1024]{1,0:T(8,128)(2,1)S(1)}, bf16[128,1024]{1,0:T(8,128)(2,1)S(1)}, u32[]{:S(2)}, u32[]{:S(2)}) %collective-permute-start.41) | collective-permute-done | bytes 262176 | tf_op jit(solution)/shard_map/ppermute | solution.py:26
  417.0 4.3 collective-permute-done.36
  421.5 5.6 %collective-permute-start.43 = (bf16[128,768]{1,0:T(8,128)(2,1)S(1)}, bf16[128,768]{1,0:T(8,128)(2,1)S(1)}, u32[]{:S(2)}, u32[]{:S(2)}) collective-permute-start(bf16[128,768]{1,0:T(8,128)(2,1)S(1)} %get-tuple-element.96), channel_id=1, source_target_pairs={{0,8},{2,10},{4,12},{6,14},{8,0},{10,2},{12,4},{14,6},{16,24},{18,... | collective-permute-start | bytes 589832 | tf_op jit(solution)/shard_map/ppermute | solution.py:26
  436.1 7.5 %collective-permute-done.44 = bf16[128,768]{1,0:T(8,128)(2,1)S(1)} collective-permute-done((bf16[128,768]{1,0:T(8,128)(2,1)S(1)}, bf16[128,768]{1,0:T(8,128)(2,1)S(1)}, u32[]{:S(2)}, u32[]{:S(2)}) %collective-permute-start.44) | collective-permute-done | bytes 196640 | tf_op jit(solution)/shard_map/ppermute | solution.py:26
  449.8 9.3 %collective-permute-done.46 = bf16[1,32,768]{2,1,0:T(8,128)(2,1)} collective-permute-done((bf16[1,32,768]{2,1,0:T(8,128)(2,1)S(1)}, bf16[1,32,768]{2,1,0:T(8,128)(2,1)}, u32[]{:S(2)}, u32[]{:S(2)}) %collective-permute-start.46) | collective-permute-done | bytes 49184 | tf_op jit(solution)/shard_map/ppermute | solution.py:37
  472.6 4.7 collective-permute-start.29
  477.3 5.1 %collective-permute-start.30 = (f32[4,416]{1,0:T(4,128)S(1)}, f32[4,416]{1,0:T(4,128)S(1)}, u32[]{:S(2)}, u32[]{:S(2)}) collective-permute-start(f32[4,416]{1,0:T(4,128)S(1)} %get-tuple-element.158), channel_id=1, source_target_pairs={{0,16},{2,18},{4,20},{6,22},{8,24},{10,26},{12,28},{14,30},{16,0},... | collective-permute-start | bytes 19976 | tf_op jit(solution)/shard_map/ppermute | solution.py:26
  (382 shorter events, 176.2 us)
Async XLA Ops:
  9.0 17.2 %collective-permute-start.1 = (bf16[1,34,2816]{2,0,1:T(2,128)(2,1)S(1)}, bf16[1,34,2816]{2,0,1:T(2,128)(2,1)S(1)}, u32[]{:S(2)}, u32[]{:S(2)}) collective-permute-start(bf16[1,34,2816]{2,0,1:T(2,128)(2,1)S(1)} %get-tuple-element.123), channel_id=1, source_target_pairs={{0,2},{1,3},{2,0},{3,1},{4,6},{5,7},{6,4},{7,5},{8,10},{9,11},{10,... | collective-permute-start | bytes 574472 | tf_op jit(solution)/shard_map/ppermute | solution.py:37
  9.0 22.7 %collective-permute-start.2 = (bf16[1,34,2816]{2,0,1:T(2,128)(2,1)S(1)}, bf16[1,34,2816]{2,0,1:T(2,128)(2,1)S(1)}, u32[]{:S(2)}, u32[]{:S(2)}) collective-permute-start(bf16[1,34,2816]{2,0,1:T(2,128)(2,1)S(1)} %get-tuple-element.122), channel_id=1, source_target_pairs={{0,3},{1,2},{2,1},{3,0},{4,7},{5,6},{6,5},{7,4},{8,11},{9,10},{10,... | collective-permute-start | bytes 574472 | tf_op jit(solution)/shard_map/ppermute | solution.py:37
  37.4 17.3 %collective-permute-start.8 = (bf16[144,768]{1,0:T(8,128)(2,1)S(1)}, bf16[144,768]{1,0:T(8,128)(2,1)S(1)}, u32[]{:S(2)}, u32[]{:S(2)}) collective-permute-start(bf16[144,768]{1,0:T(8,128)(2,1)S(1)} %get-tuple-element.134), channel_id=1, source_target_pairs={{0,16},{2,18},{4,20},{6,22},{8,24},{10,26},{12,28},{14,30},{16,0},... | collective-permute-start | bytes 663560 | tf_op jit(solution)/shard_map/ppermute | solution.py:26
  42.0 23.7 %collective-permute-start.7 = (bf16[144,768]{1,0:T(8,128)(2,1)S(1)}, bf16[144,768]{1,0:T(8,128)(2,1)}, u32[]{:S(2)}, u32[]{:S(2)}) collective-permute-start(bf16[144,768]{1,0:T(8,128)(2,1)S(1)} %get-tuple-element.134), channel_id=1, source_target_pairs={{0,8},{2,10},{4,12},{6,14},{8,0},{10,2},{12,4},{14,6},{16,24},{18,... | collective-permute-start | bytes 663560 | tf_op jit(solution)/shard_map/ppermute | solution.py:26
  42.5 24.8 %collective-permute-start.11 = (bf16[128,1024]{1,0:T(8,128)(2,1)S(1)}, bf16[128,1024]{1,0:T(8,128)(2,1)S(1)}, u32[]{:S(2)}, u32[]{:S(2)}) collective-permute-start(bf16[128,1024]{1,0:T(8,128)(2,1)S(1)} %bitcast.230), channel_id=1, source_target_pairs={{0,8},{4,12},{9,1},{13,5},{18,26},{22,30},{27,19},{31,23}} | collective-permute-start | bytes 786440 | tf_op jit(solution)/shard_map/ppermute | solution.py:113
  46.3 28.7 %collective-permute-start.3 = (bf16[1,512,1024]{2,1,0:T(8,128)(2,1)S(1)}, bf16[1,512,1024]{2,1,0:T(8,128)(2,1)}, u32[]{:S(2)}, u32[]{:S(2)}) collective-permute-start(bf16[1,512,1024]{2,1,0:T(8,128)(2,1)S(1)} %copy-done.1), channel_id=1, source_target_pairs={{0,1},{1,0},{2,3},{3,2},{4,5},{5,4},{6,7},{7,6},{8,9},{9,8},{10,11... | collective-permute-start | bytes 3145736 | tf_op jit(solution)/shard_map/ppermute | solution.py:31
  71.9 19.6 %collective-permute-start.17 = (bf16[128,1024]{1,0:T(8,128)(2,1)S(1)}, bf16[128,1024]{1,0:T(8,128)(2,1)}, u32[]{:S(2)}, u32[]{:S(2)}) collective-permute-start(bf16[128,1024]{1,0:T(8,128)(2,1)S(1)} %bitcast.241), channel_id=1, source_target_pairs={{0,24},{2,26},{4,28},{6,30},{8,16},{10,18},{12,20},{14,22},{16,8},... | collective-permute-start | bytes 786440 | tf_op jit(solution)/shard_map/ppermute | solution.py:26
  73.3 48.1 %collective-permute-start.10 = (bf16[4,144,768]{2,1,0:T(8,128)(2,1)S(1)}, bf16[4,144,768]{2,1,0:T(8,128)(2,1)}, u32[]{:S(2)}, u32[]{:S(2)}) collective-permute-start(bf16[4,144,768]{2,1,0:T(8,128)(2,1)S(1)} %pad_maximum_fusion.4.far_ref), channel_id=1, source_target_pairs={{0,4},{2,6},{4,0},{6,2},{8,12},{10,14},{12,8},{14,10},{16,20},{18,... | collective-permute-start | bytes 2654216 | tf_op jit(solution)/shard_map/ppermute | solution.py:26
  74.9 26.1 %collective-permute-start.14 = (bf16[1,128,1024]{2,1,0:T(8,128)(2,1)S(1)}, bf16[1,128,1024]{2,1,0:T(8,128)(2,1)}, u32[]{:S(2)}, u32[]{:S(2)}) collective-permute-start(bf16[1,128,1024]{2,1,0:T(8,128)(2,1)S(1)} %add_bitcast_fusion), channel_id=1, source_target_pairs={{0,4},{2,6},{4,0},{6,2},{8,12},{10,14},{12,8},{14,10},{16,20},{18,... | collective-permute-start | bytes 786440 | tf_op jit(solution)/shard_map/ppermute | solution.py:26
  79.7 44.1 %collective-permute-start.5 = (bf16[1,512,1024]{2,1,0:T(8,128)(2,1)S(1)}, bf16[1,512,1024]{2,1,0:T(8,128)(2,1)}, u32[]{:S(2)}, u32[]{:S(2)}) collective-permute-start(bf16[1,512,1024]{2,1,0:T(8,128)(2,1)S(1)} %copy-done.8), channel_id=1, source_target_pairs={{0,1},{1,0},{2,3},{3,2},{4,5},{5,4},{6,7},{7,6},{8,9},{9,8},{10,11... | collective-permute-start | bytes 3145736 | tf_op jit(solution)/shard_map/ppermute | solution.py:31
  98.9 21.4 %collective-permute-start.19 = (bf16[128,1024]{1,0:T(8,128)(2,1)S(1)}, bf16[128,1024]{1,0:T(8,128)(2,1)S(1)}, u32[]{:S(2)}, u32[]{:S(2)}) collective-permute-start(bf16[128,1024]{1,0:T(8,128)(2,1)S(1)} %copy-done.18), channel_id=1, source_target_pairs={{0,16},{2,18},{4,20},{6,22},{8,24},{10,26},{12,28},{14,30},{16,0},... | collective-permute-start | bytes 786440 | tf_op jit(solution)/shard_map/ppermute | solution.py:26
  101.0 19.3 %collective-permute-start.20 = (bf16[128,1024]{1,0:T(8,128)(2,1)S(1)}, bf16[128,1024]{1,0:T(8,128)(2,1)S(1)}, u32[]{:S(2)}, u32[]{:S(2)}) collective-permute-start(bf16[128,1024]{1,0:T(8,128)(2,1)S(1)} %copy-done.18), channel_id=1, source_target_pairs={{0,24},{2,26},{4,28},{6,30},{8,16},{10,18},{12,20},{14,22},{16,8},... | collective-permute-start | bytes 786440 | tf_op jit(solution)/shard_map/ppermute | solution.py:26
  121.4 25.9 %collective-permute-start.4 = (bf16[1024,1024]{1,0:T(8,128)(2,1)}, bf16[1024,1024]{1,0:T(8,128)(2,1)}, u32[]{:S(2)}, u32[]{:S(2)}) collective-permute-start(bf16[1024,1024]{1,0:T(8,128)(2,1)} %maximum_bitcast_fusion.xo_ref), channel_id=1, source_target_pairs={{0,2},{2,0},{4,6},{6,4},{8,10},{10,8},{12,14},{14,12},{16,18},{18,... | collective-permute-start | bytes 6291464 | tf_op jit(solution)/shard_map/ppermute | solution.py:26
  121.4 25.9 %collective-permute-start.21 = (bf16[4,128,1024]{2,1,0:T(8,128)(2,1)}, bf16[4,128,1024]{2,1,0:T(8,128)(2,1)}, u32[]{:S(2)}, u32[]{:S(2)}) collective-permute-start(bf16[4,128,1024]{2,1,0:T(8,128)(2,1)} %pad_maximum_fusion.1.far_ref.refs_0_), channel_id=1, source_target_pairs={{0,4},{2,6},{4,0},{6,2},{8,12},{10,14},{12,8},{14,10},{16,20},{18,... | collective-permute-start | bytes 3145736 | tf_op jit(solution)/shard_map/ppermute | solution.py:26
  125.1 22.1 %collective-permute-start.6 = (bf16[1024,1024]{1,0:T(8,128)(2,1)S(1)}, bf16[1024,1024]{1,0:T(8,128)(2,1)}, u32[]{:S(2)}, u32[]{:S(2)}) collective-permute-start(bf16[1024,1024]{1,0:T(8,128)(2,1)S(1)} %maximum_bitcast_fusion.1.go_ref), channel_id=1, source_target_pairs={{0,2},{2,0},{4,6},{6,4},{8,10},{10,8},{12,14},{14,12},{16,18},{18,... | collective-permute-start | bytes 6291464 | tf_op jit(solution)/shard_map/ppermute | solution.py:26
  205.0 31.7 %collective-permute-start.22 = (bf16[4,128,1024]{2,1,0:T(8,128)(2,1)}, bf16[4,128,1024]{2,1,0:T(8,128)(2,1)}, u32[]{:S(2)}, u32[]{:S(2)}) collective-permute-start(bf16[4,128,1024]{2,1,0:T(8,128)(2,1)} %get-tuple-element.69), channel_id=1, source_target_pairs={{0,4},{2,6},{4,0},{6,2},{8,12},{10,14},{12,8},{14,10},{16,20},{18,... | collective-permute-start | bytes 3145736 | tf_op jit(solution)/shard_map/ppermute | solution.py:26
  206.6 46.0 %collective-permute-start.23 = (bf16[4,128,1024]{2,1,0:T(8,128)(2,1)S(1)}, bf16[4,128,1024]{2,1,0:T(8,128)(2,1)S(1)}, u32[]{:S(2)}, u32[]{:S(2)}) collective-permute-start(bf16[4,128,1024]{2,1,0:T(8,128)(2,1)S(1)} %copy-done.5), channel_id=1, source_target_pairs={{0,4},{2,6},{4,0},{6,2},{8,12},{10,14},{12,8},{14,10},{16,20},{18,... | collective-permute-start | bytes 3145736 | tf_op jit(solution)/shard_map/ppermute | solution.py:26
  300.3 69.5 %collective-permute-start.37 = (bf16[128,1024]{1,0:T(8,128)(2,1)}, bf16[128,1024]{1,0:T(8,128)(2,1)}, u32[]{:S(2)}, u32[]{:S(2)}) collective-permute-start(bf16[128,1024]{1,0:T(8,128)(2,1)} %get-tuple-element.111), channel_id=1, source_target_pairs={{0,8},{2,10},{4,12},{6,14},{8,0},{10,2},{12,4},{14,6},{16,24},{18,... | collective-permute-start | bytes 786440 | tf_op jit(solution)/shard_map/ppermute | solution.py:26
  305.2 66.2 %collective-permute-start.38 = (bf16[128,1024]{1,0:T(8,128)(2,1)}, bf16[128,1024]{1,0:T(8,128)(2,1)}, u32[]{:S(2)}, u32[]{:S(2)}) collective-permute-start(bf16[128,1024]{1,0:T(8,128)(2,1)} %get-tuple-element.113), channel_id=1, source_target_pairs={{0,16},{2,18},{4,20},{6,22},{8,24},{10,26},{12,28},{14,30},{16,0},... | collective-permute-start | bytes 786440 | tf_op jit(solution)/shard_map/ppermute | solution.py:26
  307.1 69.2 %collective-permute-start.35 = (bf16[4,128,1024]{2,1,0:T(8,128)(2,1)}, bf16[4,128,1024]{2,1,0:T(8,128)(2,1)}, u32[]{:S(2)}, u32[]{:S(2)}) collective-permute-start(bf16[4,128,1024]{2,1,0:T(8,128)(2,1)} %get-tuple-element.89), channel_id=1, source_target_pairs={{0,4},{2,6},{4,0},{6,2},{8,12},{10,14},{12,8},{14,10},{16,20},{18,... | collective-permute-start | bytes 3145736 | tf_op jit(solution)/shard_map/ppermute | solution.py:26
  309.7 26.8 %collective-permute-start.49 = (bf16[1,128,1024]{2,1,0:T(8,128)(2,1)S(1)}, bf16[1,128,1024]{2,1,0:T(8,128)(2,1)S(1)}, u32[]{:S(2)}, u32[]{:S(2)}) collective-permute-start(bf16[1,128,1024]{2,1,0:T(8,128)(2,1)S(1)} %fusion.29), channel_id=1, source_target_pairs={{0,4},{2,6},{4,0},{6,2},{8,12},{10,14},{12,8},{14,10},{16,20},{18,... | collective-permute-start | bytes 786440 | tf_op jit(solution)/shard_map/ppermute | solution.py:26
  310.2 97.3 %collective-permute-start.24 = (bf16[1,1024,1024]{2,1,0:T(8,128)(2,1)}, bf16[1,1024,1024]{2,1,0:T(8,128)(2,1)}, u32[]{:S(2)}, u32[]{:S(2)}) collective-permute-start(bf16[1,1024,1024]{2,1,0:T(8,128)(2,1)} %slice_bitcast_fusion.1), channel_id=1, source_target_pairs={{0,2},{2,0},{4,6},{6,4},{8,10},{10,8},{12,14},{14,12},{16,18},{18,... | collective-permute-start | bytes 6291464 | tf_op jit(solution)/shard_map/ppermute | solution.py:26
  336.5 36.2 %collective-permute-start.39 = (bf16[128,1024]{1,0:T(8,128)(2,1)}, bf16[128,1024]{1,0:T(8,128)(2,1)}, u32[]{:S(2)}, u32[]{:S(2)}) collective-permute-start(bf16[128,1024]{1,0:T(8,128)(2,1)} %get-tuple-element.112), channel_id=1, source_target_pairs={{0,24},{2,26},{4,28},{6,30},{8,16},{10,18},{12,20},{14,22},{16,8},... | collective-permute-start | bytes 786440 | tf_op jit(solution)/shard_map/ppermute | solution.py:26
  376.3 52.8 %collective-permute-start.26 = (bf16[1,1024,1024]{2,1,0:T(8,128)(2,1)S(1)}, bf16[1,1024,1024]{2,1,0:T(8,128)(2,1)S(1)}, u32[]{:S(2)}, u32[]{:S(2)}) collective-permute-start(bf16[1,1024,1024]{2,1,0:T(8,128)(2,1)S(1)} %slice_bitcast_fusion), channel_id=1, source_target_pairs={{0,2},{2,0},{4,6},{6,4},{8,10},{10,8},{12,14},{14,12},{16,18},{18,... | collective-permute-start | bytes 6291464 | tf_op jit(solution)/shard_map/ppermute | solution.py:26
  384.1 19.6 %collective-permute-start.41 = (bf16[128,1024]{1,0:T(8,128)(2,1)S(1)}, bf16[128,1024]{1,0:T(8,128)(2,1)S(1)}, u32[]{:S(2)}, u32[]{:S(2)}) collective-permute-start(bf16[128,1024]{1,0:T(8,128)(2,1)S(1)} %get-tuple-element.94), channel_id=1, source_target_pairs={{0,16},{2,18},{4,20},{6,22},{8,24},{10,26},{12,28},{14,30},{16,0},... | collective-permute-start | bytes 786440 | tf_op jit(solution)/shard_map/ppermute | solution.py:26
  384.1 20.9 %collective-permute-start.42 = (bf16[128,1024]{1,0:T(8,128)(2,1)S(1)}, bf16[128,1024]{1,0:T(8,128)(2,1)S(1)}, u32[]{:S(2)}, u32[]{:S(2)}) collective-permute-start(bf16[128,1024]{1,0:T(8,128)(2,1)S(1)} %get-tuple-element.95), channel_id=1, source_target_pairs={{0,24},{2,26},{4,28},{6,30},{8,16},{10,18},{12,20},{14,22},{16,8},... | collective-permute-start | bytes 786440 | tf_op jit(solution)/shard_map/ppermute | solution.py:26
  392.6 19.2 %collective-permute-start.53 = (bf16[32,1024]{1,0:T(8,128)(2,1)S(1)}, bf16[32,1024]{1,0:T(8,128)(2,1)S(1)}, u32[]{:S(2)}, u32[]{:S(2)}) collective-permute-start(bf16[32,1024]{1,0:T(8,128)(2,1)S(1)} %get-tuple-element.130), channel_id=1, source_target_pairs={{0,1},{4,5},{9,8},{13,12},{18,19},{22,23},{27,26},{31,30}} | collective-permute-start | bytes 196616 | tf_op jit(solution)/shard_map/ppermute | solution.py:176
  412.0 21.2 %collective-permute-start.25 = (bf16[1,512,1024]{2,1,0:T(8,128)(2,1)S(1)}, bf16[1,512,1024]{2,1,0:T(8,128)(2,1)S(1)}, u32[]{:S(2)}, u32[]{:S(2)}) collective-permute-start(bf16[1,512,1024]{2,1,0:T(8,128)(2,1)S(1)} %slice.391), channel_id=1, source_target_pairs={{0,1},{1,0},{2,3},{3,2},{4,5},{5,4},{6,7},{7,6},{8,9},{9,8},{10,11... | collective-permute-start | bytes 3145736 | tf_op jit(solution)/shard_map/ppermute | solution.py:31
  417.0 19.0 %collective-permute-start.58 = (bf16[1,32,1024]{2,1,0:T(8,128)(2,1)S(1)}, bf16[1,32,1024]{2,1,0:T(8,128)(2,1)S(1)}, u32[]{:S(2)}, u32[]{:S(2)}) collective-permute-start(bf16[1,32,1024]{2,1,0:T(8,128)(2,1)S(1)} %get-tuple-element.126), channel_id=1, source_target_pairs={{0,3},{1,2},{2,1},{3,0},{4,7},{5,6},{6,5},{7,4},{8,11},{9,10},{10,... | collective-permute-start | bytes 196616 | tf_op jit(solution)/shard_map/ppermute | solution.py:37
  434.7 25.2 %collective-permute-start.27 = (bf16[1,512,1024]{2,1,0:T(8,128)(2,1)}, bf16[1,512,1024]{2,1,0:T(8,128)(2,1)S(1)}, u32[]{:S(2)}, u32[]{:S(2)}) collective-permute-start(bf16[1,512,1024]{2,1,0:T(8,128)(2,1)} %slice.390), channel_id=1, source_target_pairs={{0,1},{1,0},{2,3},{3,2},{4,5},{5,4},{6,7},{7,6},{8,9},{9,8},{10,11... | collective-permute-start | bytes 3145736 | tf_op jit(solution)/shard_map/ppermute | solution.py:31
  447.6 34.8 %collective-permute-start.47 = (bf16[1,32,768]{2,1,0:T(8,128)(2,1)}, bf16[1,32,768]{2,1,0:T(8,128)(2,1)}, u32[]{:S(2)}, u32[]{:S(2)}) collective-permute-start(bf16[1,32,768]{2,1,0:T(8,128)(2,1)} %get-tuple-element.136), channel_id=1, source_target_pairs={{0,2},{1,3},{2,0},{3,1},{4,6},{5,7},{6,4},{7,5},{8,10},{9,11},{10,... | collective-permute-start | bytes 147464 | tf_op jit(solution)/shard_map/ppermute | solution.py:37
  447.6 42.5 %collective-permute-start.48 = (bf16[1,32,768]{2,1,0:T(8,128)(2,1)}, bf16[1,32,768]{2,1,0:T(8,128)(2,1)}, u32[]{:S(2)}, u32[]{:S(2)}) collective-permute-start(bf16[1,32,768]{2,1,0:T(8,128)(2,1)} %get-tuple-element.135), channel_id=1, source_target_pairs={{0,3},{1,2},{2,1},{3,0},{4,7},{5,6},{6,5},{7,4},{8,11},{9,10},{10,... | collective-permute-start | bytes 147464 | tf_op jit(solution)/shard_map/ppermute | solution.py:37
  (74 other events, 739.0 us)

commit v4 on v3

v4 whole, which is shorter than its diff:
```python
import functools

import jax
import jax.numpy as jnp
from jax import lax
from jax.experimental import pallas as pl
from jax.experimental.pallas import tpu as pltpu
from jax.sharding import PartitionSpec as P

HD = 64
ROT = 16
EPS = 1e-05
SCALE = 0.125
F32 = jnp.float32
BF = jnp.bfloat16


def dot(left, right, left_dim, right_dim):
    return lax.dot_general(
        left, right, (((left_dim,), (right_dim,)), ((), ())), preferred_element_type=F32
    )


def swap_batch(value, mask):
    count = lax.axis_size("batch")
    return lax.ppermute(value, "batch", [(i, i ^ mask) for i in range(count)])


def swap_seq(value, mask):
    count = lax.axis_size("seq")
    return lax.ppermute(value, "seq", [(i, i ^ mask) for i in range(count)])


def swap_member(value, mask):
    members = 2 * lax.axis_size("seq")
    count = lax.axis_size("batch") * lax.axis_size("seq")
    return lax.ppermute(
        value,
        ("batch", "seq"),
        [(i, (i // members) * members + ((i % members) ^ mask)) for i in range(count)],
    )


def after(value, *others):
    return lax.optimization_barrier((value,) + others)[0]


def sort_blocks(value, axis, me):
    count = value.shape[axis]
    before, behind = value.shape[:axis], value.shape[axis + 1 :]
    bit = 1
    while bit < count:
        paired = value.reshape(before + (count // (2 * bit), 2, bit) + behind)
        flipped = jnp.flip(paired, axis + 1)
        value = jnp.where((me & bit) > 0, flipped, paired).reshape(value.shape)
        bit = 2 * bit
    return value


def busy(micros):
    return pl.CostEstimate(flops=0, bytes_accessed=int(micros * 3.5e6), transcendentals=0)


def far_groups(chunk):
    groups = lax.axis_size("batch") // 2
    return jnp.stack([chunk] + [swap_batch(chunk, 4 * k) for k in range(1, groups // 2)])


def near_groups(stack):
    return swap_batch(stack, 2)


def fold_near(send, keep):
    return send.shape[0], keep, swap_batch(send, 2), send.dtype


def fold_far(state, *others):
    half, keep, got, dtype = state
    total = keep[0].astype(F32) + got[0].astype(F32)
    for k in range(1, half):
        piece = (keep[k].astype(F32) + got[k].astype(F32)).astype(dtype)
        total = total + swap_batch(after(piece, *others), 4 * k).astype(F32)
    return total


def member():
    return (lax.axis_index("batch") % 2) * lax.axis_size("seq") + lax.axis_index("seq")


def exchange_members(pieces):
    me = member()
    out = jnp.zeros_like(pieces)
    for k in range(pieces.shape[0]):
        piece = lax.dynamic_index_in_dim(pieces, me ^ k, 0, keepdims=True)
        got = piece if k == 0 else swap_member(piece, k)
        out = lax.dynamic_update_slice_in_dim(out, got, me ^ k, 0)
    return out


def gather_merger(block):
    seq = lax.axis_size("seq")
    batch = lax.axis_size("batch")
    members = 2 * seq
    groups = batch // 2
    lows = groups // members
    every = ("batch", "seq")
    group = lax.axis_index("batch") // 2
    root = group // lows
    found = jnp.where(member() == root, block, jnp.zeros_like(block))
    for k in range(1, members):
        pairs = [
            (g * members + g // lows, (g ^ (k * lows)) * members + g // lows) for g in range(groups)
        ]
        found = found + lax.ppermute(block, every, pairs)
    whole = found[None]
    bit = 1
    while bit < lows:
        got = swap_batch(whole, 2 * bit)
        swapped = (group & bit) > 0
        whole = jnp.where(swapped, jnp.concatenate([got, whole]), jnp.concatenate([whole, got]))
        bit = 2 * bit
    return whole.reshape(-1, block.shape[1])


def far_tokens(value, *others):
    if lax.axis_size("seq") == 2:
        return jnp.concatenate([value, swap_seq(after(value, *others), 1)], 1)
    return lax.all_gather(value, "seq", axis=1, tiled=True)


def near_tokens(value, *others):
    seqs = value.shape[0] // 2
    return value[:seqs].astype(F32) + swap_batch(value[seqs:], 1).astype(F32)


def part_tokens(mine, *others):
    if lax.axis_size("seq") == 2:
        stretch = mine.shape[1] // 2
        return mine[:, :stretch] + swap_seq(after(mine[:, stretch:].astype(BF), *others), 1).astype(F32)
    return lax.psum_scatter(mine.astype(BF), "seq", scatter_dimension=1, tiled=True).astype(F32)


def reduce_merger(grad):
    seq = lax.axis_size("seq")
    batch = lax.axis_size("batch")
    members = 2 * seq
    groups = batch // 2
    lows = groups // members
    every = ("batch", "seq")
    group = lax.axis_index("batch") // 2
    root = group // lows
    me = member()
    whole = grad.reshape((lows, -1, grad.shape[1]))
    bit = lows // 2
    while bit:
        halves = whole.reshape((2, -1) + whole.shape[1:])
        side = ((group & bit) > 0).astype(jnp.int32)
        away = lax.dynamic_index_in_dim(halves, 1 - side, 0, keepdims=False).astype(BF)
        whole = lax.dynamic_index_in_dim(halves, side, 0, keepdims=False)
        whole = whole + swap_batch(away, 2 * bit).astype(F32)
        bit = bit // 2
    block = whole[0].astype(BF)
    total = whole[0]
    for k in range(1, members):
        pairs = [
            ((g ^ (k * lows)) * members + g // lows, g * members + g // lows) for g in range(groups)
        ]
        total = total + lax.ppermute(block, every, pairs).astype(F32)
    rows = total.reshape(members, -1, grad.shape[1]).astype(BF)
    mine = lax.dynamic_index_in_dim(rows, me, 0, keepdims=False).astype(F32)
    out = jnp.where(me == root, mine, jnp.zeros_like(mine))
    for k in range(1, members):
        pairs = [
            (g * members + g // lows, g * members + ((g // lows) ^ k)) for g in range(groups)
        ]
        piece = lax.dynamic_index_in_dim(rows, me ^ k, 0, keepdims=False)
        out = out + lax.ppermute(piece, every, pairs).astype(F32)
    return out


def centre(rows):
    mean = jnp.mean(rows, -1, keepdims=True)
    centered = rows - mean
    spread = jnp.mean(centered * centered, -1, keepdims=True)
    rstd = lax.rsqrt(spread + EPS)
    return centered * rstd, rstd


def lay(far, near, out_ref, info, parts):
    group, me = info[0], info[2]
    half = far.shape[0]
    rows = out_ref.shape[0] // (2 * half)
    small = rows // parts
    for k in range(2 * half):
        source = (far, near)[k % 2]
        for r in range(parts):
            start = (group ^ k) * rows
            if parts > 1:
                start = start + (me ^ r) * small
            start = pl.multiple_of(start, small)
            out_ref[pl.ds(start, small), :] = source[k // 2, r * small : (r + 1) * small, :]


def split_out(total_ref, send_ref, keep_ref, info, parts):
    group, me = info[0], info[2]
    half, rows, _ = send_ref.shape
    small = rows // parts
    for k in range(2 * half):
        target = (keep_ref, send_ref)[k % 2]
        for r in range(parts):
            start = (group ^ k) * rows
            if parts > 1:
                start = start + (me ^ r) * small
            start = pl.multiple_of(start, small)
            target[k // 2, r * small : (r + 1) * small, :] = total_ref[pl.ds(start, small), :].astype(BF)


def add_to(total_ref, i, value):
    @pl.when(i == 0)
    def _():
        total_ref[...] = value

    @pl.when(i > 0)
    def _():
        total_ref[...] += value


def add_rows(out_ref, i, value):
    add_to(out_ref, i, jnp.sum(value, 0, keepdims=True))


def pick(own, peer):
    return jnp.where(pl.program_id(0) < pl.num_programs(0) // 2, own[...], peer[...])


def whole(shape):
    return pl.BlockSpec(shape, lambda *_: (0,) * len(shape), pipeline_mode=pl.Buffered(1))


def tiles(rows):
    block = min(512, rows)
    steps = 2 * rows // block

    def own(n):
        return pl.BlockSpec((block, n), lambda i, *_: (jnp.minimum(i, steps // 2 - 1), 0))

    def peer(n):
        return pl.BlockSpec((block, n), lambda i, *_: (jnp.maximum(i - steps // 2, 0), 0))

    def every(n):
        return pl.BlockSpec((block, n), lambda i, *_: (i, 0))

    return block, steps, own, peer, every


def call(kernel, micros, steps, in_specs, out_specs, out_shape, scratch, *operands):
    return pl.pallas_call(
        kernel,
        grid_spec=pltpu.PrefetchScalarGridSpec(
            num_scalar_prefetch=1, grid=(steps,), in_specs=in_specs, out_specs=out_specs, scratch_shapes=scratch
        ),
        out_shape=out_shape,
        cost_estimate=busy(micros),
        compiler_params=pltpu.CompilerParams(vmem_limit_bytes=58 * 1024 * 1024),
    )(*operands)


def cut_kernel(counts, info, mixer_ref, widen_ref, merger_ref, small_ref, *outs):
    members, groups, slim, unit = counts
    share, wide = mixer_ref.shape
    width = wide // 3
    start = 3 * slim + groups * unit
    for r, out in enumerate(outs):
        t = info[2] ^ r
        for c in range(3):
            columns = pl.ds(pl.multiple_of(c * width + t * slim, slim), slim)
            out[:share, c * slim : (c + 1) * slim] = mixer_ref[:, columns]
        for g in range(groups):
            columns = pl.ds(pl.multiple_of((g * members + t) * unit, unit), unit)
            out[:share, 3 * slim + g * unit : 3 * slim + (g + 1) * unit] = widen_ref[:, columns]
        out[:share, start:] = merger_ref[...]
        out[share:, :] = small_ref[...]


def cut_pieces(counts, info, mixer, widen, merger, small):
    members = counts[0]
    shape = (mixer.shape[0] + small.shape[0], small.shape[1])
    return call(
        functools.partial(cut_kernel, counts),
        3,
        1,
        [whole(mixer.shape), whole(widen.shape), whole(merger.shape), whole(small.shape)],
        [whole(shape)] * members,
        [jax.ShapeDtypeStruct(shape, BF)] * members,
        [],
        info, mixer, widen, merger, small,
    )


def paste_kernel(counts, info, *refs):
    members, lead, unit = counts
    parts, out = refs[:members], refs[members]
    for r, part in enumerate(parts):
        t = info[2] ^ r
        for g in range(lead):
            columns = pl.ds(pl.multiple_of((g * members + t) * unit, unit), unit)
            out[:, columns] = part[:, g * unit : (g + 1) * unit].astype(F32)


def paste_columns(info, parts, lead):
    members = len(parts)
    rows, columns = parts[0].shape
    shape = (rows, members * columns)
    return call(
        functools.partial(paste_kernel, (members, lead, columns // lead)),
        2,
        1,
        [whole(part.shape) for part in parts],
        whole(shape),
        jax.ShapeDtypeStruct(shape, F32),
        [],
        info, *parts,
    )


def swap_pieces(pieces):
    return [pieces[0]] + [swap_member(piece, k) for k, piece in enumerate(pieces) if k]


def sum_all(value):
    count = lax.axis_size("batch")
    bit = count // 2
    while bit:
        value = value + swap_batch(value, bit)
        bit = bit // 2
    bit = lax.axis_size("seq") // 2
    while bit:
        value = value + swap_seq(value, bit)
        bit = bit // 2
    return value


def attend_kernel(heads, block, info, q_ref, k_ref, v_ref, g_ref, c_ref, s_ref, begin_ref, mixed_ref, grad_ref):
    length = q_ref.shape[0]
    half = ROT // 2
    cosine, sine = c_ref[0], s_ref[0]
    middle = length // 2
    low = pl.ds(pl.multiple_of(info[1] * middle, middle), middle)
    high = pl.ds(pl.multiple_of((1 - info[1]) * middle, middle), middle)

    def take(ref):
        return jnp.concatenate([ref[low, :], ref[high, :]], 0)

    def put(ref, value):
        ref[low, :] = value[:middle]
        ref[high, :] = value[middle:]

    def put_grad(part, value):
        grad_ref[part, low, :] = value[:middle]
        grad_ref[part, high, :] = value[middle:]

    lane = lax.broadcasted_iota(jnp.int32, cosine.shape, 1) % HD
    leading = lane < half

    def roll(value, shift):
        if value.shape[1] % 128:
            return jnp.concatenate([value[:, -shift:], value[:, :-shift]], 1)
        return pltpu.roll(value, shift % value.shape[1], 1)

    def turn(value):
        return value * cosine + jnp.where(leading, -roll(value, -half), roll(value, half)) * sine

    def turn_back(value):
        return value * cosine + jnp.where(leading, roll(value, -half), -roll(value, half)) * sine

    keys_f = turn(take(k_ref))
    values_f = take(v_ref)
    query = (turn(take(q_ref)).astype(BF).astype(F32) * SCALE).astype(BF)
    keys, values = keys_f.astype(BF), values_f.astype(BF)
    keys_t, values_t = keys_f.T.astype(BF), values_f.T.astype(BF)
    grads = take(g_ref)
    grads_t = grads.astype(F32).T
    begin = begin_ref[0]
    dq_all, dk_all, dv_all, mixed_all = [], [], [], []
    for h in range(heads):
        span = slice(h * HD, (h + 1) * HD)
        qh, kh, vh, gh = query[:, span], keys[:, span], values[:, span], grads[:, span]
        kt, vt, gt = keys_t[span], values_t[span], grads_t[span]
        dq_parts, mixed_parts = [], []
        dk = [jnp.zeros((block, HD), F32) for _ in range(length // block)]
        dv = [jnp.zeros((block, HD), F32) for _ in range(length // block)]
        for i in range(length // block):
            n = (i + 1) * block
            rows = slice(i * block, n)
            q, g = qh[rows], gh[rows]
            scores = dot(kh[:n], q, 1, 1)
            place_k = lax.broadcasted_iota(jnp.int32, (n, block), 0)
            place_q = lax.broadcasted_iota(jnp.int32, (n, block), 1) + i * block
            allowed = (place_k >= begin[:, rows]) & (place_k <= place_q)
            scores = jnp.where(allowed, scores, -1e30)
            expo = jnp.exp(scores - jnp.max(scores, 0, keepdims=True))
            prob = expo * (1.0 / jnp.sum(expo, 0, keepdims=True))
            prob_b = prob.astype(BF)
            mixed = dot(vt[:, :n], prob_b, 1, 0)
            mixed_parts.append(mixed)
            center = jnp.sum(mixed * gt[:, rows], 0, keepdims=True)
            score_grad = (prob * (dot(vh[:n], g, 1, 1) - center)).astype(BF)
            dq_parts.append(dot(kt[:, :n], score_grad, 1, 0) * SCALE)
            dk_add = dot(score_grad, q, 1, 0)
            dv_add = dot(prob_b, g, 1, 0)
            for j in range(i + 1):
                dk[j] = dk[j] + dk_add[j * block : (j + 1) * block]
                dv[j] = dv[j] + dv_add[j * block : (j + 1) * block]
        dq_all.append(jnp.concatenate(dq_parts, 1))
        mixed_all.append(jnp.concatenate(mixed_parts, 1))
        dk_all.append(jnp.concatenate(dk, 0))
        dv_all.append(jnp.concatenate(dv, 0))
    put(mixed_ref, jnp.concatenate(mixed_all, 0).T.astype(BF))
    put_grad(0, turn_back(jnp.concatenate(dq_all, 0).T).astype(BF))
    put_grad(1, turn_back(jnp.concatenate(dk_all, 1)).astype(BF))
    put_grad(2, jnp.concatenate(dv_all, 1).astype(BF))


def attend(info, side, project, mixed_grad, tables, begin):
    seqs, length = begin.shape
    seqs = seqs // 2
    skip = side * seqs
    wide = project.shape[1]
    rows = seqs * length
    width = wide // 3
    heads = min(2, width // HD)
    lanes = heads * HD
    steps = width // lanes
    block = min(256, length)

    parts = (project, project, project)
    ahead = steps
    if lanes % 128:
        parts = tuple(jnp.split(project, 3, 1))
        ahead = 0

    def of(part):
        return pl.BlockSpec((length, lanes), lambda s, h, _: (s + skip, part * ahead + h))

    table = pl.BlockSpec((1, length, lanes), lambda s, h, _: (s + skip, 0, 0))
    return pl.pallas_call(
        functools.partial(attend_kernel, heads, block),
        grid_spec=pltpu.PrefetchScalarGridSpec(
            num_scalar_prefetch=1,
            grid=(seqs, steps),
            in_specs=[
                of(0),
                of(1),
                of(2),
                of(0),
                table,
                table,
                pl.BlockSpec((1, 1, length), lambda s, h, _: (s + skip, 0, 0)),
            ],
            out_specs=[
                pl.BlockSpec((length, lanes), lambda s, h, _: (s, h)),
                pl.BlockSpec((3, length, lanes), lambda s, h, _: (0, s, h)),
            ],
        ),
        out_shape=[
            jax.ShapeDtypeStruct((rows, width), BF),
            jax.ShapeDtypeStruct((3, rows, width), BF),
        ],
        cost_estimate=busy(10 * seqs * steps),
        compiler_params=pltpu.CompilerParams(vmem_limit_bytes=56 * 1024 * 1024),
    )(info, *parts, mixed_grad, *tables, begin[:, None, :])


def project_kernel(parts, info, xo_ref, xp_ref, gm_ref, sm_ref, gf_ref, sf_ref, bias_ref, far_ref, near_ref, *refs):
    first_ref, second_ref, normed_ref, project_ref, mixer = refs

    @pl.when(pl.program_id(0) == 0)
    def _():
        lay(far_ref, near_ref, mixer, info, parts)

    normed, _ = centre(pick(xo_ref, xp_ref).astype(F32))
    first = (normed * gm_ref[...] + sm_ref[...]).astype(BF)
    first_ref[...] = first
    second_ref[...] = (normed * gf_ref[...] + sf_ref[...]).astype(BF)
    normed_ref[...] = normed.astype(BF)
    project_ref[...] = dot(first, mixer[...], 1, 0) + bias_ref[...]


def project_all(parts, info, inputs, gain, shift, gain_f, shift_f, bias, far, near):
    rows, width = inputs[0].shape
    wide = far.shape[2]
    _, steps, own, peer, every = tiles(rows)
    return call(
        functools.partial(project_kernel, parts),
        12,
        steps,
        [own(width), peer(width)] + [whole((1, width))] * 4 + [whole((1, wide))]
        + [whole(far.shape), whole(near.shape)],
        [every(width), every(width), every(width), every(wide)],
        [jax.ShapeDtypeStruct((2 * rows, width), BF)] * 3 + [jax.ShapeDtypeStruct((2 * rows, wide), F32)],
        [pltpu.VMEM((width, wide), BF)],
        info, *inputs, gain, shift, gain_f, shift_f, bias, far, near,
    )


def spread_kernel(info, go_ref, gp_ref, merger_ref, out_ref):
    out_ref[...] = dot(pick(go_ref, gp_ref), merger_ref[...], 1, 1).astype(BF)


def spread_back(info, upstream, merger):
    rows, width = upstream[0].shape
    slim = merger.shape[0]
    _, steps, own, peer, every = tiles(rows)
    return call(
        spread_kernel,
        4,
        steps,
        [own(width), peer(width), whole(merger.shape)],
        every(slim),
        jax.ShapeDtypeStruct((2 * rows, slim), BF),
        [],
        info, *upstream, merger,
    )


def widen_kernel(parts, info, second_ref, go_ref, gp_ref, bias_ref, far_ref, near_ref, *refs):
    active_ref, slope_ref, send_ref, keep_ref, widen, total = refs
    i = pl.program_id(0)
    hidden = widen.shape[1]
    piece = min(256, hidden)

    @pl.when(i == 0)
    def _():
        lay(far_ref, near_ref, widen, info, parts)
        total[...] = jnp.zeros_like(total)

    second = second_ref[...]
    upstream = pick(go_ref, gp_ref)

    def front(n):
        return dot(second, widen[:, n : n + piece], 1, 0) + bias_ref[:, n : n + piece]

    ahead = front(0)
    for n in range(0, hidden, piece):
        widened = ahead
        if n + piece < hidden:
            ahead = front(n + piece)
        bell = 0.5 + 0.5 * lax.erf(widened * (0.5**0.5))
        active = (widened * bell).astype(BF)
        slope = bell + widened * jnp.exp(-0.5 * widened * widened) * (0.15915494309189535**0.5)
        active_ref[:, n : n + piece] = active
        slope_ref[:, n : n + piece] = slope.astype(BF)
        total[n : n + piece, :] += dot(active, upstream, 0, 0)

    @pl.when(i == pl.num_programs(0) - 1)
    def _():
        split_out(total, send_ref, keep_ref, info, 1)


def narrow_kernel(parts, info, second_ref, normed_ref, go_ref, gp_ref, a_ref, s_ref, gain_ref, *refs):
    wf_ref, wn_ref, nf_ref, nn_ref, out_ref, e_ref, sums_ref, bsum_ref, send_ref, keep_ref, widen, narrow, total = refs
    i = pl.program_id(0)
    width, hidden = widen.shape
    piece = min(256, hidden)

    @pl.when(i == 0)
    def _():
        lay(wf_ref, wn_ref, widen, info, parts)
        lay(nf_ref, nn_ref, narrow, info, 1)
        total[...] = jnp.zeros_like(total)

    second = second_ref[...]
    upstream = pick(go_ref, gp_ref)
    out_ref[...] = dot(a_ref[...], narrow[...], 1, 0).astype(BF)
    grads = []
    for n in range(0, hidden, piece):
        active_grad = dot(upstream, narrow[n : n + piece, :], 1, 1)
        widened_grad = (active_grad * s_ref[:, n : n + piece].astype(F32)).astype(BF)
        grads.append(widened_grad)
        total[:, n : n + piece] += dot(second, widened_grad, 0, 0)
    widened_grad = jnp.concatenate(grads, 1)
    add_rows(bsum_ref, i, widened_grad.astype(F32))
    sums = []
    step = min(256, width)
    for n in range(0, width, step):
        second_grad = dot(widened_grad, widen[n : n + step, :], 1, 1)
        e_ref[:, n : n + step] = (second_grad * gain_ref[:, n : n + step]).astype(BF)
        product = second_grad * normed_ref[:, n : n + step].astype(F32)
        sums.append(jnp.concatenate([jnp.sum(product, 0, keepdims=True), jnp.sum(second_grad, 0, keepdims=True)], 0))
    add_to(sums_ref, i, jnp.concatenate(sums, 1))

    @pl.when(i == pl.num_programs(0) - 1)
    def _():
        split_out(total, send_ref, keep_ref, info, parts)


def feed_widen(parts, info, second, upstream, bias, far, near):
    rows, width = upstream[0].shape
    half, _, hidden = far.shape
    _, steps, own, peer, every = tiles(rows)
    shape = (half, hidden // (2 * half), width)
    return call(
        functools.partial(widen_kernel, parts),
        15,
        steps,
        [every(width), own(width), peer(width), whole((1, hidden)), whole(far.shape), whole(near.shape)],
        [every(hidden), every(hidden), whole(shape), whole(shape)],
        [jax.ShapeDtypeStruct((2 * rows, hidden), BF)] * 2 + [jax.ShapeDtypeStruct(shape, BF)] * 2,
        [pltpu.VMEM((width, hidden), BF), pltpu.VMEM((hidden, width), F32)],
        info, second, *upstream, bias, far, near,
    )


def feed_narrow(parts, info, second, normed, upstream, active, slope, gain, widen, narrow):
    rows, width = upstream[0].shape
    half, _, hidden = widen[0].shape
    _, steps, own, peer, every = tiles(rows)
    shape = (half, width // (2 * half), hidden)
    return call(
        functools.partial(narrow_kernel, parts),
        25,
        steps,
        [every(width), every(width), own(width), peer(width), every(hidden), every(hidden), whole((1, width))]
        + [whole(part.shape) for part in widen + narrow],
        [every(width), every(width), whole((2, width)), whole((1, hidden)), whole(shape), whole(shape)],
        [
            jax.ShapeDtypeStruct((2 * rows, width), BF),
            jax.ShapeDtypeStruct((2 * rows, width), BF),
            jax.ShapeDtypeStruct((2, width), F32),
            jax.ShapeDtypeStruct((1, hidden), F32),
            jax.ShapeDtypeStruct(shape, BF),
            jax.ShapeDtypeStruct(shape, BF),
        ],
        [pltpu.VMEM((width, hidden), BF), pltpu.VMEM((hidden, width), BF), pltpu.VMEM((width, hidden), F32)],
        info, second, normed, *upstream, active, slope, gain, *widen, *narrow,
    )


def merge_kernel(info, m_ref, go_ref, gp_ref, f_ref, w_ref, out_ref, grad_ref):
    mixed = m_ref[...]
    out_ref[...] = (dot(mixed, w_ref[...], 1, 0) + f_ref[...].astype(F32)).astype(BF)
    add_to(grad_ref, pl.program_id(0), dot(mixed, pick(go_ref, gp_ref), 0, 0))


def merge(info, mixed, upstream, partial, merger):
    rows, width = upstream[0].shape
    slim = mixed.shape[1]
    _, steps, own, peer, every = tiles(rows)
    return call(
        merge_kernel,
        7,
        steps,
        [every(slim), own(width), peer(width), every(width), whole(merger.shape)],
        [every(width), whole((slim, width))],
        [jax.ShapeDtypeStruct((2 * rows, width), BF), jax.ShapeDtypeStruct((slim, width), F32)],
        [],
        info, mixed, *upstream, partial, merger,
    )


def mixer_kernel(parts, info, first_ref, normed_ref, e_ref, p_ref, gain_ref, far_ref, near_ref, *refs):
    out_ref, sums_ref, bsum_ref, send_ref, keep_ref, mixer, total = refs
    i = pl.program_id(0)
    width = mixer.shape[0]

    @pl.when(i == 0)
    def _():
        lay(far_ref, near_ref, mixer, info, parts)
        total[...] = jnp.zeros_like(total)

    grad = jnp.concatenate([p_ref[0], p_ref[1], p_ref[2]], 1)
    total[...] += dot(first_ref[...], grad, 0, 0)
    sums = []
    step = min(256, width)
    for n in range(0, width, step):
        first_grad = dot(grad, mixer[n : n + step, :], 1, 1)
        e = e_ref[:, n : n + step].astype(F32)
        out_ref[:, n : n + step] = (first_grad * gain_ref[:, n : n + step] + e).astype(BF)
        product = first_grad * normed_ref[:, n : n + step].astype(F32)
        sums.append(jnp.concatenate([jnp.sum(product, 0, keepdims=True), jnp.sum(first_grad, 0, keepdims=True)], 0))
    add_to(sums_ref, i, jnp.concatenate(sums, 1))
    add_rows(bsum_ref, i, grad.astype(F32))

    @pl.when(i == pl.num_programs(0) - 1)
    def _():
        split_out(total, send_ref, keep_ref, info, parts)


def mixer_back(parts, info, first, normed, error, grads, gain, far, near):
    rows, width = first.shape
    half, _, wide = far.shape
    block, steps, own, peer, every = tiles(rows // 2)
    shape = (half, width // (2 * half), wide)
    return call(
        functools.partial(mixer_kernel, parts),
        14,
        steps,
        [every(width), every(width), every(width)]
        + [pl.BlockSpec((3, block, wide // 3), lambda i, _: (0, i, 0)), whole((1, width))]
        + [whole(far.shape), whole(near.shape)],
        [every(width), whole((2, width)), whole((1, wide)), whole(shape), whole(shape)],
        [
            jax.ShapeDtypeStruct((rows, width), BF),
            jax.ShapeDtypeStruct((2, width), F32),
            jax.ShapeDtypeStruct((1, wide), F32),
            jax.ShapeDtypeStruct(shape, BF),
            jax.ShapeDtypeStruct(shape, BF),
        ],
        [pltpu.VMEM((width, wide), BF), pltpu.VMEM((width, wide), F32)],
        info, first, normed, error, grads, gain, far, near,
    )


def turn_tables(position, lanes):
    half = ROT // 2
    lane = jnp.arange(lanes) % HD
    freq = 10000.0 ** (-((lane % half).astype(F32) * 2.0) / float(ROT))
    freq = jnp.where(lane < ROT, freq, 0.0)
    phase = position.astype(F32)[..., None] * freq
    return jnp.cos(phase), jnp.sin(phase)


def local(
    tokens,
    segments,
    cotangent,
    mixer_gain,
    mixer_shift,
    mixer_weight,
    mixer_bias,
    merger_weight,
    merger_bias,
    feeder_gain,
    feeder_shift,
    widen_weight,
    widen_bias,
    narrow_weight,
    narrow_bias,
):
    seqs, stretch, width = tokens.shape
    seq = lax.axis_size("seq")
    groups = lax.axis_size("batch") // 2
    members = 2 * seq
    devices = groups * members
    length = stretch * seq
    here = lax.axis_index("seq")
    me = member()
    group = lax.axis_index("batch") // 2
    share = mixer_weight.shape[0]
    hidden = widen_weight.shape[1]
    slim = width // members
    unit = hidden // devices
    mine_h = groups * unit
    block = members * share
    wide = 3 * slim
    turned = here if seq == 2 else jnp.zeros_like(here)
    info = jnp.stack([group, turned, me]).astype(jnp.int32)
    related = share % 16 == 0 and unit % 128 == 0 and slim % 128 == 0
    parts = members if related else 1

    vectors = (mixer_gain, mixer_shift, mixer_bias, merger_bias, feeder_gain, feeder_shift, widen_bias, narrow_bias)
    sizes = [v.shape[0] for v in vectors]
    cuts = [sum(sizes[: i + 1]) for i in range(len(sizes) - 1)]
    count = sum(sizes)
    span = wide + mine_h + width
    packed = jnp.concatenate(vectors)
    small = jnp.stack(
        [
            jnp.pad(packed, (0, span - packed.size)),
            jnp.pad(segments.reshape(-1).astype(BF), (0, span - segments.size)),
        ]
    )
    small = jnp.pad(small, ((0, 14), (0, 0)))
    if related:
        got = swap_pieces(
            cut_pieces((members, groups, slim, unit), info, mixer_weight, widen_weight, merger_weight, small)
        )
        rows_in = [piece[:share] for piece in got]
        notes = sort_blocks(jnp.stack([piece[share : share + 2] for piece in got]), 0, me)
    else:
        mixer_pieces = mixer_weight.reshape(share, 3, members, slim).transpose(2, 0, 1, 3)
        widen_pieces = widen_weight.reshape(share, groups, members, unit).transpose(2, 0, 1, 3)
        pieces = [
            mixer_pieces.reshape(members, share, wide),
            widen_pieces.reshape(members, share, mine_h),
            jnp.broadcast_to(merger_weight, (members, share, width)),
        ]
        pieces = jnp.concatenate(
            [jnp.concatenate(pieces, 2), jnp.broadcast_to(small[:2], (members, 2, span))], 1
        )
        got = exchange_members(pieces)
        rows_in = [got[t, :share] for t in range(members)]
        notes = got[:, share:]
    segs = notes[:, 1, : segments.size].astype(jnp.int32).reshape(2, seq, seqs, stretch)
    segs = segs.transpose(0, 2, 1, 3).reshape(2, seqs, length)
    segs = jnp.where(lax.axis_index("batch") % 2 == 0, segs, segs[::-1]).reshape(2 * seqs, length)
    notes = jnp.pad(notes[:, 0, :wide], ((0, (-members) % 16), (0, 0)))
    mixer_chunk = jnp.concatenate([piece[:, :wide] for piece in rows_in] + [notes], 0)
    widen_chunk = jnp.concatenate([piece[:, wide : wide + mine_h] for piece in rows_in], 0)
    merger_block = jnp.concatenate([piece[:, wide + mine_h :] for piece in rows_in], 0)

    mixer_far = far_groups(mixer_chunk)
    inputs_own = far_tokens(tokens, *got).reshape(-1, width)
    merger = gather_merger(merger_block)
    if related:
        merger = sort_blocks(merger.reshape(-1, members, share, width), 1, me).reshape(slim, width)
    mixer_near = near_groups(mixer_far)
    widen_far = far_groups(after(widen_chunk, mixer_far))
    inputs = (inputs_own, swap_batch(inputs_own, 1))
    upstream_own = far_tokens(cotangent, inputs_own).reshape(-1, width)
    upstream = (upstream_own, swap_batch(upstream_own, 1))
    widen_near = near_groups(after(widen_far, mixer_near))
    narrow_far = far_groups(after(narrow_weight, widen_far))
    narrow_near = near_groups(after(narrow_far, widen_near))
    widen = (widen_far, widen_near)
    narrow = (narrow_far, narrow_near)

    both = jnp.stack([mixer_far[:, block : block + members], mixer_near[:, block : block + members]], 1)
    gathered = sort_blocks(both.reshape(groups, members, -1)[:, :, :count], 0, group)
    gathered = gathered.reshape(devices, -1).astype(F32)
    gain_m, shift_m, bias_m, bias_o, gain_f, shift_f, bias_w, bias_n = [
        v.reshape(1, -1) for v in jnp.split(gathered, cuts, 1)
    ]
    bias_m_mine = lax.dynamic_index_in_dim(bias_m.reshape(3, members, slim), me, 1).reshape(1, -1)
    bias_w_mine = lax.dynamic_index_in_dim(bias_w.reshape(groups, members, unit), me, 1).reshape(1, -1)
    place = jnp.arange(length, dtype=jnp.int32)
    begin = jnp.sum((segs[:, None, :] < segs[:, :, None]).astype(jnp.int32), -1)
    tables = turn_tables(place[None, :] - begin, min(2, slim // HD) * HD)

    first, second, normed, project = project_all(
        parts, info, inputs, gain_m, shift_m, gain_f, shift_f, bias_m_mine, mixer_far, mixer_near
    )
    mixed_grad = spread_back(after(info, project), upstream, merger)
    mixed_a, grad_a = attend(info, 0, project, mixed_grad, tables, begin)

    active, slope, n_send, n_keep = feed_widen(
        parts, after(info, mixed_a, narrow_far), second, upstream, bias_w_mine, widen_far, widen_near
    )
    narrow_state = fold_near(n_send, n_keep)

    mixed_b, grad_b = attend(after(info, active), 1, project, mixed_grad, tables, begin)

    partial, error, feed_sums, widen_bias_grad, w_send, w_keep = feed_narrow(
        parts, after(info, mixed_b, narrow_state[2]), second, normed, upstream, active, slope, gain_f, widen, narrow
    )
    narrow_out = fold_far(narrow_state)
    widen_state = fold_near(after(w_send, narrow_state[2]), w_keep)

    mixed = jnp.concatenate([mixed_a, mixed_b], 0)
    project_grad = jnp.concatenate([grad_a, grad_b], 1)
    partial, merger_grad = merge(info, mixed, upstream, partial, merger)
    error, mixer_sums, mixer_bias_grad, m_send, m_keep = mixer_back(
        parts, after(info, partial), first, normed, error, project_grad, gain_m, mixer_far, mixer_near
    )
    own = tokens.astype(F32)
    layer_output = part_tokens(near_tokens(partial.reshape(2 * seqs, length, width)))
    mixer_state = fold_near(after(m_send, widen_state[2]), m_keep)
    widen_sum = fold_far(widen_state, narrow_out)
    merger_out = reduce_merger(merger_grad)
    mixer_sum = fold_far(mixer_state, widen_sum)

    def bring_back(total, lead):
        if related:
            got = swap_pieces([total[r * share : (r + 1) * share].astype(BF) for r in range(members)])
            return paste_columns(info, got, lead)
        got = exchange_members(total.reshape(members, share, -1).astype(BF))
        got = got.reshape(members, share, lead, -1).transpose(1, 2, 0, 3)
        return got.reshape(share, -1).astype(F32)

    widen_out = bring_back(widen_sum, groups)
    mixer_out = bring_back(mixer_sum, 3)

    error = part_tokens(near_tokens(error.reshape(2 * seqs, length, width)), layer_output)
    layer_output = (own + layer_output + (bias_o + bias_n)).astype(BF)
    normed, rstd = centre(own)
    back = rstd * (
        error
        - jnp.mean(error, -1, keepdims=True)
        - normed * jnp.mean(error * normed, -1, keepdims=True)
    )
    tokens_grad = (cotangent.astype(F32) + back).astype(BF)

    def spread_out(value, lead):
        mine = jnp.arange(members)[None, :, None] == me
        return jnp.where(mine, value.reshape(lead, 1, -1), 0.0).reshape(-1, width)

    bias_grad = jnp.sum(cotangent.astype(F32), (0, 1))[None]
    sums = (mixer_sums, spread_out(mixer_bias_grad, 3), bias_grad, feed_sums, spread_out(widen_bias_grad, groups))
    total = sum_all(jnp.concatenate(sums, 0))
    flat_index = lax.axis_index("batch") * seq + here
    at = 0
    owned = []
    for size in sizes[:-1]:
        rows = size * devices // width
        owned.append(lax.dynamic_slice_in_dim(total[at : at + rows].reshape(-1), flat_index * size, size))
        at = at + rows
    gain_m_out, shift_m_out, bias_m_out, bias_o_out, gain_f_out, shift_f_out, bias_w_out = owned
    return (
        layer_output,
        tokens_grad,
        gain_m_out,
        shift_m_out,
        mixer_out,
        bias_m_out,
        merger_out,
        bias_o_out,
        gain_f_out,
        shift_f_out,
        widen_out,
        bias_w_out,
        narrow_out,
        bias_o_out,
    )


def solution(mesh):
    vector = P(("batch", "seq"))
    matrix = P(("batch", "seq"), None)
    rows = P("batch", "seq", None)
    params = (vector, vector, matrix, vector, matrix, vector, vector, vector, matrix, vector, matrix, vector)
    return jax.shard_map(
        local,
        mesh=mesh,
        in_specs=(rows, P("batch", "seq"), rows) + params,
        out_specs=(rows, rows) + params,
        check_vma=False,
    )
```

time: 502 us -> 447 us (0.89)
  local copies, waits for them, and re-layouts: 91.3 us -> 35 us
  waiting for transfers between devices: 124 us -> 138 us
  starting transfers between devices: 91.2 us -> 79.1 us
    ppermute x4 -> x5, waiting for transfers between devices: 0.42 us -> 43.2 us  [swap_seq(): return lax.ppermute(value, 'seq', [(i, i ^ mask) for i in range(count)])]
    concatenate x49 -> x2, local copies, waits for them, and re-layouts: 33.9 us -> 0.86 us  [the longest x1 0.85 us: local(): total = sum_all(jnp.concatenate(sums, 0))]
    dynamic_update_slice x16 -> x0, local copies, waits for them, and re-layouts: 26.6 us -> none  [the longest x14 26.5 us: exchange_members(): out = lax.dynamic_update_slice_in_dim(out, got, me ^ k, 0)]
    ppermute x34, waiting for transfers between devices: 102 us -> 80.9 us  [swap_batch(): return lax.ppermute(value, 'batch', [(i, i ^ mask) for i in range(count)])]
    ppermute x34, starting transfers between devices: 63.2 us -> 48.6 us  [swap_batch(): return lax.ppermute(value, 'batch', [(i, i ^ mask) for i in range(count)])]
    reshape x14 -> x3, local copies, waits for them, and re-layouts: 7.46 us -> 0.07 us  [the longest x1 0.04 us: sort_blocks(): paired = value.reshape(before + (count // (2 * bit), 2, bit) + behind)]
    ppermute x12 -> x9, waiting for transfers between devices: 15 us -> 9.21 us  [swap_member(): lax.ppermute(value, ('batch', 'seq'), [(i, i // members * members + (i %...]
    concatenate x1, local copies, waits for them, and re-layouts: 0.11 us -> 5.51 us  [local(): packed = jnp.concatenate(vectors)]
  transfers between devices with their start and end apart: 59 -> 57, of which waited for: 20 -> 17; matrix products, arithmetic and copies ran while one was open for 23% -> 13% of each run, Pallas kernels for 9% -> 12%
where the time goes in v4:
time: 447 us; the launch traced here: 440 us
  Pallas kernels  144 us (32%)
  waiting for transfers between devices  138 us (31%)
  starting transfers between devices  79.1 us (18%)
  other arithmetic  42.1 us (9%)
  local copies, waits for them, and re-layouts  35 us (8%)
    pallas_call x9, Pallas kernels, call(): pl.pallas_call(kernel, grid_spec=pltpu.PrefetchScalarGridSpec(num_scalar_...  98.1 us
    ppermute x34, waiting for transfers between devices, swap_batch(): return lax.ppermute(value, 'batch', [(i, i ^ mask) for i in range(count)])  80.9 us
    ppermute x34, starting transfers between devices, swap_batch(): return lax.ppermute(value, 'batch', [(i, i ^ mask) for i in range(count)])  48.6 us
    pallas_call x2, Pallas kernels, attend(): pl.pallas_call(functools.partial(attend_kernel, heads, block), grid_spec=...  45.9 us
    ppermute x5, waiting for transfers between devices, swap_seq(): return lax.ppermute(value, 'seq', [(i, i ^ mask) for i in range(count)])  43.2 us
    ppermute x9, waiting for transfers between devices, swap_member(): lax.ppermute(value, ('batch', 'seq'), [(i, i // members * members + (i %...  9.21 us
  transfers between devices with their start and end apart: 57, of which 17 were waited for; matrix products, arithmetic and copies ran while one was open for 13% of the time, Pallas kernels for 12%

profile of v4, /device:TPU:0, one launch (start us, length us, event | category | flops | bytes accessed | tf_op | source)
XLA Modules:
  0.0 440.1 jit_solution(9991586756704971866)
XLA Ops:
  0.7 5.5 %concatenate.51 = bf16[416]{0:T(512)(128)(2,1)S(1)} concatenate(bf16[32]{0:T(256)(128)(2,1)} %param.18, bf16[32]{0:T(256)(128)(2,1)} %param.19, bf16[96]{0:T(256)(128)(2,1)} %param.21, bf16[32]{0:T(256)(128)(2,1)} %param.23, bf16[32]{0:T(256)(128)(2,1)} %param.24, bf16[32]{0:T(256)(128)(2,1)} %param.25, bf16[128]{0:T(256)(128)(2,1)} %param.27, bf16[32]{0:T(256)(128)(2,1)} %param.29), dimensions={0} | concatenate | bytes 1664 | tf_op jit(solution)/shard_map/concatenate | solution.py:766
  16.7 9.2 %collective-permute-done.2 = bf16[48,2816]{1,0:T(8,128)(2,1)S(1)} collective-permute-done((bf16[48,2816]{1,0:T(8,128)(2,1)}, bf16[48,2816]{1,0:T(8,128)(2,1)S(1)}, u32[]{:S(2)}, u32[]{:S(2)}) %collective-permute-start.2) | collective-permute-done | bytes 270368 | tf_op jit(solution)/shard_map/ppermute | solution.py:37
  38.6 18.0 %collective-permute-done.3 = bf16[1,512,1024]{2,1,0:T(8,128)(2,1)S(1)} collective-permute-done((bf16[1,512,1024]{2,1,0:T(8,128)(2,1)S(1)}, bf16[1,512,1024]{2,1,0:T(8,128)(2,1)S(1)}, u32[]{:S(2)}, u32[]{:S(2)}) %collective-permute-start.3) | collective-permute-done | bytes 1048608 | tf_op jit(solution)/shard_map/ppermute | solution.py:31
  56.5 3.5 collective-permute-start.12
  64.3 5.5 %multiply_sine_fusion = (f32[2,1024,128]{2,1,0:T(8,128)}, f32[2,1024,128]{2,1,0:T(8,128)}) fusion(f32[128]{0:T(128)S(1)} %compare_select_fusion.2, f32[2,1024]{1,0:T(2,128)S(1)} %subtract_convert_fusion), kind=kLoop, calls=%fused_computation.28 | loop fusion | flops 262144 | bytes 2105856 | tf_op jit(solution)/shard_map/sin | solution.py:720
  82.7 10.6 %collective-permute-done.16 = bf16[128,1024]{1,0:T(8,128)(2,1)S(1)} collective-permute-done((bf16[128,1024]{1,0:T(8,128)(2,1)S(1)}, bf16[128,1024]{1,0:T(8,128)(2,1)S(1)}, u32[]{:S(2)}, u32[]{:S(2)}) %collective-permute-start.16) | collective-permute-done | bytes 262176 | tf_op jit(solution)/shard_map/ppermute | solution.py:26
  94.4 3.4 collective-permute-start.18
  100.6 5.6 %collective-permute-done.18 = bf16[128,1024]{1,0:T(8,128)(2,1)S(1)} collective-permute-done((bf16[128,1024]{1,0:T(8,128)(2,1)S(1)}, bf16[128,1024]{1,0:T(8,128)(2,1)S(1)}, u32[]{:S(2)}, u32[]{:S(2)}) %collective-permute-start.18) | collective-permute-done | bytes 262176 | tf_op jit(solution)/shard_map/ppermute | solution.py:26
  107.3 11.4 %collective-permute-done.19 = bf16[128,1024]{1,0:T(8,128)(2,1)S(1)} collective-permute-done((bf16[128,1024]{1,0:T(8,128)(2,1)S(1)}, bf16[128,1024]{1,0:T(8,128)(2,1)S(1)}, u32[]{:S(2)}, u32[]{:S(2)}) %collective-permute-start.19) | collective-permute-done | bytes 262176 | tf_op jit(solution)/shard_map/ppermute | solution.py:26
  125.7 15.4 %collective-permute-done.21.near_ref.refs_1_ = bf16[4,128,1024]{2,1,0:T(8,128)(2,1)} collective-permute-done((bf16[4,128,1024]{2,1,0:T(8,128)(2,1)}, bf16[4,128,1024]{2,1,0:T(8,128)(2,1)}, u32[]{:S(2)}, u32[]{:S(2)}) %collective-permute-start.21) | collective-permute-done | bytes 1048608 | tf_op jit(solution)/shard_map/ppermute | solution.py:26
  141.1 11.7 %shard_map.255 = (bf16[2048,1024]{1,0:T(8,128)(2,1)}, bf16[2048,1024]{1,0:T(8,128)(2,1)}, bf16[2048,1024]{1,0:T(8,128)(2,1)}, f32[2048,768]{1,0:T(8,128)}) custom-call(s32[3]{0:T(128)} %pad_add_fusion.info, bf16[1024,1024]{1,0:T(8,128)(2,1)} %maximum_bitcast_fusion.xo_ref, bf16[1024,1024]{1,0:T(8,128)(2,1)} %collective-permute-done.4.xp_ref, ...), custom_call_target="tpu_custom_call" | custom-call | bytes 42000000 | tf_op jit(solution)/shard_map/pallas_call | solution.py:257
  152.9 6.0 %shard_map.256.g_ref = bf16[2048,256]{1,0:T(8,128)(2,1)} custom-call(s32[3]{0:T(128)} %pad_add_fusion.info, bf16[1024,1024]{1,0:T(8,128)(2,1)} %copy-done, bf16[1024,1024]{1,0:T(8,128)(2,1)} %collective-permute-done.10.gp_ref, bf16[256,1024]{1,0:T(8,128)(2,1)} %bitcast.157), custom_call_target="tpu_custom_call" | custom-call | bytes 14000000 | tf_op jit(solution)/shard_map/pallas_call | solution.py:257
  158.8 23.1 %shard_map.257 = (bf16[1024,256]{1,0:T(8,128)(2,1)}, bf16[3,1024,256]{2,1,0:T(8,128)(2,1)}) custom-call(s32[3]{0:T(128)} %pad_add_fusion.info, f32[2048,768]{1,0:T(8,128)} %get-tuple-element.68.q_ref.k_ref.v_ref, f32[2048,768]{1,0:T(8,128)} %get-tuple-element.68.q_ref.k_ref.v_ref, f32[2048,768]{1,0:T(8,128)} %get-tuple-element.68.q_ref.k_ref.v_ref, ...), custom_call_target="tpu_custom_call" | custom-call | bytes 70000000 | tf_op jit(solution)/shard_map/pallas_call | solution.py:446
  181.9 19.3 %shard_map.258 = (bf16[2048,1024]{1,0:T(8,128)(2,1)}, bf16[2048,1024]{1,0:T(8,128)(2,1)}, bf16[4,128,1024]{2,1,0:T(8,128)(2,1)}, bf16[4,128,1024]{2,1,0:T(8,128)(2,1)}) custom-call(s32[3]{0:T(128)} %pad_add_fusion.info, bf16[2048,1024]{1,0:T(8,128)(2,1)} %get-tuple-element.75.second_ref, bf16[1024,1024]{1,0:T(8,128)(2,1)} %copy-done, ...), custom_call_target="tpu_custom_call" | custom-call | bytes 52500000 | tf_op jit(solution)/shard_map/pallas_call | solution.py:257
  203.3 22.9 %shard_map.259 = (bf16[1024,256]{1,0:T(8,128)(2,1)}, bf16[3,1024,256]{2,1,0:T(8,128)(2,1)}) custom-call(s32[3]{0:T(128)} %pad_add_fusion.info, f32[2048,768]{1,0:T(8,128)} %get-tuple-element.68.q_ref.k_ref.v_ref, f32[2048,768]{1,0:T(8,128)} %get-tuple-element.68.q_ref.k_ref.v_ref, f32[2048,768]{1,0:T(8,128)} %get-tuple-element.68.q_ref.k_ref.v_ref, ...), custom_call_target="tpu_custom_call" | custom-call | bytes 70000000 | tf_op jit(solution)/shard_map/pallas_call | solution.py:446
  228.2 15.7 %collective-permute-done.23.refs_3_ = bf16[4,128,1024]{2,1,0:T(8,128)(2,1)S(1)} collective-permute-done((bf16[4,128,1024]{2,1,0:T(8,128)(2,1)S(1)}, bf16[4,128,1024]{2,1,0:T(8,128)(2,1)S(1)}, u32[]{:S(2)}, u32[]{:S(2)}) %collective-permute-start.23) | collective-permute-done | bytes 1048608 | tf_op jit(solution)/shard_map/ppermute | solution.py:26
  244.9 30.1 %shard_map.260 = (bf16[2048,1024]{1,0:T(8,128)(2,1)}, bf16[2048,1024]{1,0:T(8,128)(2,1)}, f32[2,1024]{1,0:T(2,128)}, f32[1,1024]{1,0:T(1,128)}, bf16[4,128,1024]...) custom-call(s32[3]{0:T(128)} %pad_add_fusion.info, bf16[2048,1024]{1,0:T(8,128)(2,1)} %get-tuple-element.75.second_ref, ...), custom_call_target="tpu_custom_call" | custom-call | bytes 87500000 | tf_op jit(solution)/shard_map/pallas_call | solution.py:257
  275.1 9.0 %shard_map.261 = (bf16[2048,1024]{1,0:T(8,128)(2,1)}, f32[256,1024]{1,0:T(8,128)}) custom-call(s32[3]{0:T(128)} %pad_add_fusion.info, bf16[2048,256]{1,0:T(8,128)(2,1)} %pad_maximum_fusion.3.m_ref, bf16[1024,1024]{1,0:T(8,128)(2,1)} %copy-done, bf16[1024,1024]{1,0:T(8,128)(2,1)} %collective-permute-done.10.gp_ref, ...), custom_call_target="tpu_custom_call" | custom-call | bytes 24500000 | tf_op jit(solution)/shard_map/pallas_call | solution.py:257
  286.0 3.8 pad_maximum_fusion.p_ref
  289.9 14.5 %shard_map.262 = (bf16[2048,1024]{1,0:T(8,128)(2,1)}, f32[2,1024]{1,0:T(2,128)}, f32[1,768]{1,0:T(1,128)}, bf16[4,128,768]{2,1,0:T(8,128)(2,1)}, bf16[4,128,768]{2,1,0:T(8,128)(2,1)}) custom-call(s32[3]{0:T(128)} %pad_add_fusion.info, bf16[2048,1024]{1,0:T(8,128)(2,1)} %get-tuple-element.88.first_ref, bf16[2048,1024]{1,0:T(8,128)(2,1)} %get-tuple-element.82.normed_ref, ...), custom_call_target="tpu_custom_call" | custom-call | bytes 49000000 | tf_op jit(solution)/shard_map/pallas_call | solution.py:257
  310.6 8.8 %collective-permute-start.35 = (bf16[128,1024]{1,0:T(8,128)(2,1)}, bf16[128,1024]{1,0:T(8,128)(2,1)}, u32[]{:S(2)}, u32[]{:S(2)}) collective-permute-start(bf16[128,1024]{1,0:T(8,128)(2,1)} %get-tuple-element.119), channel_id=1, source_target_pairs={{0,8},{2,10},{4,12},{6,14},{8,0},{10,2},{12,4},{14,6},{16,24},{18,... | collective-permute-start | bytes 786440 | tf_op jit(solution)/shard_map/ppermute | solution.py:26
  324.8 3.1 convert_add_fusion.1
  335.3 3.3 convert_add_fusion
  338.8 17.1 %collective-permute-done.25 = bf16[1,512,1024]{2,1,0:T(8,128)(2,1)S(1)} collective-permute-done((bf16[1,512,1024]{2,1,0:T(8,128)(2,1)}, bf16[1,512,1024]{2,1,0:T(8,128)(2,1)S(1)}, u32[]{:S(2)}, u32[]{:S(2)}) %collective-permute-start.25) | collective-permute-done | bytes 1048608 | tf_op jit(solution)/shard_map/ppermute | solution.py:31
  366.4 4.5 %collective-permute-done.49 = bf16[128,1024]{1,0:T(8,128)(2,1)S(1)} collective-permute-done((bf16[128,1024]{1,0:T(8,128)(2,1)S(1)}, bf16[128,1024]{1,0:T(8,128)(2,1)S(1)}, u32[]{:S(2)}, u32[]{:S(2)}) %collective-permute-start.49) | collective-permute-done | bytes 262176 | tf_op jit(solution)/shard_map/ppermute | solution.py:168
  374.2 4.4 collective-permute-start.40
  378.6 8.2 %collective-permute-done.27 = bf16[1,512,1024]{2,1,0:T(8,128)(2,1)S(1)} collective-permute-done((bf16[1,512,1024]{2,1,0:T(8,128)(2,1)S(1)}, bf16[1,512,1024]{2,1,0:T(8,128)(2,1)S(1)}, u32[]{:S(2)}, u32[]{:S(2)}) %collective-permute-start.27) | collective-permute-done | bytes 1048608 | tf_op jit(solution)/shard_map/ppermute | solution.py:31
  395.4 3.2 collective-permute-done.28
  400.1 5.0 %collective-permute-done.34 = bf16[4,128,768]{2,1,0:T(8,128)(2,1)S(1)} collective-permute-done((bf16[4,128,768]{2,1,0:T(8,128)(2,1)}, bf16[4,128,768]{2,1,0:T(8,128)(2,1)S(1)}, u32[]{:S(2)}, u32[]{:S(2)}) %collective-permute-start.34) | collective-permute-done | bytes 786464 | tf_op jit(solution)/shard_map/ppermute | solution.py:26
  405.4 4.3 collective-permute-start.43
  410.9 3.1 collective-permute-done.30
  416.6 4.8 %collective-permute-done.42 = bf16[128,768]{1,0:T(8,128)(2,1)S(1)} collective-permute-done((bf16[128,768]{1,0:T(8,128)(2,1)S(1)}, bf16[128,768]{1,0:T(8,128)(2,1)S(1)}, u32[]{:S(2)}, u32[]{:S(2)}) %collective-permute-start.42) | collective-permute-done | bytes 196640 | tf_op jit(solution)/shard_map/ppermute | solution.py:26
  (282 shorter events, 124.4 us)
Async XLA Ops:
  27.0 34.6 %collective-permute-start.5 = (bf16[144,768]{1,0:T(8,128)(2,1)S(1)}, bf16[144,768]{1,0:T(8,128)(2,1)}, u32[]{:S(2)}, u32[]{:S(2)}) collective-permute-start(bf16[144,768]{1,0:T(8,128)(2,1)S(1)} %pad_dynamic-update-slice_fusion), channel_id=1, source_target_pairs={{0,8},{2,10},{4,12},{6,14},{8,0},{10,2},{12,4},{14,6},{16,24},{18,... | collective-permute-start | bytes 663560 | tf_op jit(solution)/shard_map/ppermute | solution.py:26
  28.6 35.5 %collective-permute-start.6 = (bf16[144,768]{1,0:T(8,128)(2,1)S(1)}, bf16[144,768]{1,0:T(8,128)(2,1)}, u32[]{:S(2)}, u32[]{:S(2)}) collective-permute-start(bf16[144,768]{1,0:T(8,128)(2,1)S(1)} %pad_dynamic-update-slice_fusion), channel_id=1, source_target_pairs={{0,16},{2,18},{4,20},{6,22},{8,24},{10,26},{12,28},{14,30},{16,0},... | collective-permute-start | bytes 663560 | tf_op jit(solution)/shard_map/ppermute | solution.py:26
  31.2 39.2 %collective-permute-start.7 = (bf16[144,768]{1,0:T(8,128)(2,1)S(1)}, bf16[144,768]{1,0:T(8,128)(2,1)}, u32[]{:S(2)}, u32[]{:S(2)}) collective-permute-start(bf16[144,768]{1,0:T(8,128)(2,1)S(1)} %pad_dynamic-update-slice_fusion), channel_id=1, source_target_pairs={{0,24},{2,26},{4,28},{6,30},{8,16},{10,18},{12,20},{14,22},{16,8},... | collective-permute-start | bytes 663560 | tf_op jit(solution)/shard_map/ppermute | solution.py:26
  31.5 25.1 %collective-permute-start.3 = (bf16[1,512,1024]{2,1,0:T(8,128)(2,1)S(1)}, bf16[1,512,1024]{2,1,0:T(8,128)(2,1)S(1)}, u32[]{:S(2)}, u32[]{:S(2)}) collective-permute-start(bf16[1,512,1024]{2,1,0:T(8,128)(2,1)S(1)} %copy-done.1), channel_id=1, source_target_pairs={{0,1},{1,0},{2,3},{3,2},{4,5},{5,4},{6,7},{7,6},{8,9},{9,8},{10,11... | collective-permute-start | bytes 3145736 | tf_op jit(solution)/shard_map/ppermute | solution.py:31
  34.5 39.9 %collective-permute-start.11 = (bf16[128,1024]{1,0:T(8,128)(2,1)S(1)}, bf16[128,1024]{1,0:T(8,128)(2,1)S(1)}, u32[]{:S(2)}, u32[]{:S(2)}) collective-permute-start(bf16[128,1024]{1,0:T(8,128)(2,1)S(1)} %pad_maximum_fusion.5), channel_id=1, source_target_pairs={{0,8},{4,12},{9,1},{13,5},{18,26},{22,30},{27,19},{31,23}} | collective-permute-start | bytes 786440 | tf_op jit(solution)/shard_map/ppermute | solution.py:114
  56.5 17.9 %collective-permute-start.12 = (bf16[128,1024]{1,0:T(8,128)(2,1)S(1)}, bf16[128,1024]{1,0:T(8,128)(2,1)S(1)}, u32[]{:S(2)}, u32[]{:S(2)}) collective-permute-start(bf16[128,1024]{1,0:T(8,128)(2,1)S(1)} %pad_maximum_fusion.5), channel_id=1, source_target_pairs={{0,16},{4,20},{9,25},{13,29},{18,2},{22,6},{27,11},{31,15}} | collective-permute-start | bytes 786440 | tf_op jit(solution)/shard_map/ppermute | solution.py:114
  64.2 36.2 %collective-permute-start.9 = (bf16[1,512,1024]{2,1,0:T(8,128)(2,1)S(1)}, bf16[1,512,1024]{2,1,0:T(8,128)(2,1)S(1)}, u32[]{:S(2)}, u32[]{:S(2)}) collective-permute-start(bf16[1,512,1024]{2,1,0:T(8,128)(2,1)S(1)} %copy-done.6), channel_id=1, source_target_pairs={{0,1},{1,0},{2,3},{3,2},{4,5},{5,4},{6,7},{7,6},{8,9},{9,8},{10,11... | collective-permute-start | bytes 3145736 | tf_op jit(solution)/shard_map/ppermute | solution.py:31
  74.4 18.9 %collective-permute-start.16 = (bf16[128,1024]{1,0:T(8,128)(2,1)S(1)}, bf16[128,1024]{1,0:T(8,128)(2,1)S(1)}, u32[]{:S(2)}, u32[]{:S(2)}) collective-permute-start(bf16[128,1024]{1,0:T(8,128)(2,1)S(1)} %pad_maximum_fusion.6), channel_id=1, source_target_pairs={{0,16},{2,18},{4,20},{6,22},{8,24},{10,26},{12,28},{14,30},{16,0},... | collective-permute-start | bytes 786440 | tf_op jit(solution)/shard_map/ppermute | solution.py:26
  74.4 18.9 %collective-permute-start.17 = (bf16[128,1024]{1,0:T(8,128)(2,1)S(1)}, bf16[128,1024]{1,0:T(8,128)(2,1)S(1)}, u32[]{:S(2)}, u32[]{:S(2)}) collective-permute-start(bf16[128,1024]{1,0:T(8,128)(2,1)S(1)} %pad_maximum_fusion.6), channel_id=1, source_target_pairs={{0,24},{2,26},{4,28},{6,30},{8,16},{10,18},{12,20},{14,22},{16,8},... | collective-permute-start | bytes 786440 | tf_op jit(solution)/shard_map/ppermute | solution.py:26
  77.0 21.8 %collective-permute-start.14 = (bf16[1,128,1024]{2,1,0:T(8,128)(2,1)S(1)}, bf16[1,128,1024]{2,1,0:T(8,128)(2,1)S(1)}, u32[]{:S(2)}, u32[]{:S(2)}) collective-permute-start(bf16[1,128,1024]{2,1,0:T(8,128)(2,1)S(1)} %bitcast.162), channel_id=1, source_target_pairs={{0,4},{2,6},{4,0},{6,2},{8,12},{10,14},{12,8},{14,10},{16,20},{18,... | collective-permute-start | bytes 786440 | tf_op jit(solution)/shard_map/ppermute | solution.py:26
  81.2 38.6 %collective-permute-start.8 = (bf16[4,144,768]{2,1,0:T(8,128)(2,1)S(1)}, bf16[4,144,768]{2,1,0:T(8,128)(2,1)S(1)}, u32[]{:S(2)}, u32[]{:S(2)}) collective-permute-start(bf16[4,144,768]{2,1,0:T(8,128)(2,1)S(1)} %pad_maximum_fusion.4.far_ref), channel_id=1, source_target_pairs={{0,4},{2,6},{4,0},{6,2},{8,12},{10,14},{12,8},{14,10},{16,20},{18,... | collective-permute-start | bytes 2654216 | tf_op jit(solution)/shard_map/ppermute | solution.py:26
  97.7 20.9 %collective-permute-start.19 = (bf16[128,1024]{1,0:T(8,128)(2,1)S(1)}, bf16[128,1024]{1,0:T(8,128)(2,1)S(1)}, u32[]{:S(2)}, u32[]{:S(2)}) collective-permute-start(bf16[128,1024]{1,0:T(8,128)(2,1)S(1)} %copy-done.18), channel_id=1, source_target_pairs={{0,16},{2,18},{4,20},{6,22},{8,24},{10,26},{12,28},{14,30},{16,0},... | collective-permute-start | bytes 786440 | tf_op jit(solution)/shard_map/ppermute | solution.py:26
  98.8 19.9 %collective-permute-start.20 = (bf16[128,1024]{1,0:T(8,128)(2,1)S(1)}, bf16[128,1024]{1,0:T(8,128)(2,1)S(1)}, u32[]{:S(2)}, u32[]{:S(2)}) collective-permute-start(bf16[128,1024]{1,0:T(8,128)(2,1)S(1)} %copy-done.18), channel_id=1, source_target_pairs={{0,24},{2,26},{4,28},{6,30},{8,16},{10,18},{12,20},{14,22},{16,8},... | collective-permute-start | bytes 786440 | tf_op jit(solution)/shard_map/ppermute | solution.py:26
  100.4 40.8 %collective-permute-start.4 = (bf16[1024,1024]{1,0:T(8,128)(2,1)}, bf16[1024,1024]{1,0:T(8,128)(2,1)}, u32[]{:S(2)}, u32[]{:S(2)}) collective-permute-start(bf16[1024,1024]{1,0:T(8,128)(2,1)} %maximum_bitcast_fusion.xo_ref), channel_id=1, source_target_pairs={{0,2},{2,0},{4,6},{6,4},{8,10},{10,8},{12,14},{14,12},{16,18},{18,... | collective-permute-start | bytes 6291464 | tf_op jit(solution)/shard_map/ppermute | solution.py:26
  106.3 46.6 %collective-permute-start.10 = (bf16[1024,1024]{1,0:T(8,128)(2,1)S(1)}, bf16[1024,1024]{1,0:T(8,128)(2,1)}, u32[]{:S(2)}, u32[]{:S(2)}) collective-permute-start(bf16[1024,1024]{1,0:T(8,128)(2,1)S(1)} %maximum_bitcast_fusion.1.go_ref), channel_id=1, source_target_pairs={{0,2},{2,0},{4,6},{6,4},{8,10},{10,8},{12,14},{14,12},{16,18},{18,... | collective-permute-start | bytes 6291464 | tf_op jit(solution)/shard_map/ppermute | solution.py:26
  119.8 21.3 %collective-permute-start.21 = (bf16[4,128,1024]{2,1,0:T(8,128)(2,1)}, bf16[4,128,1024]{2,1,0:T(8,128)(2,1)}, u32[]{:S(2)}, u32[]{:S(2)}) collective-permute-start(bf16[4,128,1024]{2,1,0:T(8,128)(2,1)} %pad_maximum_fusion.1.far_ref.refs_0_), channel_id=1, source_target_pairs={{0,4},{2,6},{4,0},{6,2},{8,12},{10,14},{12,8},{14,10},{16,20},{18,... | collective-permute-start | bytes 3145736 | tf_op jit(solution)/shard_map/ppermute | solution.py:26
  201.2 27.1 %collective-permute-start.22 = (bf16[4,128,1024]{2,1,0:T(8,128)(2,1)}, bf16[4,128,1024]{2,1,0:T(8,128)(2,1)S(1)}, u32[]{:S(2)}, u32[]{:S(2)}) collective-permute-start(bf16[4,128,1024]{2,1,0:T(8,128)(2,1)} %get-tuple-element.80), channel_id=1, source_target_pairs={{0,4},{2,6},{4,0},{6,2},{8,12},{10,14},{12,8},{14,10},{16,20},{18,... | collective-permute-start | bytes 3145736 | tf_op jit(solution)/shard_map/ppermute | solution.py:26
  202.8 41.2 %collective-permute-start.23 = (bf16[4,128,1024]{2,1,0:T(8,128)(2,1)S(1)}, bf16[4,128,1024]{2,1,0:T(8,128)(2,1)S(1)}, u32[]{:S(2)}, u32[]{:S(2)}) collective-permute-start(bf16[4,128,1024]{2,1,0:T(8,128)(2,1)S(1)} %copy-done.5), channel_id=1, source_target_pairs={{0,4},{2,6},{4,0},{6,2},{8,12},{10,14},{12,8},{14,10},{16,20},{18,... | collective-permute-start | bytes 3145736 | tf_op jit(solution)/shard_map/ppermute | solution.py:26
  285.8 39.0 %collective-permute-start.24 = (bf16[1,1024,1024]{2,1,0:T(8,128)(2,1)S(1)}, bf16[1,1024,1024]{2,1,0:T(8,128)(2,1)}, u32[]{:S(2)}, u32[]{:S(2)}) collective-permute-start(bf16[1,1024,1024]{2,1,0:T(8,128)(2,1)S(1)} %slice_bitcast_fusion.1), channel_id=1, source_target_pairs={{0,2},{2,0},{4,6},{6,4},{8,10},{10,8},{12,14},{14,12},{16,18},{18,... | collective-permute-start | bytes 6291464 | tf_op jit(solution)/shard_map/ppermute | solution.py:26
  307.4 27.3 %collective-permute-start.26 = (bf16[1,1024,1024]{2,1,0:T(8,128)(2,1)}, bf16[1,1024,1024]{2,1,0:T(8,128)(2,1)}, u32[]{:S(2)}, u32[]{:S(2)}) collective-permute-start(bf16[1,1024,1024]{2,1,0:T(8,128)(2,1)} %slice_bitcast_fusion), channel_id=1, source_target_pairs={{0,2},{2,0},{4,6},{6,4},{8,10},{10,8},{12,14},{14,12},{16,18},{18,... | collective-permute-start | bytes 6291464 | tf_op jit(solution)/shard_map/ppermute | solution.py:26
  310.6 48.2 %collective-permute-start.35 = (bf16[128,1024]{1,0:T(8,128)(2,1)}, bf16[128,1024]{1,0:T(8,128)(2,1)}, u32[]{:S(2)}, u32[]{:S(2)}) collective-permute-start(bf16[128,1024]{1,0:T(8,128)(2,1)} %get-tuple-element.119), channel_id=1, source_target_pairs={{0,8},{2,10},{4,12},{6,14},{8,0},{10,2},{12,4},{14,6},{16,24},{18,... | collective-permute-start | bytes 786440 | tf_op jit(solution)/shard_map/ppermute | solution.py:26
  319.4 40.7 %collective-permute-start.36 = (bf16[128,1024]{1,0:T(8,128)(2,1)}, bf16[128,1024]{1,0:T(8,128)(2,1)}, u32[]{:S(2)}, u32[]{:S(2)}) collective-permute-start(bf16[128,1024]{1,0:T(8,128)(2,1)} %get-tuple-element.121), channel_id=1, source_target_pairs={{0,16},{2,18},{4,20},{6,22},{8,24},{10,26},{12,28},{14,30},{16,0},... | collective-permute-start | bytes 786440 | tf_op jit(solution)/shard_map/ppermute | solution.py:26
  331.1 24.8 %collective-permute-start.25 = (bf16[1,512,1024]{2,1,0:T(8,128)(2,1)}, bf16[1,512,1024]{2,1,0:T(8,128)(2,1)S(1)}, u32[]{:S(2)}, u32[]{:S(2)}) collective-permute-start(bf16[1,512,1024]{2,1,0:T(8,128)(2,1)} %slice.408), channel_id=1, source_target_pairs={{0,1},{1,0},{2,3},{3,2},{4,5},{5,4},{6,7},{7,6},{8,9},{9,8},{10,11... | collective-permute-start | bytes 3145736 | tf_op jit(solution)/shard_map/ppermute | solution.py:31
  333.2 28.2 %collective-permute-start.37 = (bf16[128,1024]{1,0:T(8,128)(2,1)}, bf16[128,1024]{1,0:T(8,128)(2,1)S(1)}, u32[]{:S(2)}, u32[]{:S(2)}) collective-permute-start(bf16[128,1024]{1,0:T(8,128)(2,1)} %get-tuple-element.120), channel_id=1, source_target_pairs={{0,24},{2,26},{4,28},{6,30},{8,16},{10,18},{12,20},{14,22},{16,8},... | collective-permute-start | bytes 786440 | tf_op jit(solution)/shard_map/ppermute | solution.py:26
  334.8 38.2 %collective-permute-start.33 = (bf16[4,128,1024]{2,1,0:T(8,128)(2,1)}, bf16[4,128,1024]{2,1,0:T(8,128)(2,1)S(1)}, u32[]{:S(2)}, u32[]{:S(2)}) collective-permute-start(bf16[4,128,1024]{2,1,0:T(8,128)(2,1)} %get-tuple-element.101), channel_id=1, source_target_pairs={{0,4},{2,6},{4,0},{6,2},{8,12},{10,14},{12,8},{14,10},{16,20},{18,... | collective-permute-start | bytes 3145736 | tf_op jit(solution)/shard_map/ppermute | solution.py:26
  361.5 25.2 %collective-permute-start.27 = (bf16[1,512,1024]{2,1,0:T(8,128)(2,1)S(1)}, bf16[1,512,1024]{2,1,0:T(8,128)(2,1)S(1)}, u32[]{:S(2)}, u32[]{:S(2)}) collective-permute-start(bf16[1,512,1024]{2,1,0:T(8,128)(2,1)S(1)} %slice.407), channel_id=1, source_target_pairs={{0,1},{1,0},{2,3},{3,2},{4,5},{5,4},{6,7},{7,6},{8,9},{9,8},{10,11... | collective-permute-start | bytes 3145736 | tf_op jit(solution)/shard_map/ppermute | solution.py:31
  371.7 52.9 %collective-permute-start.51 = (bf16[32,1024]{1,0:T(8,128)(2,1)}, bf16[32,1024]{1,0:T(8,128)(2,1)S(1)}, u32[]{:S(2)}, u32[]{:S(2)}) collective-permute-start(bf16[32,1024]{1,0:T(8,128)(2,1)} %get-tuple-element.140), channel_id=1, source_target_pairs={{0,1},{4,5},{9,8},{13,12},{18,19},{22,23},{27,26},{31,30}} | collective-permute-start | bytes 196616 | tf_op jit(solution)/shard_map/ppermute | solution.py:177
  374.2 17.4 %collective-permute-start.38 = (bf16[128,1024]{1,0:T(8,128)(2,1)}, bf16[128,1024]{1,0:T(8,128)(2,1)}, u32[]{:S(2)}, u32[]{:S(2)}) collective-permute-start(bf16[128,1024]{1,0:T(8,128)(2,1)} %get-tuple-element.105), channel_id=1, source_target_pairs={{0,8},{2,10},{4,12},{6,14},{8,0},{10,2},{12,4},{14,6},{16,24},{18,... | collective-permute-start | bytes 786440 | tf_op jit(solution)/shard_map/ppermute | solution.py:26
  374.2 19.8 %collective-permute-start.39 = (bf16[128,1024]{1,0:T(8,128)(2,1)}, bf16[128,1024]{1,0:T(8,128)(2,1)}, u32[]{:S(2)}, u32[]{:S(2)}) collective-permute-start(bf16[128,1024]{1,0:T(8,128)(2,1)} %get-tuple-element.106), channel_id=1, source_target_pairs={{0,16},{2,18},{4,20},{6,22},{8,24},{10,26},{12,28},{14,30},{16,0},... | collective-permute-start | bytes 786440 | tf_op jit(solution)/shard_map/ppermute | solution.py:26
  374.2 19.8 %collective-permute-start.40 = (bf16[128,1024]{1,0:T(8,128)(2,1)S(1)}, bf16[128,1024]{1,0:T(8,128)(2,1)}, u32[]{:S(2)}, u32[]{:S(2)}) collective-permute-start(bf16[128,1024]{1,0:T(8,128)(2,1)S(1)} %get-tuple-element.107), channel_id=1, source_target_pairs={{0,24},{2,26},{4,28},{6,30},{8,16},{10,18},{12,20},{14,22},{16,8},... | collective-permute-start | bytes 786440 | tf_op jit(solution)/shard_map/ppermute | solution.py:26
  386.7 18.4 %collective-permute-start.34 = (bf16[4,128,768]{2,1,0:T(8,128)(2,1)}, bf16[4,128,768]{2,1,0:T(8,128)(2,1)S(1)}, u32[]{:S(2)}, u32[]{:S(2)}) collective-permute-start(bf16[4,128,768]{2,1,0:T(8,128)(2,1)} %get-tuple-element.102), channel_id=1, source_target_pairs={{0,4},{2,6},{4,0},{6,2},{8,12},{10,14},{12,8},{14,10},{16,20},{18,... | collective-permute-start | bytes 2359304 | tf_op jit(solution)/shard_map/ppermute | solution.py:26
  405.4 17.2 %collective-permute-start.43 = (bf16[128,768]{1,0:T(8,128)(2,1)S(1)}, bf16[128,768]{1,0:T(8,128)(2,1)S(1)}, u32[]{:S(2)}, u32[]{:S(2)}) collective-permute-start(bf16[128,768]{1,0:T(8,128)(2,1)S(1)} %get-tuple-element.110), channel_id=1, source_target_pairs={{0,24},{2,26},{4,28},{6,30},{8,16},{10,18},{12,20},{14,22},{16,8},... | collective-permute-start | bytes 589832 | tf_op jit(solution)/shard_map/ppermute | solution.py:26
  (57 other events, 643.6 us)
